TPU v7x, 128 devices: a whole 4x4x4 slice. The times are simulated.
128 devices in a mesh: row: 8 (over x, y_lo), col: 4 (over z), dp: 4 (over y_hi, core).
Axes of the slice: x: 4, y: 4 (y_hi: 2, y_lo: 2; y = y_hi * 2 + y_lo), z: 4, core: 2. Of those that a mesh axis runs over, the one named last changes fastest.
Arguments:
- inputs: bfloat16 [4, 2048, 10240], P('dp', 'col', 'row'), may hold values from -0.06591797 to 0.06591797
- grad_out: bfloat16 [4, 2048, 10240], P('dp', 'row', 'col'), may hold values from -6 to 6
- weight: bfloat16 [10240, 10240], P('row', 'col'), may hold values from -0.078125 to 0.078125
Outputs:
- grad_in: bfloat16 [4, 2048, 10240], P('dp', 'col', 'row')
- grad_weight: bfloat16 [10240, 10240], P('row', 'col')
All inputs are finite; a program needn't handle non-finite values.
Results may differ from a plain program's by a relative error of at most 0.001.
Values may be sent and summed in bfloat16 or wider, within the bound.
No kernel may reach another device: no remote copies, remote signals or barrier semaphores. Data moves between devices by JAX's collectives and lax.ppermute only.
A program may use at most 192 MiB of HBM per device.

v0:
```python
import jax
import jax.numpy as jnp
from jax import lax
from jax.sharding import PartitionSpec as P


def local(inputs, grad_out, weight):
    input_rep = lax.all_gather(inputs, "col", axis=1, tiled=True)[0]
    grads_rep = lax.all_gather(grad_out, "row", axis=1, tiled=True)[0]
    partial_total = lax.dot_general(
        input_rep, grads_rep, (((0,), (0,)), ((), ())), preferred_element_type=jnp.float32
    )
    grad_weight = lax.psum(partial_total, "dp").astype(jnp.bfloat16)
    grad_in = lax.psum_scatter(
        lax.dot_general(
            grads_rep, weight, (((1,), (1,)), ((), ())), preferred_element_type=jnp.float32
        ),
        "col",
        scatter_dimension=0,
        tiled=True,
    )
    return (grad_in.astype(jnp.bfloat16)[None], grad_weight)


def solution(mesh):
    in_specs = (P("dp", "col", "row"), P("dp", "row", "col"), P("row", "col"))
    out_specs = (P("dp", "col", "row"), P("row", "col"))
    return jax.shard_map(local, mesh=mesh, in_specs=in_specs, out_specs=out_specs, check_vma=False)
```

profile of v0, /device:TPU:1, one launch (start us, length us, event | category | flops | bytes accessed | tf_op | source)
XLA Modules:
  0.0 541.1 jit_solution(16905380769764896206)
XLA Ops:
  7.2 0.0 all-gather.3.cloned.1.call-start
  7.2 0.7 all-gather.3.cloned.1.call-update
  7.9 0.0 all-gather.5.cloned.1.call-start
  7.9 0.7 all-gather.5.cloned.1.call-update
  8.6 0.0 reduce-scatter.2.cloned.1.call-start
  8.7 211.8 %all-gather.3.cloned.1.call-done = bf16[1,2048,2560]{2,1,0:T(8,128)(2,1)} async-done(((bf16[1,256,2560]{2,1,0:T(8,128)(2,1)}), bf16[1,2048,2560]{2,1,0:T(8,128)(2,1)}) %all-gather.3.cloned.1.call-update) | async-done | bytes 10485776 | tf_op jit(solution)/shard_map/all_gather | solution.py:9
  220.5 19.5 %fusion.2 = f32[2048,1280]{1,0:T(8,128)} fusion(bf16[1280,2560]{1,0:T(8,128)(2,1)} %param.5, bf16[1,2048,2560]{2,1,0:T(8,128)(2,1)} %all-gather.3.cloned.1.call-done), kind=kOutput, calls=%fused_computation.2 | convolution fusion | flops 13421772800 | bytes 27525120 | tf_op jit(solution)/shard_map/dot_general | solution.py:15
  240.1 0.0 reduce-scatter.2.cloned.1.call-update
  240.1 40.8 %all-gather.5.cloned.1.call-done = bf16[1,2048,1280]{2,1,0:T(8,128)(2,1)} async-done(((bf16[1,512,1280]{2,1,0:T(8,128)(2,1)}), bf16[1,2048,1280]{2,1,0:T(8,128)(2,1)}) %all-gather.5.cloned.1.call-update) | async-done | bytes 5242896 | tf_op jit(solution)/shard_map/all_gather | solution.py:8
  280.9 21.0 %fusion = f32[1280,2560]{1,0:T(8,128)} fusion(bf16[1,2048,2560]{2,1,0:T(8,128)(2,1)} %all-gather.3.cloned.1.call-done, bf16[1,2048,1280]{2,1,0:T(8,128)(2,1)} %all-gather.5.cloned.1.call-done), kind=kOutput, calls=%fused_computation | convolution fusion | flops 13421772800 | bytes 28835840 | tf_op jit(solution)/shard_map/dot_general | solution.py:10
  301.8 229.8 %all-reduce.1 = bf16[1280,2560]{1,0:T(8,128)(2,1)} all-reduce(f32[1280,2560]{1,0:T(8,128)} %fusion), channel_id=1, replica_groups=mesh['row'=8,'col'=4,'dp'=4] {'dp'}, use_global_device_ids=true, to_apply=%region_1.0 | all-reduce | flops 3276800 | bytes 19660800 | tf_op jit(solution)/shard_map/psum | solution.py:13
  531.7 0.0 reduce-scatter.2.cloned.1.call-done
  531.7 2.9 convert_bitcast_fusion
Async XLA Ops:
  7.2 213.4 %all-gather.3.cloned.1.call-start = ((), (), s32[]{:S(2)}) async-start(), calls=%async_computation.1 | async-start | bytes 11796480 | tf_op jit(solution)/shard_map/all_gather | solution.py:9
  7.9 273.0 %all-gather.5.cloned.1.call-start = ((), (), s32[]{:S(2)}) async-start(), calls=%async_computation.3 | async-start | bytes 6553600 | tf_op jit(solution)/shard_map/all_gather | solution.py:8
  8.6 523.0 %reduce-scatter.2.cloned.1.call-start = ((), (), s32[]{:S(2)}) async-start(), calls=%async_computation.2 | async-start | bytes 13107200 | tf_op jit(solution)/shard_map/reduce_scatter | solution.py:14
Sparse Core Ops, SparseCore 0:
  9.6 210.8 all-gather.2
  222.2 58.6 all-gather.4
  283.3 98.1 reduce-scatter.1
where the time goes:
time: 541 us
  waiting for transfers between devices  254 us (47%)
  blocking collectives  230 us (43%)
  matrix products  40.5 us (7%)
  between operations  13.7 us (3%)
    psum x1, blocking collectives, local(): grad_weight = lax.psum(partial_total, 'dp').astype(jnp.bfloat16)  230 us
    all_gather x1, waiting for transfers between devices, local(): grads_rep = lax.all_gather(grad_out, 'row', axis=1, tiled=True)[0]  212 us
    all_gather x1, waiting for transfers between devices, local(): input_rep = lax.all_gather(inputs, 'col', axis=1, tiled=True)[0]  40.8 us
    dot_general x1, matrix products, local(): lax.dot_general(input_rep, grads_rep, (((0,), (0,)), ((), ())), preferred...  21 us
    dot_general x1, matrix products, local(): lax.dot_general(grads_rep, weight, (((1,), (1,)), ((), ())), preferred_el...  19.5 us
  transfers between devices with their start and end apart: 3, of which 2 were waited for; matrix products, arithmetic and copies ran while one was open for 7% of the time, Pallas kernels for 0%

commit v1 on v0

v1 whole, which is shorter than its diff:
```python
import functools

import jax
import jax.numpy as jnp
from jax import lax
from jax.experimental import pallas as pl
from jax.experimental.pallas import tpu as pltpu
from jax.sharding import PartitionSpec as P

X_UP = [(r, (r + 2) % 8) for r in range(8)]
X_DOWN = [(r, (r - 2) % 8) for r in range(8)]
Y_SWAP = [(r, r ^ 1) for r in range(8)]
Z_UP = [(c, (c + 1) % 4) for c in range(4)]
Z_DOWN = [(c, (c - 1) % 4) for c in range(4)]
CORE_SWAP = [(d, d ^ 1) for d in range(4)]
FAR_SWAP = [(d, d ^ 2) for d in range(4)]

WIDTHS = (1024, 1536)
F32, BF16 = jnp.float32, jnp.bfloat16
ANY = pl.BlockSpec(memory_space=pl.ANY)
VMEM = pl.BlockSpec(memory_space=pltpu.VMEM)
SMEM = pl.BlockSpec(memory_space=pltpu.SMEM)
HBM = pl.BlockSpec(memory_space=pltpu.HBM)
CHEAP = pl.CostEstimate(flops=1, bytes_accessed=1, transcendentals=0)
POWER = 15.0
TAIL = 16
STEP = 32


def call(kernel, outs, scratch=(), specs=(), out_specs=None, mib=24, aliases=None):
    return pl.pallas_call(
        kernel,
        in_specs=list(specs),
        out_specs=out_specs or [VMEM] * len(outs),
        out_shape=list(outs),
        scratch_shapes=list(scratch),
        input_output_aliases=aliases or {},
        compiler_params=pltpu.CompilerParams(vmem_limit_bytes=mib << 20),
        cost_estimate=CHEAP,
    )


def after(x, *deps):
    return lax.optimization_barrier((x, *deps))[0]


def encode(src, dst, lo=0):
    n, c = src.shape

    def top_of(i, m):
        v = jnp.abs(src[pl.ds(pl.multiple_of(i * STEP, STEP), STEP), :])
        return jnp.maximum(m, jnp.max(v.reshape(STEP // 8, 8, c), axis=0))

    top = jnp.max(lax.fori_loop(0, n // STEP, top_of, jnp.zeros((8, c), F32)), keepdims=True)
    e = jnp.ceil(jnp.log2(jnp.clip(top, 2.0**-118, 2.0**120)))
    scale = jnp.exp2(8.0 - e)

    @pl.loop(0, n // STEP)
    def _(i):
        rows = pl.ds(pl.multiple_of(i * STEP, STEP), STEP)
        v = src[rows, :] * scale
        v2 = v * v
        v4 = v2 * v2
        dst[rows, :] = ((v4 * v4) * v4 * (v2 * v)).astype(BF16)

    dst[n:, :] = jnp.broadcast_to(e, (TAIL, c)).astype(BF16)


def scale_of(msg):
    n = msg.shape[0] - TAIL
    return jnp.exp2(msg[n:, 0:128].astype(F32)[0:1, 0:1] - 8.0)


def decode(y, scale):
    y = y.astype(F32)
    r = jnp.exp2(jnp.log2(jnp.abs(y)) * (1.0 / POWER)) * scale
    r = jnp.where(y == 0.0, 0.0, r)
    return jnp.where(y < 0.0, -r, r)


def looped(n, body):
    @pl.loop(0, n // STEP)
    def _(i):
        body(pl.ds(pl.multiple_of(i * STEP, STEP), STEP))


def weight_dot(held, grads, out):
    out[...] = lax.dot_general(held[...], grads[...], (((0,), (0,)), ((), ())), preferred_element_type=F32)


def give_kernel(first, at, inputs, a, b, a_up, a_dn, far_lo, far_hi, b_up, b_dn, b_far, give, grads, held, in_sem, sems):
    x, y, core = at[0], at[1], at[2]
    rows, width = a.shape[0], grads.shape[1]
    cols = pl.ds(first, width)
    half = give.shape[0]
    fetch = pltpu.make_async_copy(
        inputs.at[:, pl.ds(pl.multiple_of((1 - core) * half, half), half)], held, in_sem
    )
    fetch.start()
    copies = []

    def put(src, d, e, offset):
        r = 2 * lax.rem(x + d, 4) + lax.rem(y + e, 2)
        start = pl.multiple_of(r * rows + offset, rows // 2)
        copy = pltpu.make_async_copy(src, grads.at[pl.ds(start, src.shape[0])], sems.at[len(copies)])
        copy.start()
        copies.append(copy)

    put(a.at[:, cols], 0, 0, 0)
    put(b.at[:, cols], 0, 1, 0)
    put(a_up.at[:, cols], 1, 0, 0)
    put(a_dn.at[:, cols], 3, 0, 0)
    put(far_lo.at[:, cols], 2, 0, 0)
    put(far_hi.at[:, cols], 2, 0, rows // 2)
    put(b_up.at[:, cols], 1, 1, 0)
    put(b_dn.at[:, cols], 3, 1, 0)
    put(b_far.at[:, cols], 2, 1, 0)
    fetch.wait()
    for copy in copies:
        copy.wait()
    weight_dot(held, grads, give)


def keep_kernel(at, inputs, grads, keep, held, in_sem):
    half = keep.shape[0]
    fetch = pltpu.make_async_copy(
        inputs.at[:, pl.ds(pl.multiple_of(at[2] * half, half), half)], held, in_sem
    )
    fetch.start()
    fetch.wait()
    weight_dot(held, grads, keep)


def pair_kernel(keep, got, msg, total):
    def add(rows):
        total[rows, :] = keep[rows, :] + got[rows, :]

    looped(keep.shape[0], add)
    encode(total, msg)


def decode_kernel(msg, out):
    s = scale_of(msg)

    def one(rows):
        out[rows, :] = decode(msg[rows, :], s)

    looped(out.shape[0], one)


def final_kernel(at, mine, got, out):
    s = scale_of(got)

    def add(rows):
        out[rows, :] = (mine[rows, :] + decode(got[rows, :], s)).astype(BF16)

    looped(out.shape[0], add)


def place_kernel(first, at, own, other, old, out, sems):
    half, width = own.shape
    copies = []
    for i, (src, which) in enumerate(((own, at[2]), (other, 1 - at[2]))):
        rows = pl.ds(pl.multiple_of(which * half, half), half)
        copies.append(pltpu.make_async_copy(src, out.at[rows, pl.ds(first, width)], sems.at[i]))
    for copy in copies:
        copy.start()
    for copy in copies:
        copy.wait()


def block_sums(at, weight, grads, blocks, bufs, held, sems, done):
    rows = bufs.shape[1]
    fetch = pltpu.make_async_copy(weight, held, sems.at[0])
    fetch.start()
    copies = []
    for i, (s, part) in enumerate(blocks):
        start = lax.rem(at[3] + s, 4) * (2 * rows) + part * rows
        tokens = pl.ds(pl.multiple_of(start, rows), rows)
        first = 0
        for g in grads:
            width = g.shape[1]
            copies.append(
                pltpu.make_async_copy(g.at[tokens], bufs.at[i, :, pl.ds(first, width)], sems.at[1 + len(copies)])
            )
            copies[-1].start()
            first += width
    fetch.wait()
    for i in range(len(blocks)):
        for copy in copies[i * len(grads) : (i + 1) * len(grads)]:
            copy.wait()
        done(i, lax.dot_general(bufs[i], held[...], (((1,), (0,)), ((), ())), preferred_element_type=F32))


def first_kernel(n, at, weight, *refs):
    grads, (up, dn, totals, bufs, held, sems) = refs[:n], refs[n:]

    def done(i, value):
        totals[i // 2, pl.ds(256 * (i % 2), 256), :] = value
        if i % 2:
            encode(totals.at[i // 2], (up, dn)[i // 2])

    block_sums(at, weight, grads, ((2, 0), (1, 1), (3, 0), (2, 1)), bufs, held, sems, done)


def rest_kernel(n, at, weight, *refs):
    grads, (up, dn, own, bufs, held, sems) = refs[:n], refs[n:]

    def done(i, value):
        (up, dn, own.at[pl.ds(0, 256)], own.at[pl.ds(256, 256)])[i][...] = value

    block_sums(at, weight, grads, ((1, 0), (3, 1), (0, 0), (0, 1)), bufs, held, sems, done)


def second_kernel(at, up, dn, from_dn, from_up, up_msg, dn_msg, total):
    for mine, msg, first, dst in ((up, from_dn, 0, up_msg), (dn, from_up, 256, dn_msg)):
        s = scale_of(msg)

        @pl.loop(0, 256 // STEP)
        def _(i):
            at = pl.multiple_of(i * STEP, STEP)
            rows = pl.ds(at, STEP)
            total[rows, :] = mine[rows, :] + decode(msg[pl.ds(first + at, STEP), :], s)

        encode(total, dst)


def last_kernel(own, from_dn, from_up, second_dn, second_up, out):
    s1, s2, s3, s4 = (scale_of(m) for m in (from_dn, from_up, second_dn, second_up))

    @pl.loop(0, 256 // STEP)
    def _(i):
        at = pl.multiple_of(i * STEP, STEP)
        lo, hi = pl.ds(at, STEP), pl.ds(256 + at, STEP)
        out[lo, :] = (own[lo, :] + (decode(second_dn[lo, :], s3) + decode(from_up[lo, :], s2))).astype(BF16)
        out[hi, :] = (own[hi, :] + (decode(from_dn[hi, :], s1) + decode(second_up[lo, :], s4))).astype(BF16)


def shape(*dims, dtype=F32):
    return jax.ShapeDtypeStruct(dims, dtype)


def local(inputs, grad_out, weight):
    row, col, dp = (lax.axis_index(n) for n in ("row", "col", "dp"))
    at = jnp.stack([row // 2, row % 2, dp % 2, col]).astype(jnp.int32)
    input_rep = lax.all_gather(inputs, "col", axis=1, tiled=True)[0]
    tokens, features = input_rep.shape
    outs = weight.shape[1]
    dma, dmas = pltpu.SemaphoreType.DMA, lambda n: pltpu.SemaphoreType.DMA((n,))

    a = grad_out[0]
    h = a.shape[0] // 2
    a_dn = lax.ppermute(a, "row", X_UP)
    a_up = lax.ppermute(a, "row", X_DOWN)
    b = lax.ppermute(a, "row", Y_SWAP)
    weight_t = weight.T
    far_lo = lax.ppermute(after(a_up, weight_t)[:h], "row", X_DOWN)
    far_hi = lax.ppermute(a_dn[h:], "row", X_UP)
    b_dn = lax.ppermute(b, "row", X_UP)
    b_up = lax.ppermute(b, "row", X_DOWN)
    b_far = lax.ppermute(jnp.concatenate([far_lo, far_hi], axis=0), "row", Y_SWAP)
    pieces = (a, b, a_up, a_dn, far_lo, far_hi, b_up, b_dn, b_far)

    spans, first = [], 0
    for width in WIDTHS:
        spans.append((first, width))
        first += width
    grads, sent, got = [], [], []

    def weight_chunk(j, at, middle=None):
        first, width = spans[j]
        half = features // 2
        held = pltpu.VMEM((tokens, half), BF16)
        give, g = call(
            functools.partial(give_kernel, first),
            [shape(half, width), shape(tokens, width, dtype=BF16)],
            [held, dma, dmas(9)],
            [SMEM] + [HBM] * 10,
        )(at, input_rep, *pieces)
        swapped = lax.ppermute(give, "dp", CORE_SWAP)
        middle = middle and middle(g, give)
        (keep,) = call(keep_kernel, [shape(half, width)], [held, dma], [SMEM, HBM, VMEM])(
            after(at, give if middle is None else middle[0]), input_rep, g
        )
        (msg,) = call(
            pair_kernel, [shape(half + TAIL, width, dtype=BF16)], [pltpu.VMEM((half, width), F32)], [VMEM] * 2
        )(keep, swapped)
        grads.append(g)
        sent.append(msg)
        got.append(lax.ppermute(msg, "dp", FAR_SWAP))
        return middle

    n = len(spans)
    scratch = [pltpu.VMEM((4, 256, outs), BF16), pltpu.VMEM((outs, features), BF16), dmas(1 + 4 * n)]
    msg = shape(512 + TAIL, features, dtype=BF16)

    def send_terms(g, give):
        return call(
            functools.partial(first_kernel, n),
            [msg, msg],
            [pltpu.VMEM((2, 512, features), F32)] + scratch,
            [SMEM] + [HBM] * (n + 1),
            mib=28,
        )(after(at, give), weight_t, grads[0], g)

    weight_chunk(0, at)
    up_msg, dn_msg = weight_chunk(1, after(at, sent[0]), send_terms)
    from_dn = lax.ppermute(up_msg, "col", Z_UP)
    from_up = lax.ppermute(dn_msg, "col", Z_DOWN)
    up, dn, own = call(
        functools.partial(rest_kernel, n),
        [shape(256, features), shape(256, features), shape(512, features)],
        scratch,
        [SMEM] + [HBM] * (n + 1),
        mib=28,
    )(after(at, sent[1]), weight_t, *grads)
    msg = shape(256 + TAIL, features, dtype=BF16)

    half = features // 2

    def finish(j, at, grad_weight=None):
        first, width = spans[j]
        (mine,) = call(decode_kernel, [shape(half, width)], (), [VMEM])(sent[j])
        (total,) = call(final_kernel, [shape(half, width, dtype=BF16)], (), [SMEM] + [VMEM] * 2)(at, mine, got[j])
        other = lax.ppermute(total, "dp", CORE_SWAP)
        old = () if grad_weight is None else (grad_weight,)
        kernel = functools.partial(place_kernel, first)
        if not old:
            kernel = lambda at, own, other, out, sems, k=kernel: k(at, own, other, None, out, sems)
        (grad_weight,) = call(
            kernel,
            [shape(features, outs, dtype=BF16)],
            [dmas(2)],
            [SMEM, ANY, ANY] + [ANY] * len(old),
            [ANY],
            aliases={3: 0} if old else None,
        )(at, total, other, *old)
        return total, grad_weight

    total, grad_weight = finish(0, after(at, sent[1]))
    msg = shape(256 + TAIL, features, dtype=BF16)
    up_msg, dn_msg = call(second_kernel, [msg, msg], [pltpu.VMEM((256, features), F32)], [SMEM] + [VMEM] * 4)(
        after(at, total), up, dn, from_dn, from_up
    )
    second_dn = lax.ppermute(up_msg, "col", Z_UP)
    second_up = lax.ppermute(dn_msg, "col", Z_DOWN)
    (grad_in,) = call(last_kernel, [shape(512, features, dtype=BF16)], (), [VMEM] * 5)(
        own, from_dn, from_up, second_dn, second_up
    )
    _, grad_weight = finish(1, after(at, grad_in), grad_weight)
    return (grad_in[None], grad_weight)


def solution(mesh):
    in_specs = (P("dp", "col", "row"), P("dp", "row", "col"), P("row", "col"))
    out_specs = (P("dp", "col", "row"), P("row", "col"))
    return jax.shard_map(local, mesh=mesh, in_specs=in_specs, out_specs=out_specs, check_vma=False)
```

time: 541 us -> 241 us (0.45)
  blocking collectives: 230 us -> 0 us
  waiting for transfers between devices: 254 us -> 98.3 us
  Pallas kernels: 0 us -> 69.7 us
  matrix products: 40.5 us -> 0 us
  starting transfers between devices: 0.11 us -> 29.5 us
  local copies, waits for them, and re-layouts: 0 us -> 27.2 us
    psum x1 -> x0, blocking collectives: 230 us -> none  [local(): grad_weight = lax.psum(partial_total, 'dp').astype(jnp.bfloat16)]
    all_gather x1 -> x0, waiting for transfers between devices: 212 us -> none  [local(): grads_rep = lax.all_gather(grad_out, 'row', axis=1, tiled=True)[0]]
    ppermute x0 -> x18, waiting for transfers between devices: none -> 97.6 us  [the longest x2 24.9 us: weight_chunk(): got.append(lax.ppermute(msg, 'dp', FAR_SWAP))]
    pallas_call x0 -> x16, Pallas kernels: none -> 69.7 us  [the longest x2 14.4 us: weight_chunk(): call(functools.partial(give_kernel, first), [shape(half, width), shape(to...]
    all_gather x1, waiting for transfers between devices: 40.8 us -> 0.01 us  [local(): input_rep = lax.all_gather(inputs, 'col', axis=1, tiled=True)[0]]
    dot_general x2 -> x0, matrix products: 40.5 us -> none  [the longest x1 21 us: local(): lax.dot_general(input_rep, grads_rep, (((0,), (0,)), ((), ())), preferred...]
    ppermute x0 -> x18, starting transfers between devices: none -> 29.4 us  [the longest x2 5.87 us: weight_chunk(): swapped = lax.ppermute(give, 'dp', CORE_SWAP)]
    unnamed x0 -> x37, local copies, waits for them, and re-layouts: none -> 27.1 us
  transfers between devices with their start and end apart: 3 -> 19, of which waited for: 2 -> 10; matrix products, arithmetic and copies ran while one was open for 7% -> 4% of each run, Pallas kernels for 0% -> 20%
where the time goes in v1:
time: 241 us; the launch traced here: 240 us
  waiting for transfers between devices  98.3 us (41%)
  Pallas kernels  69.7 us (29%)
  starting transfers between devices  29.5 us (12%)
  local copies, waits for them, and re-layouts  27.2 us (11%)
  between operations  14.3 us (6%)
    unnamed x37, local copies, waits for them, and re-layouts  27.1 us
    ppermute x2, waiting for transfers between devices, weight_chunk(): got.append(lax.ppermute(msg, 'dp', FAR_SWAP))  24.9 us
    ppermute x1, waiting for transfers between devices, local(): b_up = lax.ppermute(b, 'row', X_DOWN)  21.5 us
    ppermute x1, waiting for transfers between devices, local(): a_up = lax.ppermute(a, 'row', X_DOWN)  17 us
    pallas_call x2, Pallas kernels, weight_chunk(): call(functools.partial(give_kernel, first), [shape(half, width), shape(to...  14.4 us
    pallas_call x1, Pallas kernels, send_terms(): call(functools.partial(first_kernel, n), [msg, msg], [pltpu.VMEM((2, 512,...  13.4 us
    ppermute x1, waiting for transfers between devices, local(): second_dn = lax.ppermute(up_msg, 'col', Z_UP)  11.6 us
    pallas_call x1, Pallas kernels, local(): call(functools.partial(rest_kernel, n), [shape(256, features), shape(256,...  10.2 us
  transfers between devices with their start and end apart: 19, of which 10 were waited for; matrix products, arithmetic and copies ran while one was open for 4% of the time, Pallas kernels for 20%

profile of v1, /device:TPU:1, one launch (start us, length us, event | category | flops | bytes accessed | tf_op | source)
XLA Modules:
  0.0 240.1 jit_solution(6368758267810340594)
XLA Ops:
  7.9 3.4 %collective-permute-start.1 = (bf16[256,2560]{1,0:T(8,128)(2,1)}, bf16[256,2560]{1,0:T(8,128)(2,1)S(1)}, u32[]{:S(2)}, u32[]{:S(2)}) collective-permute-start(bf16[256,2560]{1,0:T(8,128)(2,1)} %bitcast.18), channel_id=1, source_target_pairs={{0,96},{16,112},{32,0},{48,16},{64,32},{80,48},{96,64},{112,80},{1... | collective-permute-start | bytes 3932168 | tf_op jit(solution)/shard_map/ppermute | solution.py:254
  12.6 9.5 %copy.6 = bf16[1280,2560]{0,1:T(8,128)(2,1)} copy(bf16[1280,2560]{1,0:T(8,128)(2,1)} %param.5) | data formatting | bytes 13107200 | tf_op args[2]
  22.1 17.0 %collective-permute-done.1.a_up = bf16[256,2560]{1,0:T(8,128)(2,1)S(1)} collective-permute-done((bf16[256,2560]{1,0:T(8,128)(2,1)}, bf16[256,2560]{1,0:T(8,128)(2,1)S(1)}, u32[]{:S(2)}, u32[]{:S(2)}) %collective-permute-start.1) | collective-permute-done | bytes 1310752 | tf_op jit(solution)/shard_map/ppermute | solution.py:254
  39.1 3.5 %collective-permute-start.3 = (bf16[128,2560]{1,0:T(8,128)(2,1)S(1)}, bf16[128,2560]{1,0:T(8,128)(2,1)S(1)}, u32[]{:S(2)}, u32[]{:S(2)}) collective-permute-start(bf16[128,2560]{1,0:T(8,128)(2,1)S(1)} %slice.6), channel_id=1, source_target_pairs={{0,96},{16,112},{32,0},{48,16},{64,32},{80,48},{96,64},{112,80},{1... | collective-permute-start | bytes 1966088 | tf_op jit(solution)/shard_map/ppermute | solution.py:257
  42.7 2.7 %collective-permute-start.5 = (bf16[256,2560]{1,0:T(8,128)(2,1)}, bf16[256,2560]{1,0:T(8,128)(2,1)}, u32[]{:S(2)}, u32[]{:S(2)}) collective-permute-start(bf16[256,2560]{1,0:T(8,128)(2,1)} %collective-permute-done.b), channel_id=1, source_target_pairs={{0,96},{16,112},{32,0},{48,16},{64,32},{80,48},{96,64},{112,80},{1... | collective-permute-start | bytes 3932168 | tf_op jit(solution)/shard_map/ppermute | solution.py:260
  45.4 9.8 %collective-permute-done.3.far_lo = bf16[128,2560]{1,0:T(8,128)(2,1)S(1)} collective-permute-done((bf16[128,2560]{1,0:T(8,128)(2,1)S(1)}, bf16[128,2560]{1,0:T(8,128)(2,1)S(1)}, u32[]{:S(2)}, u32[]{:S(2)}) %collective-permute-start.3) | collective-permute-done | bytes 655392 | tf_op jit(solution)/shard_map/ppermute | solution.py:257
  55.1 3.4 %collective-permute-done.4.far_hi = bf16[128,2560]{1,0:T(8,128)(2,1)S(1)} collective-permute-done((bf16[128,2560]{1,0:T(8,128)(2,1)S(1)}, bf16[128,2560]{1,0:T(8,128)(2,1)S(1)}, u32[]{:S(2)}, u32[]{:S(2)}) %collective-permute-start.4) | collective-permute-done | bytes 655392 | tf_op jit(solution)/shard_map/ppermute | solution.py:258
  61.9 21.5 %collective-permute-done.5.b_up = bf16[256,2560]{1,0:T(8,128)(2,1)} collective-permute-done((bf16[256,2560]{1,0:T(8,128)(2,1)}, bf16[256,2560]{1,0:T(8,128)(2,1)}, u32[]{:S(2)}, u32[]{:S(2)}) %collective-permute-start.5) | collective-permute-done | bytes 1310752 | tf_op jit(solution)/shard_map/ppermute | solution.py:260
  83.3 3.2 %collective-permute-done.6.b_dn = bf16[256,2560]{1,0:T(8,128)(2,1)} collective-permute-done((bf16[256,2560]{1,0:T(8,128)(2,1)}, bf16[256,2560]{1,0:T(8,128)(2,1)}, u32[]{:S(2)}, u32[]{:S(2)}) %collective-permute-start.6) | collective-permute-done | bytes 1310752 | tf_op jit(solution)/shard_map/ppermute | solution.py:259
  86.6 2.5 %copy-done = bf16[1,2048,1280]{2,1,0:T(8,128)(2,1)S(1)} copy-done((bf16[1,2048,1280]{2,1,0:T(8,128)(2,1)S(1)}, bf16[1,2048,1280]{2,1,0:T(8,128)(2,1)}, u32[]{:S(2)}) %copy-start) | copy-done | bytes 5242904
  91.5 5.4 %shard_map.50 = (f32[640,1024]{1,0:T(8,128)S(1)}, bf16[2048,1024]{1,0:T(8,128)(2,1)S(1)}) custom-call(s32[4]{0:T(128)S(1)} %pad_add_fusion.at, bf16[2048,1280]{1,0:T(8,128)(2,1)S(1)} %bitcast.8, bf16[256,2560]{1,0:T(8,128)(2,1)S(1)} %bitcast.21, bf16[256,2560]{1,0:T(8,128)(2,1)} %collective-permute-done.b, ...), custom_call_target="tpu_custom_call" | custom-call | flops 1 | bytes 1 | tf_op jit(solution)/shard_map/pallas_call | solution.py:274
  96.9 5.5 %collective-permute-start.8 = (f32[640,1024]{1,0:T(8,128)S(1)}, f32[640,1024]{1,0:T(8,128)S(1)}, u32[]{:S(2)}, u32[]{:S(2)}) collective-permute-start(f32[640,1024]{1,0:T(8,128)S(1)} %get-tuple-element.22), channel_id=1, source_target_pairs={{0,1},{1,0},{2,3},{3,2},{4,5},{5,4},{6,7},{7,6},{8,9},{9,8},{10,11... | collective-permute-start | bytes 7864328 | tf_op jit(solution)/shard_map/ppermute | solution.py:280
  102.4 3.7 %shard_map.51.keep = f32[640,1024]{1,0:T(8,128)S(1)} custom-call(s32[4]{0:T(128)S(1)} %pad_add_fusion.at, bf16[2048,1280]{1,0:T(8,128)(2,1)S(1)} %bitcast.9, bf16[2048,1024]{1,0:T(8,128)(2,1)S(1)} %get-tuple-element.24.grads.refs_0_), custom_call_target="tpu_custom_call" | custom-call | flops 1 | bytes 1 | tf_op jit(solution)/shard_map/pallas_call | solution.py:282
  109.5 9.0 %shard_map.53 = (f32[640,1536]{1,0:T(8,128)}, bf16[2048,1536]{1,0:T(8,128)(2,1)S(1)}) custom-call(s32[4]{0:T(128)S(1)} %pad_add_fusion.at, bf16[2048,1280]{1,0:T(8,128)(2,1)S(1)} %bitcast.12, bf16[256,2560]{1,0:T(8,128)(2,1)S(1)} %bitcast.22, bf16[256,2560]{1,0:T(8,128)(2,1)} %collective-permute-done.b, bf16[256,2560]{1,0:T(8,128)(2,1)S(1)} %collective-permute-done.1.a_up, ...), custom_call_target="tpu_custom_call" | custom-call | flops 1 | bytes 1 | tf_op jit(solution)/shard_map/pallas_call | solution.py:274
  118.5 2.7 %copy-done.1 = bf16[2048,1536]{1,0:T(8,128)(2,1)} copy-done((bf16[2048,1536]{1,0:T(8,128)(2,1)}, bf16[2048,1536]{1,0:T(8,128)(2,1)S(1)}, u32[]{:S(2)}) %copy-start.1) | copy-done | bytes 6291480
  121.6 2.8 %copy-done.2 = bf16[2048,1536]{1,0:T(8,128)(2,1)S(1)} copy-done((bf16[2048,1536]{1,0:T(8,128)(2,1)S(1)}, bf16[2048,1536]{1,0:T(8,128)(2,1)}, u32[]{:S(2)}) %copy-start.2) | copy-done | bytes 6291480
  124.4 2.2 copy-done.6
  126.6 13.4 %shard_map.54 = (bf16[528,1280]{1,0:T(8,128)(2,1)}, bf16[528,1280]{1,0:T(8,128)(2,1)S(1)}) custom-call(s32[4]{0:T(128)S(1)} %pad_add_fusion.at, bf16[2560,1280]{1,0:T(8,128)(2,1)S(1)} %bitcast.16, bf16[2048,1024]{1,0:T(8,128)(2,1)S(1)} %copy-done.6, bf16[2048,1536]{1,0:T(8,128)(2,1)S(1)} %copy-done.2), custom_call_target="tpu_custom_call" | custom-call | flops 1 | bytes 1 | tf_op jit(solution)/shard_map/pallas_call | solution.py:298
  141.4 2.5 %collective-permute-start.11 = (bf16[528,1280]{1,0:T(8,128)(2,1)S(1)}, bf16[528,1280]{1,0:T(8,128)(2,1)S(1)}, u32[]{:S(2)}, u32[]{:S(2)}) collective-permute-start(bf16[528,1280]{1,0:T(8,128)(2,1)S(1)} %get-tuple-element.33), channel_id=1, source_target_pairs={{0,12},{4,0},{8,4},{12,8},{1,13},{5,1},{9,5},{13,9},{2,14},{6,2},{... | collective-permute-start | bytes 4055048 | tf_op jit(solution)/shard_map/ppermute | solution.py:309
  143.9 2.9 %collective-permute-start.12 = (bf16[656,1024]{1,0:T(8,128)(2,1)S(1)}, bf16[656,1024]{1,0:T(8,128)(2,1)S(1)}, u32[]{:S(2)}, u32[]{:S(2)}) collective-permute-start(bf16[656,1024]{1,0:T(8,128)(2,1)S(1)} %copy-done.11), channel_id=1, source_target_pairs={{0,2},{1,3},{2,0},{3,1},{4,6},{5,7},{6,4},{7,5},{8,10},{9,11},{10,... | collective-permute-start | bytes 4030472 | tf_op jit(solution)/shard_map/ppermute | solution.py:290
  146.8 2.8 %copy-done.3 = bf16[2048,1536]{1,0:T(8,128)(2,1)S(1)} copy-done((bf16[2048,1536]{1,0:T(8,128)(2,1)S(1)}, bf16[2048,1536]{1,0:T(8,128)(2,1)}, u32[]{:S(2)}) %copy-start.3) | copy-done | bytes 6291480
  149.6 5.0 %shard_map.55.keep = f32[640,1536]{1,0:T(8,128)S(1)} custom-call(s32[4]{0:T(128)S(1)} %pad_add_fusion.at, bf16[2048,1280]{1,0:T(8,128)(2,1)S(1)} %bitcast.13, bf16[2048,1536]{1,0:T(8,128)(2,1)S(1)} %copy-done.3), custom_call_target="tpu_custom_call" | custom-call | flops 1 | bytes 1 | tf_op jit(solution)/shard_map/pallas_call | solution.py:282
  158.7 10.2 %shard_map.57 = (f32[256,1280]{1,0:T(8,128)S(1)}, f32[256,1280]{1,0:T(8,128)S(1)}, f32[512,1280]{1,0:T(8,128)S(1)}) custom-call(s32[4]{0:T(128)S(1)} %pad_add_fusion.at, bf16[2560,1280]{1,0:T(8,128)(2,1)S(1)} %bitcast.17, bf16[2048,1024]{1,0:T(8,128)(2,1)S(1)} %copy-done.7, bf16[2048,1536]{1,0:T(8,128)(2,1)S(1)} %copy-done.4), custom_call_target="tpu_custom_call" | custom-call | flops 1 | bytes 1 | tf_op jit(solution)/shard_map/pallas_call | solution.py:310
  168.9 7.1 %collective-permute-done.12.got = bf16[656,1024]{1,0:T(8,128)(2,1)S(1)} collective-permute-done((bf16[656,1024]{1,0:T(8,128)(2,1)S(1)}, bf16[656,1024]{1,0:T(8,128)(2,1)S(1)}, u32[]{:S(2)}, u32[]{:S(2)}) %collective-permute-start.12) | collective-permute-done | bytes 1343520 | tf_op jit(solution)/shard_map/ppermute | solution.py:290
  178.1 3.2 %shard_map.60 = (bf16[272,1280]{1,0:T(8,128)(2,1)S(1)}, bf16[272,1280]{1,0:T(8,128)(2,1)S(1)}) custom-call(s32[4]{0:T(128)S(1)} %pad_add_fusion.at, f32[256,1280]{1,0:T(8,128)S(1)} %get-tuple-element.35.up, f32[256,1280]{1,0:T(8,128)S(1)} %get-tuple-element.36.dn, bf16[528,1280]{1,0:T(8,128)(2,1)S(1)} %collective-permute-done.10.from_dn, ...), custom_call_target="tpu_custom_call" | custom-call | flops 1 | bytes 1 | tf_op jit(solution)/shard_map/pallas_call | solution.py:342
  181.4 2.7 %collective-permute-start.14 = (bf16[272,1280]{1,0:T(8,128)(2,1)S(1)}, bf16[272,1280]{1,0:T(8,128)(2,1)S(1)}, u32[]{:S(2)}, u32[]{:S(2)}) collective-permute-start(bf16[272,1280]{1,0:T(8,128)(2,1)S(1)} %get-tuple-element.38), channel_id=1, source_target_pairs={{0,12},{4,0},{8,4},{12,8},{1,13},{5,1},{9,5},{13,9},{2,14},{6,2},{... | collective-permute-start | bytes 2088968 | tf_op jit(solution)/shard_map/ppermute | solution.py:346
  185.9 11.6 %collective-permute-done.13.second_dn = bf16[272,1280]{1,0:T(8,128)(2,1)S(1)} collective-permute-done((bf16[272,1280]{1,0:T(8,128)(2,1)S(1)}, bf16[272,1280]{1,0:T(8,128)(2,1)S(1)}, u32[]{:S(2)}, u32[]{:S(2)}) %collective-permute-start.13) | collective-permute-done | bytes 696352 | tf_op jit(solution)/shard_map/ppermute | solution.py:345
  197.5 3.9 %shard_map.61 = bf16[512,1280]{1,0:T(8,128)(2,1)} custom-call(f32[512,1280]{1,0:T(8,128)S(1)} %get-tuple-element.32.own, bf16[528,1280]{1,0:T(8,128)(2,1)S(1)} %collective-permute-done.10.from_dn, bf16[528,1280]{1,0:T(8,128)(2,1)S(1)} %collective-permute-done.11.from_up, bf16[272,1280]{1,0:T(8,128)(2,1)S(1)} %collective-permute-done.13.second_dn, ...), custom_call_target="tpu_custom_call" | custom-call | flops 1 | bytes 1 | tf_op jit(solution)/shard_map/pallas_call | solution.py:347
  201.4 17.8 %collective-permute-done.15.got = bf16[656,1536]{1,0:T(8,128)(2,1)S(1)} collective-permute-done((bf16[656,1536]{1,0:T(8,128)(2,1)S(1)}, bf16[656,1536]{1,0:T(8,128)(2,1)S(1)}, u32[]{:S(2)}, u32[]{:S(2)}) %collective-permute-start.15) | collective-permute-done | bytes 2015264 | tf_op jit(solution)/shard_map/ppermute | solution.py:290
  219.2 2.7 %shard_map.63.own = bf16[640,1536]{1,0:T(8,128)(2,1)S(1)} custom-call(s32[4]{0:T(128)S(1)} %pad_add_fusion.at, f32[640,1536]{1,0:T(8,128)S(1)} %shard_map.62.mine, bf16[656,1536]{1,0:T(8,128)(2,1)S(1)} %collective-permute-done.15.got), custom_call_target="tpu_custom_call" | custom-call | flops 1 | bytes 1 | tf_op jit(solution)/shard_map/pallas_call | solution.py:324
  223.3 5.4 %collective-permute-done.17.other = bf16[640,1024]{1,0:T(8,128)(2,1)S(1)} collective-permute-done((bf16[640,1024]{1,0:T(8,128)(2,1)S(1)}, bf16[640,1024]{1,0:T(8,128)(2,1)S(1)}, u32[]{:S(2)}, u32[]{:S(2)}) %collective-permute-start.17) | collective-permute-done | bytes 1310752 | tf_op jit(solution)/shard_map/ppermute | solution.py:325
  230.8 2.5 %shard_map.65 = bf16[1280,2560]{1,0:T(8,128)(2,1)} custom-call(s32[4]{0:T(128)S(1)} %pad_add_fusion.at, bf16[640,1536]{1,0:T(8,128)(2,1)S(1)} %shard_map.63.own, bf16[640,1536]{1,0:T(8,128)(2,1)S(1)} %collective-permute-done.16.other, bf16[1280,2560]{1,0:T(8,128)(2,1)} %shard_map.64.old), custom_call_target="tpu_custom_call", output_to_operand_aliasing={{}: (3, {})} | custom-call | flops 1 | bytes 1 | tf_op jit(solution)/shard_map/pallas_call | solution.py:330
  (66 shorter events, 24.6 us)
Async XLA Ops:
  7.2 79.4 %all-gather.2.cloned.1.call-start = ((), (), s32[]{:S(2)}) async-start(), calls=%async_computation | async-start | bytes 6553600 | tf_op jit(solution)/shard_map/all_gather | solution.py:246
  7.9 31.1 %collective-permute-start.1 = (bf16[256,2560]{1,0:T(8,128)(2,1)}, bf16[256,2560]{1,0:T(8,128)(2,1)S(1)}, u32[]{:S(2)}, u32[]{:S(2)}) collective-permute-start(bf16[256,2560]{1,0:T(8,128)(2,1)} %bitcast.18), channel_id=1, source_target_pairs={{0,96},{16,112},{32,0},{48,16},{64,32},{80,48},{96,64},{112,80},{1... | collective-permute-start | bytes 3932168 | tf_op jit(solution)/shard_map/ppermute | solution.py:254
  11.3 31.3 %collective-permute-start.2 = (bf16[256,2560]{1,0:T(8,128)(2,1)}, bf16[256,2560]{1,0:T(8,128)(2,1)S(1)}, u32[]{:S(2)}, u32[]{:S(2)}) collective-permute-start(bf16[256,2560]{1,0:T(8,128)(2,1)} %bitcast.19), channel_id=1, source_target_pairs={{0,32},{16,48},{32,64},{48,80},{64,96},{80,112},{96,0},{112,16},{1... | collective-permute-start | bytes 3932168 | tf_op jit(solution)/shard_map/ppermute | solution.py:253
  11.3 31.4 %collective-permute-start = (bf16[256,2560]{1,0:T(8,128)(2,1)}, bf16[256,2560]{1,0:T(8,128)(2,1)}, u32[]{:S(2)}, u32[]{:S(2)}) collective-permute-start(bf16[256,2560]{1,0:T(8,128)(2,1)} %bitcast.20), channel_id=1, source_target_pairs={{0,16},{16,0},{32,48},{48,32},{64,80},{80,64},{96,112},{112,96},{1... | collective-permute-start | bytes 3932168 | tf_op jit(solution)/shard_map/ppermute | solution.py:255
  39.1 16.1 %collective-permute-start.3 = (bf16[128,2560]{1,0:T(8,128)(2,1)S(1)}, bf16[128,2560]{1,0:T(8,128)(2,1)S(1)}, u32[]{:S(2)}, u32[]{:S(2)}) collective-permute-start(bf16[128,2560]{1,0:T(8,128)(2,1)S(1)} %slice.6), channel_id=1, source_target_pairs={{0,96},{16,112},{32,0},{48,16},{64,32},{80,48},{96,64},{112,80},{1... | collective-permute-start | bytes 1966088 | tf_op jit(solution)/shard_map/ppermute | solution.py:257
  42.6 15.9 %collective-permute-start.4 = (bf16[128,2560]{1,0:T(8,128)(2,1)S(1)}, bf16[128,2560]{1,0:T(8,128)(2,1)S(1)}, u32[]{:S(2)}, u32[]{:S(2)}) collective-permute-start(bf16[128,2560]{1,0:T(8,128)(2,1)S(1)} %slice.8), channel_id=1, source_target_pairs={{0,32},{16,48},{32,64},{48,80},{64,96},{80,112},{96,0},{112,16},{1... | collective-permute-start | bytes 1966088 | tf_op jit(solution)/shard_map/ppermute | solution.py:258
  42.7 40.6 %collective-permute-start.5 = (bf16[256,2560]{1,0:T(8,128)(2,1)}, bf16[256,2560]{1,0:T(8,128)(2,1)}, u32[]{:S(2)}, u32[]{:S(2)}) collective-permute-start(bf16[256,2560]{1,0:T(8,128)(2,1)} %collective-permute-done.b), channel_id=1, source_target_pairs={{0,96},{16,112},{32,0},{48,16},{64,32},{80,48},{96,64},{112,80},{1... | collective-permute-start | bytes 3932168 | tf_op jit(solution)/shard_map/ppermute | solution.py:260
  45.4 41.2 %collective-permute-start.6 = (bf16[256,2560]{1,0:T(8,128)(2,1)}, bf16[256,2560]{1,0:T(8,128)(2,1)}, u32[]{:S(2)}, u32[]{:S(2)}) collective-permute-start(bf16[256,2560]{1,0:T(8,128)(2,1)} %collective-permute-done.b), channel_id=1, source_target_pairs={{0,32},{16,48},{32,64},{48,80},{64,96},{80,112},{96,0},{112,16},{1... | collective-permute-start | bytes 3932168 | tf_op jit(solution)/shard_map/ppermute | solution.py:259
  60.5 26.1 %collective-permute-start.7 = (bf16[256,2560]{1,0:T(8,128)(2,1)}, bf16[256,2560]{1,0:T(8,128)(2,1)}, u32[]{:S(2)}, u32[]{:S(2)}) collective-permute-start(bf16[256,2560]{1,0:T(8,128)(2,1)} %pad_maximum_fusion), channel_id=1, source_target_pairs={{0,16},{16,0},{32,48},{48,32},{64,80},{80,64},{96,112},{112,96},{1... | collective-permute-start | bytes 3932168 | tf_op jit(solution)/shard_map/ppermute | solution.py:261
  86.6 2.5 %copy-start = (bf16[1,2048,1280]{2,1,0:T(8,128)(2,1)S(1)}, bf16[1,2048,1280]{2,1,0:T(8,128)(2,1)}, u32[]{:S(2)}) copy-start(bf16[1,2048,1280]{2,1,0:T(8,128)(2,1)} %all-gather.2.cloned.1.call-done) | copy-start | bytes 15728644
  96.8 9.2 %copy-start.5 = (bf16[2048,1024]{1,0:T(8,128)(2,1)}, bf16[2048,1024]{1,0:T(8,128)(2,1)S(1)}, u32[]{:S(2)}) copy-start(bf16[2048,1024]{1,0:T(8,128)(2,1)S(1)} %get-tuple-element.24.grads.refs_0_) | copy-start | bytes 12582916
  96.9 10.0 %collective-permute-start.8 = (f32[640,1024]{1,0:T(8,128)S(1)}, f32[640,1024]{1,0:T(8,128)S(1)}, u32[]{:S(2)}, u32[]{:S(2)}) collective-permute-start(f32[640,1024]{1,0:T(8,128)S(1)} %get-tuple-element.22), channel_id=1, source_target_pairs={{0,1},{1,0},{2,3},{3,2},{4,5},{5,4},{6,7},{7,6},{8,9},{9,8},{10,11... | collective-permute-start | bytes 7864328 | tf_op jit(solution)/shard_map/ppermute | solution.py:280
  102.4 7.1 %slice-start = ((s8[5242880]{0:T(1024)(128)(4,1)}), s8[4194304]{0:T(1024)(128)(4,1)S(1)}, s32[]{:S(2)}) async-start(s8[5242880]{0:T(1024)(128)(4,1)} %bitcast.10), calls=%async_computation.1 | async-start | bytes 8388608
  102.4 7.1 %slice-start.1 = ((s8[5242880]{0:T(1024)(128)(4,1)}), s8[1048576]{0:T(1024)(128)(4,1)S(1)}, s32[]{:S(2)}) async-start(s8[5242880]{0:T(1024)(128)(4,1)} %bitcast.10), calls=%async_computation.2 | async-start | bytes 2097152
  106.1 3.4 %copy-start.13 = (bf16[1,256,2560]{2,1,0:T(8,128)(2,1)S(1)}, bf16[1,256,2560]{2,1,0:T(8,128)(2,1)}, u32[]{:S(2)}) copy-start(bf16[1,256,2560]{2,1,0:T(8,128)(2,1)} %param.4) | copy-start | bytes 3932164
  106.9 14.7 %slice-start.2 = ((s8[6553600]{0:T(1024)(128)(4,1)}), s8[4194304]{0:T(1024)(128)(4,1)S(1)}, s32[]{:S(2)}) async-start(s8[6553600]{0:T(1024)(128)(4,1)} %bitcast.14), calls=%async_computation.3 | async-start | bytes 8388608
  109.5 12.1 %slice-start.3 = ((s8[6553600]{0:T(1024)(128)(4,1)}), s8[2359296]{0:T(1024)(128)(4,1)S(1)}, s32[]{:S(2)}) async-start(s8[6553600]{0:T(1024)(128)(4,1)} %bitcast.14), calls=%async_computation.4 | async-start | bytes 4718592
  118.5 2.7 %copy-start.1 = (bf16[2048,1536]{1,0:T(8,128)(2,1)}, bf16[2048,1536]{1,0:T(8,128)(2,1)S(1)}, u32[]{:S(2)}) copy-start(bf16[2048,1536]{1,0:T(8,128)(2,1)S(1)} %get-tuple-element.28.refs_1_.grads) | copy-start | bytes 18874372
  121.2 33.4 %collective-permute-start.9 = (f32[640,1536]{1,0:T(8,128)}, f32[640,1536]{1,0:T(8,128)S(1)}, u32[]{:S(2)}, u32[]{:S(2)}) collective-permute-start(f32[640,1536]{1,0:T(8,128)} %get-tuple-element.26), channel_id=1, source_target_pairs={{0,1},{1,0},{2,3},{3,2},{4,5},{5,4},{6,7},{7,6},{8,9},{9,8},{10,11... | collective-permute-start | bytes 11796488 | tf_op jit(solution)/shard_map/ppermute | solution.py:280
  121.6 2.8 %copy-start.2 = (bf16[2048,1536]{1,0:T(8,128)(2,1)S(1)}, bf16[2048,1536]{1,0:T(8,128)(2,1)}, u32[]{:S(2)}) copy-start(bf16[2048,1536]{1,0:T(8,128)(2,1)} %copy-done.1) | copy-start | bytes 18874372
  126.6 17.3 %copy-start.11 = (bf16[656,1024]{1,0:T(8,128)(2,1)S(1)}, bf16[656,1024]{1,0:T(8,128)(2,1)}, u32[]{:S(2)}) copy-start(bf16[656,1024]{1,0:T(8,128)(2,1)} %copy-done.10) | copy-start | bytes 4030468
  140.0 38.1 %collective-permute-start.10 = (bf16[528,1280]{1,0:T(8,128)(2,1)}, bf16[528,1280]{1,0:T(8,128)(2,1)S(1)}, u32[]{:S(2)}, u32[]{:S(2)}) collective-permute-start(bf16[528,1280]{1,0:T(8,128)(2,1)} %get-tuple-element.29), channel_id=1, source_target_pairs={{0,4},{4,8},{8,12},{12,0},{1,5},{5,9},{9,13},{13,1},{2,6},{6,10},{... | collective-permute-start | bytes 4055048 | tf_op jit(solution)/shard_map/ppermute | solution.py:308
  141.4 36.7 %collective-permute-start.11 = (bf16[528,1280]{1,0:T(8,128)(2,1)S(1)}, bf16[528,1280]{1,0:T(8,128)(2,1)S(1)}, u32[]{:S(2)}, u32[]{:S(2)}) collective-permute-start(bf16[528,1280]{1,0:T(8,128)(2,1)S(1)} %get-tuple-element.33), channel_id=1, source_target_pairs={{0,12},{4,0},{8,4},{12,8},{1,13},{5,1},{9,5},{13,9},{2,14},{6,2},{... | collective-permute-start | bytes 4055048 | tf_op jit(solution)/shard_map/ppermute | solution.py:309
  143.9 32.1 %collective-permute-start.12 = (bf16[656,1024]{1,0:T(8,128)(2,1)S(1)}, bf16[656,1024]{1,0:T(8,128)(2,1)S(1)}, u32[]{:S(2)}, u32[]{:S(2)}) collective-permute-start(bf16[656,1024]{1,0:T(8,128)(2,1)S(1)} %copy-done.11), channel_id=1, source_target_pairs={{0,2},{1,3},{2,0},{3,1},{4,6},{5,7},{6,4},{7,5},{8,10},{9,11},{10,... | collective-permute-start | bytes 4030472 | tf_op jit(solution)/shard_map/ppermute | solution.py:290
  146.8 2.8 %copy-start.3 = (bf16[2048,1536]{1,0:T(8,128)(2,1)S(1)}, bf16[2048,1536]{1,0:T(8,128)(2,1)}, u32[]{:S(2)}) copy-start(bf16[2048,1536]{1,0:T(8,128)(2,1)} %copy-done.1) | copy-start | bytes 18874372
  154.6 3.7 %copy-start.4 = (bf16[2048,1536]{1,0:T(8,128)(2,1)S(1)}, bf16[2048,1536]{1,0:T(8,128)(2,1)}, u32[]{:S(2)}) copy-start(bf16[2048,1536]{1,0:T(8,128)(2,1)} %copy-done.1) | copy-start | bytes 18874372
  154.7 4.0 %copy-start.7 = (bf16[2048,1024]{1,0:T(8,128)(2,1)S(1)}, bf16[2048,1024]{1,0:T(8,128)(2,1)}, u32[]{:S(2)}) copy-start(bf16[2048,1024]{1,0:T(8,128)(2,1)} %copy-done.5) | copy-start | bytes 12582916
  156.7 62.6 %collective-permute-start.15 = (bf16[656,1536]{1,0:T(8,128)(2,1)S(1)}, bf16[656,1536]{1,0:T(8,128)(2,1)S(1)}, u32[]{:S(2)}, u32[]{:S(2)}) collective-permute-start(bf16[656,1536]{1,0:T(8,128)(2,1)S(1)} %shard_map.56.msg), channel_id=1, source_target_pairs={{0,2},{1,3},{2,0},{3,1},{4,6},{5,7},{6,4},{7,5},{8,10},{9,11},{10,... | collective-permute-start | bytes 6045704 | tf_op jit(solution)/shard_map/ppermute | solution.py:290
  181.3 16.2 %collective-permute-start.13 = (bf16[272,1280]{1,0:T(8,128)(2,1)S(1)}, bf16[272,1280]{1,0:T(8,128)(2,1)S(1)}, u32[]{:S(2)}, u32[]{:S(2)}) collective-permute-start(bf16[272,1280]{1,0:T(8,128)(2,1)S(1)} %get-tuple-element.37), channel_id=1, source_target_pairs={{0,4},{4,8},{8,12},{12,0},{1,5},{5,9},{9,13},{13,1},{2,6},{6,10},{... | collective-permute-start | bytes 2088968 | tf_op jit(solution)/shard_map/ppermute | solution.py:345
  181.4 16.1 %collective-permute-start.14 = (bf16[272,1280]{1,0:T(8,128)(2,1)S(1)}, bf16[272,1280]{1,0:T(8,128)(2,1)S(1)}, u32[]{:S(2)}, u32[]{:S(2)}) collective-permute-start(bf16[272,1280]{1,0:T(8,128)(2,1)S(1)} %get-tuple-element.38), channel_id=1, source_target_pairs={{0,12},{4,0},{8,4},{12,8},{1,13},{5,1},{9,5},{13,9},{2,14},{6,2},{... | collective-permute-start | bytes 2088968 | tf_op jit(solution)/shard_map/ppermute | solution.py:346
  221.9 8.9 %collective-permute-start.16 = (bf16[640,1536]{1,0:T(8,128)(2,1)S(1)}, bf16[640,1536]{1,0:T(8,128)(2,1)S(1)}, u32[]{:S(2)}, u32[]{:S(2)}) collective-permute-start(bf16[640,1536]{1,0:T(8,128)(2,1)S(1)} %shard_map.63.own), channel_id=1, source_target_pairs={{0,1},{1,0},{2,3},{3,2},{4,5},{5,4},{6,7},{7,6},{8,9},{9,8},{10,11... | collective-permute-start | bytes 5898248 | tf_op jit(solution)/shard_map/ppermute | solution.py:325
  223.3 5.5 %collective-permute-start.17 = (bf16[640,1024]{1,0:T(8,128)(2,1)S(1)}, bf16[640,1024]{1,0:T(8,128)(2,1)S(1)}, u32[]{:S(2)}, u32[]{:S(2)}) collective-permute-start(bf16[640,1024]{1,0:T(8,128)(2,1)S(1)} %shard_map.59.own), channel_id=1, source_target_pairs={{0,1},{1,0},{2,3},{3,2},{4,5},{5,4},{6,7},{7,6},{8,9},{9,8},{10,11... | collective-permute-start | bytes 3932168 | tf_op jit(solution)/shard_map/ppermute | solution.py:325
  (5 other events, 6.6 us)
Sparse Core Ops, SparseCore 0:
  9.7 60.3 all-gather.1

commit v2 on v0

v2 whole, which is shorter than its diff:
```python
import functools

import jax
import jax.numpy as jnp
from jax import lax
from jax.experimental import pallas as pl
from jax.experimental.pallas import tpu as pltpu
from jax.sharding import PartitionSpec as P

X_UP = [(r, (r + 2) % 8) for r in range(8)]
X_DOWN = [(r, (r - 2) % 8) for r in range(8)]
Y_SWAP = [(r, r ^ 1) for r in range(8)]
Z_UP = [(c, (c + 1) % 4) for c in range(4)]
Z_DOWN = [(c, (c - 1) % 4) for c in range(4)]
CORE_SWAP = [(d, d ^ 1) for d in range(4)]
FAR_SWAP = [(d, d ^ 2) for d in range(4)]

WIDTHS = (1280, 1280)
F32, BF16 = jnp.float32, jnp.bfloat16
ANY = pl.BlockSpec(memory_space=pl.ANY)
VMEM = pl.BlockSpec(memory_space=pltpu.VMEM)
SMEM = pl.BlockSpec(memory_space=pltpu.SMEM)
POWER = 15.0
PARTS = (1, 4)
SCHEDULE = (
    ("A", 0), ("T", 0), ("K0", 6), ("M", 150), ("P0", 0), ("K1", 0),
    ("P1", 0), ("B", 0), ("F0", 0), ("S", 30), ("L", 0), ("F1", 0),
    ("X0", 0), ("Y1", 0), ("Z1", 0),
)
TAIL = 16
STEP = 32


def call(kernel, outs, scratch=(), specs=(), out_specs=None, mib=14, aliases=None, us=0):
    return pl.pallas_call(
        kernel,
        in_specs=list(specs),
        out_specs=out_specs or [VMEM] * len(outs),
        out_shape=list(outs),
        scratch_shapes=list(scratch),
        input_output_aliases=aliases or {},
        compiler_params=pltpu.CompilerParams(vmem_limit_bytes=mib << 20),
        cost_estimate=pl.CostEstimate(flops=1 + us * 10**9, bytes_accessed=1, transcendentals=0),
    )


def after(x, *deps):
    return lax.optimization_barrier((x, *deps))[0]


def encode(srcs, dst):
    c = dst.shape[1]
    m = jnp.zeros((8, c), F32)
    for src in srcs:

        def top_of(i, m, src=src):
            v = jnp.abs(src[pl.ds(pl.multiple_of(i * STEP, STEP), STEP), :])
            return jnp.maximum(m, jnp.max(v.reshape(STEP // 8, 8, c), axis=0))

        m = lax.fori_loop(0, src.shape[0] // STEP, top_of, m)
    e = jnp.ceil(jnp.log2(jnp.clip(jnp.max(m, keepdims=True), 2.0**-118, 2.0**120)))
    scale = jnp.exp2(8.0 - e)
    first = 0
    for src in srcs:

        @pl.loop(0, src.shape[0] // STEP)
        def _(i, src=src, first=first):
            at = pl.multiple_of(i * STEP, STEP)
            v = src[pl.ds(at, STEP), :] * scale
            v2 = v * v
            v4 = v2 * v2
            dst[pl.ds(first + at, STEP), :] = ((v4 * v4) * v4 * (v2 * v)).astype(BF16)

        first += src.shape[0]
    dst[first:, :] = jnp.broadcast_to(e, (TAIL, c)).astype(BF16)


def scale_of(msg):
    n = msg.shape[0] - TAIL
    return jnp.exp2(msg[n:, 0:128].astype(F32)[0:1, 0:1] - 8.0)


def decode(y, scale):
    y = y.astype(F32)
    r = jnp.exp2(jnp.log2(jnp.abs(y)) * (1.0 / POWER)) * scale
    r = jnp.where(y == 0.0, 0.0, r)
    return jnp.where(y < 0.0, -r, r)


def looped(n, body):
    @pl.loop(0, n // STEP)
    def _(i):
        body(pl.multiple_of(i * STEP, STEP))


def turn_kernel(at, *refs):
    pieces, (out, bufs, sems) = refs[:5], refs[5:]
    rows = pieces[0].shape[0]
    copies, first = [], 0
    for i, src in enumerate(pieces):
        copies.append(pltpu.make_async_copy(src, bufs.at[pl.ds(first, src.shape[0])], sems.at[i]))
        copies[-1].start()
        first += src.shape[0]
    for copy in copies:
        copy.wait()
    for d in range(4):
        for f in range(0, out.shape[0], 256):
            tokens = pl.ds(pl.multiple_of(lax.rem(at[3] + d, 4) * rows, rows), rows)
            out[f : f + 256, tokens] = bufs[d * rows : (d + 1) * rows, f : f + 256].T


def weight_kernel(first, parts, at, inputs, *refs):
    gives, keep = refs[10 : 10 + parts], refs[10 + parts]
    weight_parts(first, at, inputs, refs[:10], gives, keep, *refs[11 + parts :])


def weight_parts(first, at, inputs, pieces, gives, keep, held, grads, sems):
    x, y, core = at[0], at[1], at[2]
    rows, width = pieces[0].shape[0], grads.shape[1]
    half = keep.shape[0]
    copies = [pltpu.make_async_copy(inputs, held, sems.at[10])]
    copies[0].start()
    for i, src in enumerate(pieces):
        d, lo = ((0, 0), (1, 0), (2, 0), (2, rows // 2), (3, 0))[i % 5]
        r = 2 * lax.rem(x + d, 4) + lax.rem(y + i // 5, 2)
        start = pl.multiple_of(r * rows + lo, rows // 2)
        dst = grads.at[pl.ds(start, src.shape[0])]
        copies.append(pltpu.make_async_copy(src.at[:, pl.ds(first, width)], dst, sems.at[i]))
        copies[-1].start()
    for copy in copies:
        copy.wait()
    def dot(which):
        features = pl.ds(pl.multiple_of(which * half, half), half)
        return jnp.dot(held[features, :], grads[...], preferred_element_type=F32)

    value, n = dot(1 - core), gives[0].shape[0]
    for i, give in enumerate(gives):
        give[...] = value[i * n : (i + 1) * n]
    keep[...] = dot(core)


def pair_kernel(at, keep, *refs):
    gots, (msg, total) = refs[:-2], refs[-2:]
    n = gots[0].shape[0]
    for k, got in enumerate(gots):

        def add(i, k=k, got=got):
            rows = pl.ds(k * n + i, STEP)
            total[rows, :] = keep[rows, :] + got[pl.ds(i, STEP), :]

        looped(n, add)
    encode([total], msg)


def decode_kernel(msg, out):
    s = scale_of(msg)

    def one(i):
        out[pl.ds(i, STEP), :] = decode(msg[pl.ds(i, STEP), :], s)

    looped(out.shape[0], one)


def final_kernel(at, mine, got, *outs):
    s = scale_of(got)
    n = outs[0].shape[0]
    for k, out in enumerate(outs):

        def add(i, k=k, out=out):
            rows = pl.ds(k * n + i, STEP)
            out[pl.ds(i, STEP), :] = (mine[rows, :] + decode(got[rows, :], s)).astype(BF16)

        looped(n, add)


def place_kernel(spots, at, *refs):
    out, sems = refs[-2:]
    copies = []
    for src, (first, other) in zip(refs, spots):
        half, width = src.shape
        which = 1 - at[2] if other else at[2]
        rows = pl.ds(pl.multiple_of(which * half, half), half)
        copies.append(pltpu.make_async_copy(src, out.at[rows, pl.ds(first, width)], sems.at[len(copies)]))
        copies[-1].start()
    for copy in copies:
        copy.wait()


def gate_kernel(at, got, out):
    out[0] = at[0]


def term_kernel(at, weight, *refs):
    pieces, (up, dn, terms, bufs, held, sems) = refs[:5], refs[5:]
    rows = bufs.shape[1]
    fetch = pltpu.make_async_copy(weight, held, sems.at[5])
    fetch.start()
    copies = []
    for i, (piece, d, lo) in enumerate(zip(pieces, (0, 1, 2, 2, 3), (0, 0, 0, rows // 2, 0))):
        copy = pltpu.make_async_copy(piece, bufs.at[d, pl.ds(lo, piece.shape[0])], sems.at[i])
        copy.start()
        copies.append((copy, d))
    fetch.wait()
    for d in range(4):
        for copy, i in copies:
            if i == d:
                copy.wait()
        s = lax.rem(at[0] + d + 4 - at[3], 4)
        terms[s] = lax.dot_general(bufs[d], held[...], (((1,), (1,)), ((), ())), preferred_element_type=F32)
    h = terms.shape[1] // 2
    lo, hi = pl.ds(0, h), pl.ds(h, h)
    encode([terms.at[2, lo], terms.at[1, hi]], up)
    encode([terms.at[3, lo], terms.at[2, hi]], dn)


def meet(terms, from_dn, from_up, sums):
    h = terms.shape[1] // 2
    dn, up = scale_of(from_dn), scale_of(from_up)

    def add(i):
        lo, hi = pl.ds(i, STEP), pl.ds(h + i, STEP)
        sums[lo, :] = terms[1, lo, :] + decode(from_dn[lo, :], dn)
        sums[hi, :] = terms[3, hi, :] + decode(from_up[hi, :], up)
        sums[pl.ds(2 * h + i, STEP), :] = terms[0, lo, :] + decode(from_up[lo, :], up)
        sums[pl.ds(3 * h + i, STEP), :] = terms[0, hi, :] + decode(from_dn[hi, :], dn)

    looped(h, add)


def meet_kernel(at, terms, from_dn, from_up, sums):
    meet(terms, from_dn, from_up, sums)


def second_kernel(at, sums_a, terms, from_dn, from_up, up, dn, sums_b):
    meet(terms, from_dn, from_up, sums_b)
    h = sums_a.shape[0] // 4
    for first, msg in ((0, up), (h, dn)):
        encode([sums_a.at[pl.ds(first, h)], sums_b.at[pl.ds(first, h)]], msg)


def last_kernel(at, sums_a, sums_b, second_dn, second_up, out):
    dn, up = scale_of(second_dn), scale_of(second_up)
    h = sums_a.shape[0] // 4
    for k, sums in enumerate((sums_a, sums_b)):
        first = lax.rem(at[1] + k, 2) * (2 * h)

        def add(i):
            msg = pl.ds(k * h + i, STEP)
            a = sums[pl.ds(2 * h + i, STEP), :] + decode(second_dn[msg, :], dn)
            b = sums[pl.ds(3 * h + i, STEP), :] + decode(second_up[msg, :], up)
            out[pl.ds(pl.multiple_of(first + i, STEP), STEP), :] = a.astype(BF16)
            out[pl.ds(pl.multiple_of(first + h + i, STEP), STEP), :] = b.astype(BF16)

        looped(h, add)


def shape(*dims, dtype=F32):
    return jax.ShapeDtypeStruct(dims, dtype)


def local(inputs, grad_out, weight):
    row, col, dp = (lax.axis_index(n) for n in ("row", "col", "dp"))
    where = jnp.stack([row // 2, row % 2, dp % 2, col]).astype(jnp.int32)
    features, outs = weight.shape
    half = features // 2
    dmas = lambda n: pltpu.SemaphoreType.DMA((n,))

    a = grad_out[0]
    rows = a.shape[0]
    h = rows // 2
    a_dn = lax.ppermute(a, "row", X_UP)
    a_up = lax.ppermute(a, "row", X_DOWN)
    b = lax.ppermute(a, "row", Y_SWAP)
    i_dn = lax.ppermute(inputs[0], "col", Z_UP)
    i_up = lax.ppermute(inputs[0], "col", Z_DOWN)
    far_lo = lax.ppermute(a_up[:h], "row", X_DOWN)
    far_hi = lax.ppermute(a_dn[h:], "row", X_UP)
    b_dn = lax.ppermute(after(b, far_hi), "row", X_UP)
    b_up = lax.ppermute(after(b, far_lo), "row", X_DOWN)
    i_far_lo = lax.ppermute(i_up[:rows], "col", Z_DOWN)
    i_far_hi = lax.ppermute(i_dn[rows:], "col", Z_UP)
    b_far_lo = lax.ppermute(far_lo, "row", Y_SWAP)
    b_far_hi = lax.ppermute(far_hi, "row", Y_SWAP)
    side_a, side_b = (a, a_up, far_lo, far_hi, a_dn), (b, b_up, b_far_lo, b_far_hi, b_dn)
    input_pieces = (inputs[0], i_up, i_far_lo, i_far_hi, i_dn)
    tokens = 8 * rows

    spans, first = [], 0
    for width in WIDTHS:
        spans.append((first, width))
        first += width

    last = []

    def ordered(kernel, outs, scratch, specs, *args, **kw):
        results = call(kernel, outs, scratch, [SMEM] + specs, **kw)(after(where, *last), *args)
        last[:] = [results[0]]
        return results

    def terms_of(side, us=0):
        msg = shape(rows + TAIL, features, dtype=BF16)
        up, dn, terms = ordered(
            term_kernel,
            [msg, msg, shape(4, rows, features)],
            [pltpu.VMEM((4, rows, outs), BF16), pltpu.VMEM((features, outs), BF16), dmas(6)],
            [ANY] * 6,
            weight,
            *side,
            mib=22,
            us=us,
        )
        return terms, lax.ppermute(up, "col", Z_UP), lax.ppermute(dn, "col", Z_DOWN)

    def weight_of(j, us=0):
        first, width = spans[j]
        parts = PARTS[j]
        *gives, keep = ordered(
            functools.partial(weight_kernel, first, parts),
            [shape(half // parts, width)] * parts + [shape(half, width)],
            [pltpu.VMEM((features, tokens), BF16), pltpu.VMEM((tokens, width), BF16), dmas(11)],
            [ANY] * 11,
            env["T"],
            *side_a,
            *side_b,
            us=us,
            mib=20,
        )
        return [keep] + [lax.ppermute(give, "dp", CORE_SWAP) for give in gives]

    def pair_of(j, us=0):
        width = spans[j][1]
        parts = env["K%d" % j]
        (msg,) = ordered(
            pair_kernel,
            [shape(half + TAIL, width, dtype=BF16)],
            [pltpu.VMEM((half, width), F32)],
            [VMEM] * len(parts),
            *parts,
            us=us,
        )
        return msg, lax.ppermute(msg, "dp", FAR_SWAP)

    def final_of(j, us=0):
        width = spans[j][1]
        sent, got = env["P%d" % j]
        (mine,) = call(decode_kernel, [shape(half, width)], (), [VMEM])(sent)
        (own,) = ordered(final_kernel, [shape(half, width, dtype=BF16)], (), [VMEM] * 2, mine, got, us=us)
        return own, lax.ppermute(own, "dp", CORE_SWAP)

    def turn(us=0):
        (turned,) = ordered(
            turn_kernel,
            [shape(features, tokens, dtype=BF16)],
            [pltpu.VMEM((tokens, features), BF16), dmas(5)],
            [ANY] * 5,
            *input_pieces,
            us=us,
        )
        return turned

    def meet_of(us=0):
        (sums,) = ordered(meet_kernel, [shape(2 * rows, features)], (), [VMEM] * 3, *env["A"], us=us)
        return sums

    def second_of(us=0):
        msg = shape(rows + TAIL, features, dtype=BF16)
        up, dn, sums = ordered(
            second_kernel, [msg, msg, shape(2 * rows, features)], (), [VMEM] * 4, env["M"], *env["B"], mib=18, us=us
        )
        return sums, lax.ppermute(up, "col", Z_UP), lax.ppermute(dn, "col", Z_DOWN)

    def last_of(us=0):
        out = [shape(2 * rows, features, dtype=BF16)]
        (grad_in,) = ordered(last_kernel, out, (), [VMEM] * 4, env["M"], *env["S"], us=us)
        return grad_in

    def place(chunks, sides, us=0):
        old = [env["X"]] if "X" in env else []
        spots = [(j, i) for j in chunks for i in sides]
        n = len(spots)
        (out,) = ordered(
            functools.partial(place_kernel, [(spans[j][0], i) for j, i in spots]),
            [shape(features, outs, dtype=BF16)],
            [dmas(n)],
            [ANY] * (n + len(old)),
            *[env["F%d" % j][i] for j, i in spots],
            *old,
            out_specs=[ANY],
            aliases={n + 1: 0} if old else None,
            us=us,
        )
        return out

    def gate(j, us):
        ordered(gate_kernel, [shape(1, dtype=jnp.int32)], (), [ANY], env["P%d" % j][1], out_specs=[SMEM], us=us)

    env = {}
    for name, us in SCHEDULE:
        if name == "A":
            env[name] = terms_of(side_a, us)
        elif name == "B":
            env[name] = terms_of(side_b, us)
        elif name[0] in "XYZ":
            env["X"] = place([int(c) for c in name[1:]], {"X": (0, 1), "Y": (0,), "Z": (1,)}[name[0]], us)
        elif name[0] == "G":
            gate(int(name[1]), us)
        elif name[0] in "KPF":
            env[name] = {"K": weight_of, "P": pair_of, "F": final_of}[name[0]](int(name[1]), us)
        else:
            env[name] = {"T": turn, "M": meet_of, "S": second_of, "L": last_of}[name](us)
    grad_in, grad_weight = env["L"], env["X"]
    return (grad_in[None], grad_weight)


def solution(mesh):
    in_specs = (P("dp", "col", "row"), P("dp", "row", "col"), P("row", "col"))
    out_specs = (P("dp", "col", "row"), P("row", "col"))
    return jax.shard_map(local, mesh=mesh, in_specs=in_specs, out_specs=out_specs, check_vma=False)
```

time: 541 us -> 195 us (0.36)
  blocking collectives: 230 us -> 0 us
  waiting for transfers between devices: 254 us -> 71.9 us
  Pallas kernels: 0 us -> 74.8 us
  matrix products: 40.5 us -> 0 us
  starting transfers between devices: 0.11 us -> 38.6 us
  between operations: 13.7 us -> 1.03 us
  local copies, waits for them, and re-layouts: 0 us -> 8.2 us
    all_gather x2 -> x0, waiting for transfers between devices: 253 us -> none  [the longest x1 212 us: local(): grads_rep = lax.all_gather(grad_out, 'row', axis=1, tiled=True)[0]]
    psum x1 -> x0, blocking collectives: 230 us -> none  [local(): grad_weight = lax.psum(partial_total, 'dp').astype(jnp.bfloat16)]
    pallas_call x0 -> x17, Pallas kernels: none -> 74.8 us  [the longest x15 71.6 us: ordered(): call(kernel, outs, scratch, [SMEM] + specs, **kw)]
    ppermute x0 -> x28, waiting for transfers between devices: none -> 71.9 us  [the longest x1 23 us: local(): a_dn = lax.ppermute(a, 'row', X_UP)]
    dot_general x2 -> x0, matrix products: 40.5 us -> none  [the longest x1 21 us: local(): lax.dot_general(input_rep, grads_rep, (((0,), (0,)), ((), ())), preferred...]
    ppermute x0 -> x28, starting transfers between devices: none -> 38.6 us  [the longest x5 5.87 us: weight_of(): return [keep] + [lax.ppermute(give, 'dp', CORE_SWAP) for give in gives]]
    unnamed x0 -> x24, local copies, waits for them, and re-layouts: none -> 7.16 us
  transfers between devices with their start and end apart: 3 -> 28, of which waited for: 2 -> 15; matrix products, arithmetic and copies ran while one was open for 7% -> 1% of each run, Pallas kernels for 0% -> 36%
where the time goes in v2:
time: 195 us
  Pallas kernels  74.8 us (38%)
  waiting for transfers between devices  71.9 us (37%)
  starting transfers between devices  38.6 us (20%)
  local copies, waits for them, and re-layouts  8.2 us (4%)
    pallas_call x15, Pallas kernels, ordered(): call(kernel, outs, scratch, [SMEM] + specs, **kw)  71.6 us
    ppermute x1, waiting for transfers between devices, local(): a_dn = lax.ppermute(a, 'row', X_UP)  23 us
    ppermute x1, waiting for transfers between devices, second_of(): lax.ppermute(dn, 'col', Z_DOWN)  10.4 us
    ppermute x1, waiting for transfers between devices, local(): far_hi = lax.ppermute(a_dn[h:], 'row', X_UP)  10 us
    ppermute x2, waiting for transfers between devices, terms_of(): lax.ppermute(dn, 'col', Z_DOWN)  9.08 us
    ppermute x5, waiting for transfers between devices, weight_of(): return [keep] + [lax.ppermute(give, 'dp', CORE_SWAP) for give in gives]  8.8 us
    unnamed x24, local copies, waits for them, and re-layouts  7.16 us
    ppermute x5, starting transfers between devices, weight_of(): return [keep] + [lax.ppermute(give, 'dp', CORE_SWAP) for give in gives]  5.87 us
  transfers between devices with their start and end apart: 28, of which 15 were waited for; matrix products, arithmetic and copies ran while one was open for 1% of the time, Pallas kernels for 36%

profile of v2, /device:TPU:1, one launch (start us, length us, event | category | flops | bytes accessed | tf_op | source)
XLA Modules:
  0.0 194.5 jit_solution(10829655455025407791)
XLA Ops:
  0.6 2.1 %collective-permute-start.2 = (bf16[256,2560]{1,0:T(8,128)(2,1)}, bf16[256,2560]{1,0:T(8,128)(2,1)S(1)}, u32[]{:S(2)}, u32[]{:S(2)}) collective-permute-start(bf16[256,2560]{1,0:T(8,128)(2,1)} %bitcast.9), channel_id=1, source_target_pairs={{0,32},{16,48},{32,64},{48,80},{64,96},{80,112},{96,0},{112,16},{1... | collective-permute-start | bytes 3932168 | tf_op jit(solution)/shard_map/ppermute | solution.py:271
  4.1 1.8 collective-permute-start.6
  7.1 2.1 %collective-permute-start.4 = (bf16[512,1280]{1,0:T(8,128)(2,1)}, bf16[512,1280]{1,0:T(8,128)(2,1)S(1)}, u32[]{:S(2)}, u32[]{:S(2)}) collective-permute-start(bf16[512,1280]{1,0:T(8,128)(2,1)} %bitcast.16), channel_id=1, source_target_pairs={{0,12},{4,0},{8,4},{12,8},{1,13},{5,1},{9,5},{13,9},{2,14},{6,2},{... | collective-permute-start | bytes 3932168 | tf_op jit(solution)/shard_map/ppermute | solution.py:275
  9.3 23.0 %collective-permute-done.2.refs_4_ = bf16[256,2560]{1,0:T(8,128)(2,1)S(1)} collective-permute-done((bf16[256,2560]{1,0:T(8,128)(2,1)}, bf16[256,2560]{1,0:T(8,128)(2,1)S(1)}, u32[]{:S(2)}, u32[]{:S(2)}) %collective-permute-start.2) | collective-permute-done | bytes 1310752 | tf_op jit(solution)/shard_map/ppermute | solution.py:271
  32.9 2.3 %collective-permute-start.1 = (bf16[128,2560]{1,0:T(8,128)(2,1)S(1)}, bf16[128,2560]{1,0:T(8,128)(2,1)}, u32[]{:S(2)}, u32[]{:S(2)}) collective-permute-start(bf16[128,2560]{1,0:T(8,128)(2,1)S(1)} %slice.16), channel_id=1, source_target_pairs={{0,96},{16,112},{32,0},{48,16},{64,32},{80,48},{96,64},{112,80},{1... | collective-permute-start | bytes 1966088 | tf_op jit(solution)/shard_map/ppermute | solution.py:276
  38.3 10.0 %collective-permute-done.3.refs_3_ = bf16[128,2560]{1,0:T(8,128)(2,1)} collective-permute-done((bf16[128,2560]{1,0:T(8,128)(2,1)S(1)}, bf16[128,2560]{1,0:T(8,128)(2,1)}, u32[]{:S(2)}, u32[]{:S(2)}) %collective-permute-start.3) | collective-permute-done | bytes 655392 | tf_op jit(solution)/shard_map/ppermute | solution.py:277
  48.3 2.7 %collective-permute-start.9 = (bf16[256,2560]{1,0:T(8,128)(2,1)}, bf16[256,2560]{1,0:T(8,128)(2,1)}, u32[]{:S(2)}, u32[]{:S(2)}) collective-permute-start(bf16[256,2560]{1,0:T(8,128)(2,1)} %collective-permute-done.8.refs_5_.refs_0_), channel_id=1, source_target_pairs={{0,96},{16,112},{32,0},{48,16},{64,32},{80,48},{96,64},{112,80},{1... | collective-permute-start | bytes 3932168 | tf_op jit(solution)/shard_map/ppermute | solution.py:279
  52.9 4.2 %collective-permute-start.5 = (bf16[256,1280]{1,0:T(8,128)(2,1)}, bf16[256,1280]{1,0:T(8,128)(2,1)}, u32[]{:S(2)}, u32[]{:S(2)}) collective-permute-start(bf16[256,1280]{1,0:T(8,128)(2,1)} %slice.18), channel_id=1, source_target_pairs={{0,12},{4,0},{8,4},{12,8},{1,13},{5,1},{9,5},{13,9},{2,14},{6,2},{... | collective-permute-start | bytes 1966088 | tf_op jit(solution)/shard_map/ppermute | solution.py:280
  59.5 2.9 %copy-done = bf16[1280,2560]{1,0:T(8,128)(2,1)S(1)} copy-done((bf16[1280,2560]{1,0:T(8,128)(2,1)S(1)}, bf16[1280,2560]{1,0:T(8,128)(2,1)}, u32[]{:S(2)}) %copy-start) | copy-done | bytes 6553624
  63.7 11.4 %shard_map.50 = (bf16[272,1280]{1,0:T(8,128)(2,1)S(1)}, bf16[272,1280]{1,0:T(8,128)(2,1)S(1)}, f32[4,256,1280]{2,1,0:T(8,128)S(1)}) custom-call(s32[4]{0:T(128)S(1)} %pad_add_fusion.at, bf16[1280,2560]{1,0:T(8,128)(2,1)S(1)} %copy-done, bf16[256,2560]{1,0:T(8,128)(2,1)S(1)} %bitcast.12, bf16[256,2560]{1,0:T(8,128)(2,1)S(1)} %collective-permute-done.refs_1_, ...), custom_call_target="tpu_custom_call" | custom-call | flops 1 | bytes 1 | tf_op jit(solution)/shard_map/pallas_call | solution.py:296
  76.7 3.4 %shard_map.51.inputs = bf16[1280,2048]{1,0:T(8,128)(2,1)S(1)} custom-call(s32[4]{0:T(128)S(1)} %pad_add_fusion.at, bf16[512,1280]{1,0:T(8,128)(2,1)S(1)} %bitcast.17, bf16[512,1280]{1,0:T(8,128)(2,1)S(1)} %copy-done.6, bf16[256,1280]{1,0:T(8,128)(2,1)} %collective-permute-done.5.refs_2_, bf16[256,1280]{1,0:T(8,128)(2,1)S(1)} %copy-done.9, ...), custom_call_target="tpu_custom_call" | custom-call | flops 1 | bytes 1 | tf_op jit(solution)/shard_map/pallas_call | solution.py:296
  80.1 4.3 %collective-permute-done.10.refs_7_.refs_2_ = bf16[128,2560]{1,0:T(8,128)(2,1)} collective-permute-done((bf16[128,2560]{1,0:T(8,128)(2,1)}, bf16[128,2560]{1,0:T(8,128)(2,1)}, u32[]{:S(2)}, u32[]{:S(2)}) %collective-permute-start.10) | collective-permute-done | bytes 655392 | tf_op jit(solution)/shard_map/ppermute | solution.py:282
  84.4 9.8 %shard_map.52 = (f32[640,1280]{1,0:T(8,128)}, f32[640,1280]{1,0:T(8,128)S(1)}) custom-call(s32[4]{0:T(128)S(1)} %pad_add_fusion.at, bf16[1280,2048]{1,0:T(8,128)(2,1)S(1)} %shard_map.51.inputs, bf16[256,2560]{1,0:T(8,128)(2,1)S(1)} %bitcast.13, bf16[256,2560]{1,0:T(8,128)(2,1)S(1)} %collective-permute-done.refs_1_, ...), custom_call_target="tpu_custom_call" | custom-call | flops 6000000000 | bytes 1 | tf_op jit(solution)/shard_map/pallas_call | solution.py:296
  94.2 4.3 %collective-permute-start.15 = (f32[640,1280]{1,0:T(8,128)}, f32[640,1280]{1,0:T(8,128)}, u32[]{:S(2)}, u32[]{:S(2)}) collective-permute-start(f32[640,1280]{1,0:T(8,128)} %get-tuple-element.39), channel_id=1, source_target_pairs={{0,1},{1,0},{2,3},{3,2},{4,5},{5,4},{6,7},{7,6},{8,9},{9,8},{10,11... | collective-permute-start | bytes 9830408 | tf_op jit(solution)/shard_map/ppermute | solution.py:328
  98.6 1.9 shard_map.53.sums_a
  100.4 3.9 %collective-permute-done.15.refs_0_ = f32[640,1280]{1,0:T(8,128)} collective-permute-done((f32[640,1280]{1,0:T(8,128)}, f32[640,1280]{1,0:T(8,128)}, u32[]{:S(2)}, u32[]{:S(2)}) %collective-permute-start.15) | collective-permute-done | bytes 3276832 | tf_op jit(solution)/shard_map/ppermute | solution.py:328
  104.4 3.8 %shard_map.54.msg = bf16[656,1280]{1,0:T(8,128)(2,1)S(1)} custom-call(s32[4]{0:T(128)S(1)} %pad_add_fusion.at, f32[640,1280]{1,0:T(8,128)S(1)} %get-tuple-element.44.keep, f32[640,1280]{1,0:T(8,128)} %collective-permute-done.15.refs_0_), custom_call_target="tpu_custom_call" | custom-call | flops 1 | bytes 1 | tf_op jit(solution)/shard_map/pallas_call | solution.py:296
  108.2 3.0 %collective-permute-start.20 = (bf16[656,1280]{1,0:T(8,128)(2,1)S(1)}, bf16[656,1280]{1,0:T(8,128)(2,1)S(1)}, u32[]{:S(2)}, u32[]{:S(2)}) collective-permute-start(bf16[656,1280]{1,0:T(8,128)(2,1)S(1)} %shard_map.54.msg), channel_id=1, source_target_pairs={{0,2},{1,3},{2,0},{3,1},{4,6},{5,7},{6,4},{7,5},{8,10},{9,11},{10,... | collective-permute-start | bytes 5038088 | tf_op jit(solution)/shard_map/ppermute | solution.py:341
  111.2 9.8 %shard_map.55 = (f32[160,1280]{1,0:T(8,128)S(1)}, f32[160,1280]{1,0:T(8,128)S(1)}, f32[160,1280]{1,0:T(8,128)S(1)}, f32[160,1280]{1,0:T(8,128)S(1)}, f32[640,1280]{1,0:T(8,128)S(1)}) custom-call(s32[4]{0:T(128)S(1)} %pad_add_fusion.at, bf16[1280,2048]{1,0:T(8,128)(2,1)S(1)} %shard_map.51.inputs, bf16[256,2560]{1,0:T(8,128)(2,1)S(1)} %bitcast.14, ...), custom_call_target="tpu_custom_call" | custom-call | flops 1 | bytes 1 | tf_op jit(solution)/shard_map/pallas_call | solution.py:296
  127.5 2.3 %shard_map.56.msg = bf16[656,1280]{1,0:T(8,128)(2,1)S(1)} custom-call(s32[4]{0:T(128)S(1)} %pad_add_fusion.at, f32[640,1280]{1,0:T(8,128)S(1)} %get-tuple-element.48.keep, f32[160,1280]{1,0:T(8,128)S(1)} %collective-permute-done.16.refs_0_, f32[160,1280]{1,0:T(8,128)S(1)} %collective-permute-done.17.refs_1_, ...), custom_call_target="tpu_custom_call" | custom-call | flops 1 | bytes 1 | tf_op jit(solution)/shard_map/pallas_call | solution.py:296
  129.8 12.5 %shard_map.57 = (bf16[272,1280]{1,0:T(8,128)(2,1)S(1)}, bf16[272,1280]{1,0:T(8,128)(2,1)S(1)}, f32[4,256,1280]{2,1,0:T(8,128)S(1)}) custom-call(s32[4]{0:T(128)S(1)} %pad_add_fusion.at, bf16[1280,2560]{1,0:T(8,128)(2,1)S(1)} %bitcast.8, bf16[256,2560]{1,0:T(8,128)(2,1)} %collective-permute-done.8.refs_5_.refs_0_, ...), custom_call_target="tpu_custom_call" | custom-call | flops 1 | bytes 1 | tf_op jit(solution)/shard_map/pallas_call | solution.py:296
  145.6 2.1 %collective-permute-done.20.got = bf16[656,1280]{1,0:T(8,128)(2,1)S(1)} collective-permute-done((bf16[656,1280]{1,0:T(8,128)(2,1)S(1)}, bf16[656,1280]{1,0:T(8,128)(2,1)S(1)}, u32[]{:S(2)}, u32[]{:S(2)}) %collective-permute-start.20) | collective-permute-done | bytes 1679392 | tf_op jit(solution)/shard_map/ppermute | solution.py:341
  147.7 2.4 %shard_map.59.refs_0_ = bf16[640,1280]{1,0:T(8,128)(2,1)S(1)} custom-call(s32[4]{0:T(128)S(1)} %pad_add_fusion.at, f32[640,1280]{1,0:T(8,128)S(1)} %shard_map.58.mine, bf16[656,1280]{1,0:T(8,128)(2,1)S(1)} %collective-permute-done.20.got), custom_call_target="tpu_custom_call" | custom-call | flops 1 | bytes 1 | tf_op jit(solution)/shard_map/pallas_call | solution.py:296
  150.1 9.1 %collective-permute-done.22.from_up = bf16[272,1280]{1,0:T(8,128)(2,1)S(1)} collective-permute-done((bf16[272,1280]{1,0:T(8,128)(2,1)S(1)}, bf16[272,1280]{1,0:T(8,128)(2,1)S(1)}, u32[]{:S(2)}, u32[]{:S(2)}) %collective-permute-start.22) | collective-permute-done | bytes 696352 | tf_op jit(solution)/shard_map/ppermute | solution.py:312
  160.2 3.1 %shard_map.60 = (bf16[272,1280]{1,0:T(8,128)(2,1)S(1)}, bf16[272,1280]{1,0:T(8,128)(2,1)S(1)}, f32[512,1280]{1,0:T(8,128)S(1)}) custom-call(s32[4]{0:T(128)S(1)} %pad_add_fusion.at, f32[512,1280]{1,0:T(8,128)S(1)} %shard_map.53.sums_a, f32[4,256,1280]{2,1,0:T(8,128)S(1)} %get-tuple-element.56.terms, bf16[272,1280]{1,0:T(8,128)(2,1)S(1)} %collective-permute-done.21.from_dn, ...), custom_call_target="tpu_custom_call" | custom-call | flops 30000001024 | bytes 1 | tf_op jit(solution)/shard_map/pallas_call | solution.py:296
  166.4 2.2 %collective-permute-start.26 = (bf16[640,1280]{1,0:T(8,128)(2,1)S(1)}, bf16[640,1280]{1,0:T(8,128)(2,1)S(1)}, u32[]{:S(2)}, u32[]{:S(2)}) collective-permute-start(bf16[640,1280]{1,0:T(8,128)(2,1)S(1)} %shard_map.59.refs_0_), channel_id=1, source_target_pairs={{0,1},{1,0},{2,3},{3,2},{4,5},{5,4},{6,7},{7,6},{8,9},{9,8},{10,11... | collective-permute-start | bytes 4915208 | tf_op jit(solution)/shard_map/ppermute | solution.py:348
  168.6 10.4 %collective-permute-done.24.second_up = bf16[272,1280]{1,0:T(8,128)(2,1)S(1)} collective-permute-done((bf16[272,1280]{1,0:T(8,128)(2,1)S(1)}, bf16[272,1280]{1,0:T(8,128)(2,1)S(1)}, u32[]{:S(2)}, u32[]{:S(2)}) %collective-permute-start.24) | collective-permute-done | bytes 696352 | tf_op jit(solution)/shard_map/ppermute | solution.py:370
  180.5 3.0 %shard_map.61 = bf16[512,1280]{1,0:T(8,128)(2,1)} custom-call(s32[4]{0:T(128)S(1)} %pad_add_fusion.at, f32[512,1280]{1,0:T(8,128)S(1)} %shard_map.53.sums_a, f32[512,1280]{1,0:T(8,128)S(1)} %get-tuple-element.60.sums_b, bf16[272,1280]{1,0:T(8,128)(2,1)S(1)} %collective-permute-done.23.second_dn, bf16[272,1280]{1,0:T(8,128)(2,1)S(1)} %collective-permute-done.24.second_up), custom_call_target="tpu_custom_call" | custom-call | flops 1 | bytes 1 | tf_op jit(solution)/shard_map/pallas_call | solution.py:296
  184.3 2.4 %shard_map.63.refs_0_ = bf16[640,1280]{1,0:T(8,128)(2,1)S(1)} custom-call(s32[4]{0:T(128)S(1)} %pad_add_fusion.at, f32[640,1280]{1,0:T(8,128)S(1)} %shard_map.62.mine, bf16[656,1280]{1,0:T(8,128)(2,1)S(1)} %collective-permute-done.25.got), custom_call_target="tpu_custom_call" | custom-call | flops 1 | bytes 1 | tf_op jit(solution)/shard_map/pallas_call | solution.py:296
  186.7 1.9 collective-permute-start.27
  188.6 2.3 %shard_map.64.refs_1_ = bf16[1280,2560]{1,0:T(8,128)(2,1)} custom-call(s32[4]{0:T(128)S(1)} %pad_add_fusion.at, bf16[640,1280]{1,0:T(8,128)(2,1)S(1)} %shard_map.59.refs_0_, bf16[640,1280]{1,0:T(8,128)(2,1)S(1)} %collective-permute-done.26.refs_1_), custom_call_target="tpu_custom_call" | custom-call | flops 1 | bytes 1 | tf_op jit(solution)/shard_map/pallas_call | solution.py:296
  192.6 1.7 shard_map.66
  (71 shorter events, 31.4 us)
Async XLA Ops:
  0.6 31.6 %collective-permute-start.2 = (bf16[256,2560]{1,0:T(8,128)(2,1)}, bf16[256,2560]{1,0:T(8,128)(2,1)S(1)}, u32[]{:S(2)}, u32[]{:S(2)}) collective-permute-start(bf16[256,2560]{1,0:T(8,128)(2,1)} %bitcast.9), channel_id=1, source_target_pairs={{0,32},{16,48},{32,64},{48,80},{64,96},{80,112},{96,0},{112,16},{1... | collective-permute-start | bytes 3932168 | tf_op jit(solution)/shard_map/ppermute | solution.py:271
  2.7 30.1 %collective-permute-start = (bf16[256,2560]{1,0:T(8,128)(2,1)}, bf16[256,2560]{1,0:T(8,128)(2,1)S(1)}, u32[]{:S(2)}, u32[]{:S(2)}) collective-permute-start(bf16[256,2560]{1,0:T(8,128)(2,1)} %bitcast.10), channel_id=1, source_target_pairs={{0,96},{16,112},{32,0},{48,16},{64,32},{80,48},{96,64},{112,80},{1... | collective-permute-start | bytes 3932168 | tf_op jit(solution)/shard_map/ppermute | solution.py:272
  4.1 31.9 %collective-permute-start.6 = (bf16[512,1280]{1,0:T(8,128)(2,1)}, bf16[512,1280]{1,0:T(8,128)(2,1)S(1)}, u32[]{:S(2)}, u32[]{:S(2)}) collective-permute-start(bf16[512,1280]{1,0:T(8,128)(2,1)} %bitcast.15), channel_id=1, source_target_pairs={{0,4},{4,8},{8,12},{12,0},{1,5},{5,9},{9,13},{13,1},{2,6},{6,10},{... | collective-permute-start | bytes 3932168 | tf_op jit(solution)/shard_map/ppermute | solution.py:274
  5.8 32.4 %collective-permute-start.8 = (bf16[256,2560]{1,0:T(8,128)(2,1)}, bf16[256,2560]{1,0:T(8,128)(2,1)}, u32[]{:S(2)}, u32[]{:S(2)}) collective-permute-start(bf16[256,2560]{1,0:T(8,128)(2,1)} %bitcast.11), channel_id=1, source_target_pairs={{0,16},{16,0},{32,48},{48,32},{64,80},{80,64},{96,112},{112,96},{1... | collective-permute-start | bytes 3932168 | tf_op jit(solution)/shard_map/ppermute | solution.py:273
  7.1 43.8 %collective-permute-start.4 = (bf16[512,1280]{1,0:T(8,128)(2,1)}, bf16[512,1280]{1,0:T(8,128)(2,1)S(1)}, u32[]{:S(2)}, u32[]{:S(2)}) collective-permute-start(bf16[512,1280]{1,0:T(8,128)(2,1)} %bitcast.16), channel_id=1, source_target_pairs={{0,12},{4,0},{8,4},{12,8},{1,13},{5,1},{9,5},{13,9},{2,14},{6,2},{... | collective-permute-start | bytes 3932168 | tf_op jit(solution)/shard_map/ppermute | solution.py:275
  32.3 15.9 %collective-permute-start.3 = (bf16[128,2560]{1,0:T(8,128)(2,1)S(1)}, bf16[128,2560]{1,0:T(8,128)(2,1)}, u32[]{:S(2)}, u32[]{:S(2)}) collective-permute-start(bf16[128,2560]{1,0:T(8,128)(2,1)S(1)} %slice.17), channel_id=1, source_target_pairs={{0,32},{16,48},{32,64},{48,80},{64,96},{80,112},{96,0},{112,16},{1... | collective-permute-start | bytes 1966088 | tf_op jit(solution)/shard_map/ppermute | solution.py:277
  32.9 15.4 %collective-permute-start.1 = (bf16[128,2560]{1,0:T(8,128)(2,1)S(1)}, bf16[128,2560]{1,0:T(8,128)(2,1)}, u32[]{:S(2)}, u32[]{:S(2)}) collective-permute-start(bf16[128,2560]{1,0:T(8,128)(2,1)S(1)} %slice.16), channel_id=1, source_target_pairs={{0,96},{16,112},{32,0},{48,16},{64,32},{80,48},{96,64},{112,80},{1... | collective-permute-start | bytes 1966088 | tf_op jit(solution)/shard_map/ppermute | solution.py:276
  37.1 21.3 %collective-permute-start.7 = (bf16[256,1280]{1,0:T(8,128)(2,1)S(1)}, bf16[256,1280]{1,0:T(8,128)(2,1)S(1)}, u32[]{:S(2)}, u32[]{:S(2)}) collective-permute-start(bf16[256,1280]{1,0:T(8,128)(2,1)S(1)} %slice.19), channel_id=1, source_target_pairs={{0,4},{4,8},{8,12},{12,0},{1,5},{5,9},{9,13},{13,1},{2,6},{6,10},{... | collective-permute-start | bytes 1966088 | tf_op jit(solution)/shard_map/ppermute | solution.py:281
  48.3 36.1 %collective-permute-start.12 = (bf16[256,2560]{1,0:T(8,128)(2,1)}, bf16[256,2560]{1,0:T(8,128)(2,1)}, u32[]{:S(2)}, u32[]{:S(2)}) collective-permute-start(bf16[256,2560]{1,0:T(8,128)(2,1)} %collective-permute-done.8.refs_5_.refs_0_), channel_id=1, source_target_pairs={{0,32},{16,48},{32,64},{48,80},{64,96},{80,112},{96,0},{112,16},{1... | collective-permute-start | bytes 3932168 | tf_op jit(solution)/shard_map/ppermute | solution.py:278
  48.3 36.1 %collective-permute-start.9 = (bf16[256,2560]{1,0:T(8,128)(2,1)}, bf16[256,2560]{1,0:T(8,128)(2,1)}, u32[]{:S(2)}, u32[]{:S(2)}) collective-permute-start(bf16[256,2560]{1,0:T(8,128)(2,1)} %collective-permute-done.8.refs_5_.refs_0_), channel_id=1, source_target_pairs={{0,96},{16,112},{32,0},{48,16},{64,32},{80,48},{96,64},{112,80},{1... | collective-permute-start | bytes 3932168 | tf_op jit(solution)/shard_map/ppermute | solution.py:279
  52.9 22.2 %collective-permute-start.5 = (bf16[256,1280]{1,0:T(8,128)(2,1)}, bf16[256,1280]{1,0:T(8,128)(2,1)}, u32[]{:S(2)}, u32[]{:S(2)}) collective-permute-start(bf16[256,1280]{1,0:T(8,128)(2,1)} %slice.18), channel_id=1, source_target_pairs={{0,12},{4,0},{8,4},{12,8},{1,13},{5,1},{9,5},{13,9},{2,14},{6,2},{... | collective-permute-start | bytes 1966088 | tf_op jit(solution)/shard_map/ppermute | solution.py:280
  57.1 18.2 %collective-permute-start.11 = (bf16[128,2560]{1,0:T(8,128)(2,1)}, bf16[128,2560]{1,0:T(8,128)(2,1)S(1)}, u32[]{:S(2)}, u32[]{:S(2)}) collective-permute-start(bf16[128,2560]{1,0:T(8,128)(2,1)} %collective-permute-done.3.refs_3_), channel_id=1, source_target_pairs={{0,16},{16,0},{32,48},{48,32},{64,80},{80,64},{96,112},{112,96},{1... | collective-permute-start | bytes 1966088 | tf_op jit(solution)/shard_map/ppermute | solution.py:283
  59.3 25.1 %collective-permute-start.10 = (bf16[128,2560]{1,0:T(8,128)(2,1)}, bf16[128,2560]{1,0:T(8,128)(2,1)}, u32[]{:S(2)}, u32[]{:S(2)}) collective-permute-start(bf16[128,2560]{1,0:T(8,128)(2,1)} %collective-permute-done.1.refs_2_), channel_id=1, source_target_pairs={{0,16},{16,0},{32,48},{48,32},{64,80},{80,64},{96,112},{112,96},{1... | collective-permute-start | bytes 1966088 | tf_op jit(solution)/shard_map/ppermute | solution.py:282
  63.7 13.0 %copy-start.7 = (bf16[1,512,1280]{2,1,0:T(8,128)(2,1)S(1)}, bf16[1,512,1280]{2,1,0:T(8,128)(2,1)}, u32[]{:S(2)}) copy-start(bf16[1,512,1280]{2,1,0:T(8,128)(2,1)} %param.3) | copy-start | bytes 3932164
  63.7 13.0 %copy-start.9 = (bf16[256,1280]{1,0:T(8,128)(2,1)S(1)}, bf16[256,1280]{1,0:T(8,128)(2,1)}, u32[]{:S(2)}) copy-start(bf16[256,1280]{1,0:T(8,128)(2,1)} %copy-done.8) | copy-start | bytes 1966084
  75.1 23.4 %collective-permute-start.14 = (bf16[272,1280]{1,0:T(8,128)(2,1)S(1)}, bf16[272,1280]{1,0:T(8,128)(2,1)S(1)}, u32[]{:S(2)}, u32[]{:S(2)}) collective-permute-start(bf16[272,1280]{1,0:T(8,128)(2,1)S(1)} %get-tuple-element.42), channel_id=1, source_target_pairs={{0,12},{4,0},{8,4},{12,8},{1,13},{5,1},{9,5},{13,9},{2,14},{6,2},{... | collective-permute-start | bytes 2088968 | tf_op jit(solution)/shard_map/ppermute | solution.py:312
  75.3 23.2 %collective-permute-start.13 = (bf16[272,1280]{1,0:T(8,128)(2,1)S(1)}, bf16[272,1280]{1,0:T(8,128)(2,1)S(1)}, u32[]{:S(2)}, u32[]{:S(2)}) collective-permute-start(bf16[272,1280]{1,0:T(8,128)(2,1)S(1)} %get-tuple-element.34), channel_id=1, source_target_pairs={{0,4},{4,8},{8,12},{12,0},{1,5},{5,9},{9,13},{13,1},{2,6},{6,10},{... | collective-permute-start | bytes 2088968 | tf_op jit(solution)/shard_map/ppermute | solution.py:312
  94.2 10.1 %collective-permute-start.15 = (f32[640,1280]{1,0:T(8,128)}, f32[640,1280]{1,0:T(8,128)}, u32[]{:S(2)}, u32[]{:S(2)}) collective-permute-start(f32[640,1280]{1,0:T(8,128)} %get-tuple-element.39), channel_id=1, source_target_pairs={{0,1},{1,0},{2,3},{3,2},{4,5},{5,4},{6,7},{7,6},{8,9},{9,8},{10,11... | collective-permute-start | bytes 9830408 | tf_op jit(solution)/shard_map/ppermute | solution.py:328
  104.4 25.4 %slice-start = ((s8[6553600]{0:T(1024)(128)(4,1)}), s8[4194304]{0:T(1024)(128)(4,1)S(1)}, s32[]{:S(2)}) async-start(s8[6553600]{0:T(1024)(128)(4,1)} %bitcast.7), calls=%async_computation | async-start | bytes 8388608
  108.2 21.6 %slice-start.1 = ((s8[6553600]{0:T(1024)(128)(4,1)}), s8[2359296]{0:T(1024)(128)(4,1)S(1)}, s32[]{:S(2)}) async-start(s8[6553600]{0:T(1024)(128)(4,1)} %bitcast.7), calls=%async_computation.1 | async-start | bytes 4718592
  108.2 39.5 %collective-permute-start.20 = (bf16[656,1280]{1,0:T(8,128)(2,1)S(1)}, bf16[656,1280]{1,0:T(8,128)(2,1)S(1)}, u32[]{:S(2)}, u32[]{:S(2)}) collective-permute-start(bf16[656,1280]{1,0:T(8,128)(2,1)S(1)} %shard_map.54.msg), channel_id=1, source_target_pairs={{0,2},{1,3},{2,0},{3,1},{4,6},{5,7},{6,4},{7,5},{8,10},{9,11},{10,... | collective-permute-start | bytes 5038088 | tf_op jit(solution)/shard_map/ppermute | solution.py:341
  121.1 2.9 %collective-permute-start.17 = (f32[160,1280]{1,0:T(8,128)S(1)}, f32[160,1280]{1,0:T(8,128)S(1)}, u32[]{:S(2)}, u32[]{:S(2)}) collective-permute-start(f32[160,1280]{1,0:T(8,128)S(1)} %get-tuple-element.49), channel_id=1, source_target_pairs={{0,1},{1,0},{2,3},{3,2},{4,5},{5,4},{6,7},{7,6},{8,9},{9,8},{10,11... | collective-permute-start | bytes 2457608 | tf_op jit(solution)/shard_map/ppermute | solution.py:328
  122.0 3.1 %collective-permute-start.18 = (f32[160,1280]{1,0:T(8,128)S(1)}, f32[160,1280]{1,0:T(8,128)S(1)}, u32[]{:S(2)}, u32[]{:S(2)}) collective-permute-start(f32[160,1280]{1,0:T(8,128)S(1)} %get-tuple-element.50), channel_id=1, source_target_pairs={{0,1},{1,0},{2,3},{3,2},{4,5},{5,4},{6,7},{7,6},{8,9},{9,8},{10,11... | collective-permute-start | bytes 2457608 | tf_op jit(solution)/shard_map/ppermute | solution.py:328
  122.1 4.2 %collective-permute-start.19 = (f32[160,1280]{1,0:T(8,128)S(1)}, f32[160,1280]{1,0:T(8,128)S(1)}, u32[]{:S(2)}, u32[]{:S(2)}) collective-permute-start(f32[160,1280]{1,0:T(8,128)S(1)} %get-tuple-element.51), channel_id=1, source_target_pairs={{0,1},{1,0},{2,3},{3,2},{4,5},{5,4},{6,7},{7,6},{8,9},{9,8},{10,11... | collective-permute-start | bytes 2457608 | tf_op jit(solution)/shard_map/ppermute | solution.py:328
  122.5 5.0 %collective-permute-start.16 = (f32[160,1280]{1,0:T(8,128)S(1)}, f32[160,1280]{1,0:T(8,128)S(1)}, u32[]{:S(2)}, u32[]{:S(2)}) collective-permute-start(f32[160,1280]{1,0:T(8,128)S(1)} %get-tuple-element.46), channel_id=1, source_target_pairs={{0,1},{1,0},{2,3},{3,2},{4,5},{5,4},{6,7},{7,6},{8,9},{9,8},{10,11... | collective-permute-start | bytes 2457608 | tf_op jit(solution)/shard_map/ppermute | solution.py:328
  142.3 16.9 %collective-permute-start.22 = (bf16[272,1280]{1,0:T(8,128)(2,1)S(1)}, bf16[272,1280]{1,0:T(8,128)(2,1)S(1)}, u32[]{:S(2)}, u32[]{:S(2)}) collective-permute-start(bf16[272,1280]{1,0:T(8,128)(2,1)S(1)} %get-tuple-element.57), channel_id=1, source_target_pairs={{0,12},{4,0},{8,4},{12,8},{1,13},{5,1},{9,5},{13,9},{2,14},{6,2},{... | collective-permute-start | bytes 2088968 | tf_op jit(solution)/shard_map/ppermute | solution.py:312
  142.5 17.7 %collective-permute-start.21 = (bf16[272,1280]{1,0:T(8,128)(2,1)S(1)}, bf16[272,1280]{1,0:T(8,128)(2,1)S(1)}, u32[]{:S(2)}, u32[]{:S(2)}) collective-permute-start(bf16[272,1280]{1,0:T(8,128)(2,1)S(1)} %get-tuple-element.53), channel_id=1, source_target_pairs={{0,4},{4,8},{8,12},{12,0},{1,5},{5,9},{9,13},{13,1},{2,6},{6,10},{... | collective-permute-start | bytes 2088968 | tf_op jit(solution)/shard_map/ppermute | solution.py:312
  145.4 38.8 %collective-permute-start.25 = (bf16[656,1280]{1,0:T(8,128)(2,1)S(1)}, bf16[656,1280]{1,0:T(8,128)(2,1)S(1)}, u32[]{:S(2)}, u32[]{:S(2)}) collective-permute-start(bf16[656,1280]{1,0:T(8,128)(2,1)S(1)} %shard_map.56.msg), channel_id=1, source_target_pairs={{0,2},{1,3},{2,0},{3,1},{4,6},{5,7},{6,4},{7,5},{8,10},{9,11},{10,... | collective-permute-start | bytes 5038088 | tf_op jit(solution)/shard_map/ppermute | solution.py:341
  163.3 15.7 %collective-permute-start.24 = (bf16[272,1280]{1,0:T(8,128)(2,1)S(1)}, bf16[272,1280]{1,0:T(8,128)(2,1)S(1)}, u32[]{:S(2)}, u32[]{:S(2)}) collective-permute-start(bf16[272,1280]{1,0:T(8,128)(2,1)S(1)} %get-tuple-element.61), channel_id=1, source_target_pairs={{0,12},{4,0},{8,4},{12,8},{1,13},{5,1},{9,5},{13,9},{2,14},{6,2},{... | collective-permute-start | bytes 2088968 | tf_op jit(solution)/shard_map/ppermute | solution.py:370
  163.7 16.8 %collective-permute-start.23 = (bf16[272,1280]{1,0:T(8,128)(2,1)S(1)}, bf16[272,1280]{1,0:T(8,128)(2,1)S(1)}, u32[]{:S(2)}, u32[]{:S(2)}) collective-permute-start(bf16[272,1280]{1,0:T(8,128)(2,1)S(1)} %get-tuple-element.58), channel_id=1, source_target_pairs={{0,4},{4,8},{8,12},{12,0},{1,5},{5,9},{9,13},{13,1},{2,6},{6,10},{... | collective-permute-start | bytes 2088968 | tf_op jit(solution)/shard_map/ppermute | solution.py:370
  166.4 22.2 %collective-permute-start.26 = (bf16[640,1280]{1,0:T(8,128)(2,1)S(1)}, bf16[640,1280]{1,0:T(8,128)(2,1)S(1)}, u32[]{:S(2)}, u32[]{:S(2)}) collective-permute-start(bf16[640,1280]{1,0:T(8,128)(2,1)S(1)} %shard_map.59.refs_0_), channel_id=1, source_target_pairs={{0,1},{1,0},{2,3},{3,2},{4,5},{5,4},{6,7},{7,6},{8,9},{9,8},{10,11... | collective-permute-start | bytes 4915208 | tf_op jit(solution)/shard_map/ppermute | solution.py:348
  186.7 5.9 %collective-permute-start.27 = (bf16[640,1280]{1,0:T(8,128)(2,1)S(1)}, bf16[640,1280]{1,0:T(8,128)(2,1)S(1)}, u32[]{:S(2)}, u32[]{:S(2)}) collective-permute-start(bf16[640,1280]{1,0:T(8,128)(2,1)S(1)} %shard_map.63.refs_0_), channel_id=1, source_target_pairs={{0,1},{1,0},{2,3},{3,2},{4,5},{5,4},{6,7},{7,6},{8,9},{9,8},{10,11... | collective-permute-start | bytes 4915208 | tf_op jit(solution)/shard_map/ppermute | solution.py:348
  (8 other events, 42.2 us)

commit v3 on v2

--- a/solution.py
+++ b/solution.py
@@ -21,12 +21,13 @@
 VMEM = pl.BlockSpec(memory_space=pltpu.VMEM)
 SMEM = pl.BlockSpec(memory_space=pltpu.SMEM)
 POWER = 15.0
-PARTS = (1, 4)
+PARTS = (1, 2)
 SCHEDULE = (
-    ("A", 0), ("T", 0), ("K0", 6), ("M", 150), ("P0", 0), ("K1", 0),
-    ("P1", 0), ("B", 0), ("F0", 0), ("S", 30), ("L", 0), ("F1", 0),
-    ("X0", 0), ("Y1", 0), ("Z1", 0),
+    ("A", 0), ("T", 0), ("K0", 6), ("M", 150), ("P0", 0), ("B", 0),
+    ("K1", 0), ("P1", 0), ("F0", 0), ("S", 30), ("X0", 0), ("L", 0),
+    ("F1", 0), ("Y1", 0), ("Z1", 0),
 )
+HALVES = (1, 1)
 TAIL = 16
 STEP = 32
 
@@ -54,10 +55,18 @@
     for src in srcs:
 
         def top_of(i, m, src=src):
-            v = jnp.abs(src[pl.ds(pl.multiple_of(i * STEP, STEP), STEP), :])
-            return jnp.maximum(m, jnp.max(v.reshape(STEP // 8, 8, c), axis=0))
+            return top_with(m, src[pl.ds(pl.multiple_of(i * STEP, STEP), STEP), :])
 
         m = lax.fori_loop(0, src.shape[0] // STEP, top_of, m)
+    encode_with(m, srcs, dst)
+
+
+def top_with(m, v):
+    return jnp.maximum(m, jnp.max(jnp.abs(v).reshape(STEP // 8, 8, v.shape[1]), axis=0))
+
+
+def encode_with(m, srcs, dst):
+    c = dst.shape[1]
     e = jnp.ceil(jnp.log2(jnp.clip(jnp.max(m, keepdims=True), 2.0**-118, 2.0**120)))
     scale = jnp.exp2(8.0 - e)
     first = 0
@@ -94,7 +103,7 @@
 
 
 def turn_kernel(at, *refs):
-    pieces, (out, bufs, sems) = refs[:5], refs[5:]
+    pieces, (out, bufs, sems) = refs[:-3], refs[-3:]
     rows = pieces[0].shape[0]
     copies, first = [], 0
     for i, src in enumerate(pieces):
@@ -109,47 +118,58 @@
             out[f : f + 256, tokens] = bufs[d * rows : (d + 1) * rows, f : f + 256].T
 
 
-def weight_kernel(first, parts, at, inputs, *refs):
-    gives, keep = refs[10 : 10 + parts], refs[10 + parts]
-    weight_parts(first, at, inputs, refs[:10], gives, keep, *refs[11 + parts :])
-
-
-def weight_parts(first, at, inputs, pieces, gives, keep, held, grads, sems):
+def weight_kernel(first, parts, own, at, inputs, *refs):
+    n = 10 + parts + own
+    weight_parts(first, at, inputs, refs[:10], refs[10 : 10 + parts], refs[10 + parts : n], *refs[n:])
+
+
+def weight_parts(first, at, inputs, pieces, gives, keeps, grads, sems):
     x, y, core = at[0], at[1], at[2]
     rows, width = pieces[0].shape[0], grads.shape[1]
-    half = keep.shape[0]
-    copies = [pltpu.make_async_copy(inputs, held, sems.at[10])]
-    copies[0].start()
-    for i, src in enumerate(pieces):
-        d, lo = ((0, 0), (1, 0), (2, 0), (2, rows // 2), (3, 0))[i % 5]
-        r = 2 * lax.rem(x + d, 4) + lax.rem(y + i // 5, 2)
-        start = pl.multiple_of(r * rows + lo, rows // 2)
-        dst = grads.at[pl.ds(start, src.shape[0])]
-        copies.append(pltpu.make_async_copy(src.at[:, pl.ds(first, width)], dst, sems.at[i]))
-        copies[-1].start()
-    for copy in copies:
-        copy.wait()
-    def dot(which):
-        features = pl.ds(pl.multiple_of(which * half, half), half)
-        return jnp.dot(held[features, :], grads[...], preferred_element_type=F32)
-
-    value, n = dot(1 - core), gives[0].shape[0]
-    for i, give in enumerate(gives):
-        give[...] = value[i * n : (i + 1) * n]
-    keep[...] = dot(core)
+    half = inputs.shape[0] // 2
+    cut = width // 2 // 256 * 256
+    tiles = ((0, cut), (cut, width - cut))
+    copies = []
+    for t, (column, n) in enumerate(tiles):
+        for i, src in enumerate(pieces):
+            d, lo = ((0, 0), (1, 0), (2, 0), (2, rows // 2), (3, 0))[i % 5]
+            r = 2 * lax.rem(x + d, 4) + lax.rem(y + i // 5, 2)
+            start = pl.multiple_of(r * rows + lo, rows // 2)
+            dst = grads.at[pl.ds(start, src.shape[0]), pl.ds(column, n)]
+            copy = pltpu.make_async_copy(src.at[:, pl.ds(first + column, n)], dst, sems.at[10 * t + i])
+            copy.start()
+            copies.append(copy)
+    wanted = [1 - core] * (len(gives) > 0) + [core] * len(keeps)
+    for t, (column, n) in enumerate(tiles):
+        for copy in copies[10 * t : 10 * t + 10]:
+            copy.wait()
+        columns = pl.ds(column, n)
+        for i, which in enumerate(wanted):
+            features = pl.ds(pl.multiple_of(which * half, half), half)
+            value = jnp.dot(inputs[features, :], grads[:, columns], preferred_element_type=F32)
+            if i == 0 and gives:
+                m = gives[0].shape[0]
+                for k, give in enumerate(gives):
+                    give[:, columns] = value[k * m : (k + 1) * m]
+            else:
+                keeps[0][:, columns] = value
 
 
 def pair_kernel(at, keep, *refs):
     gots, (msg, total) = refs[:-2], refs[-2:]
     n = gots[0].shape[0]
+    m = jnp.zeros((8, total.shape[1]), F32)
     for k, got in enumerate(gots):
 
-        def add(i, k=k, got=got):
+        def add(i, m, k=k, got=got):
+            i = pl.multiple_of(i * STEP, STEP)
             rows = pl.ds(k * n + i, STEP)
-            total[rows, :] = keep[rows, :] + got[pl.ds(i, STEP), :]
-
-        looped(n, add)
-    encode([total], msg)
+            value = keep[rows, :] + got[pl.ds(i, STEP), :]
+            total[rows, :] = value
+            return top_with(m, value)
+
+        m = lax.fori_loop(0, n // STEP, add, m)
+    encode_with(m, [total], msg)
 
 
 def decode_kernel(msg, out):
@@ -161,26 +181,25 @@
     looped(out.shape[0], one)
 
 
-def final_kernel(at, mine, got, *outs):
+def final_kernel(first, at, mine, got, out):
     s = scale_of(got)
-    n = outs[0].shape[0]
-    for k, out in enumerate(outs):
-
-        def add(i, k=k, out=out):
-            rows = pl.ds(k * n + i, STEP)
-            out[pl.ds(i, STEP), :] = (mine[rows, :] + decode(got[rows, :], s)).astype(BF16)
-
-        looped(n, add)
+
+    def add(i):
+        rows = pl.ds(first + i, STEP)
+        out[pl.ds(i, STEP), :] = (mine[rows, :] + decode(got[rows, :], s)).astype(BF16)
+
+    looped(out.shape[0], add)
 
 
 def place_kernel(spots, at, *refs):
     out, sems = refs[-2:]
+    half = out.shape[0] // 2
     copies = []
-    for src, (first, other) in zip(refs, spots):
-        half, width = src.shape
+    for src, (column, row, other) in zip(refs, spots):
+        n, width = src.shape
         which = 1 - at[2] if other else at[2]
-        rows = pl.ds(pl.multiple_of(which * half, half), half)
-        copies.append(pltpu.make_async_copy(src, out.at[rows, pl.ds(first, width)], sems.at[len(copies)]))
+        rows = pl.ds(pl.multiple_of(which * half + row, n), n)
+        copies.append(pltpu.make_async_copy(src, out.at[rows, pl.ds(column, width)], sems.at[len(copies)]))
         copies[-1].start()
     for copy in copies:
         copy.wait()
@@ -276,7 +295,7 @@
     far_lo = lax.ppermute(a_up[:h], "row", X_DOWN)
     far_hi = lax.ppermute(a_dn[h:], "row", X_UP)
     b_dn = lax.ppermute(after(b, far_hi), "row", X_UP)
-    b_up = lax.ppermute(after(b, far_lo), "row", X_DOWN)
+    b_up = lax.ppermute(b, "row", X_DOWN)
     i_far_lo = lax.ppermute(i_up[:rows], "col", Z_DOWN)
     i_far_hi = lax.ppermute(i_dn[rows:], "col", Z_UP)
     b_far_lo = lax.ppermute(far_lo, "row", Y_SWAP)
@@ -311,21 +330,21 @@
         )
         return terms, lax.ppermute(up, "col", Z_UP), lax.ppermute(dn, "col", Z_DOWN)
 
-    def weight_of(j, us=0):
+    def weight_of(j, us=0, parts=None, own=1):
         first, width = spans[j]
-        parts = PARTS[j]
-        *gives, keep = ordered(
-            functools.partial(weight_kernel, first, parts),
-            [shape(half // parts, width)] * parts + [shape(half, width)],
-            [pltpu.VMEM((features, tokens), BF16), pltpu.VMEM((tokens, width), BF16), dmas(11)],
-            [ANY] * 11,
+        parts = PARTS[j] if parts is None else parts
+        got = ordered(
+            functools.partial(weight_kernel, first, parts, own),
+            [shape(half // max(parts, 1), width)] * parts + [shape(half, width)] * own,
+            [pltpu.VMEM((tokens, width), BF16), dmas(20)],
+            [VMEM] + [ANY] * 10,
             env["T"],
             *side_a,
             *side_b,
             us=us,
             mib=20,
         )
-        return [keep] + [lax.ppermute(give, "dp", CORE_SWAP) for give in gives]
+        return list(got[parts:]) + [lax.ppermute(give, "dp", CORE_SWAP) for give in got[:parts]]
 
     def pair_of(j, us=0):
         width = spans[j][1]
@@ -344,15 +363,18 @@
         width = spans[j][1]
         sent, got = env["P%d" % j]
         (mine,) = call(decode_kernel, [shape(half, width)], (), [VMEM])(sent)
-        (own,) = ordered(final_kernel, [shape(half, width, dtype=BF16)], (), [VMEM] * 2, mine, got, us=us)
-        return own, lax.ppermute(own, "dp", CORE_SWAP)
+        own, n = [], half // HALVES[j]
+        for first in range(0, half, n):
+            kernel = functools.partial(final_kernel, first)
+            own += ordered(kernel, [shape(n, width, dtype=BF16)], (), [VMEM] * 2, mine, got, us=us)
+        return own, [lax.ppermute(v, "dp", CORE_SWAP) for v in own]
 
     def turn(us=0):
         (turned,) = ordered(
             turn_kernel,
             [shape(features, tokens, dtype=BF16)],
-            [pltpu.VMEM((tokens, features), BF16), dmas(5)],
-            [ANY] * 5,
+            [pltpu.VMEM((tokens, features), BF16), dmas(len(input_pieces))],
+            [ANY] * len(input_pieces),
             *input_pieces,
             us=us,
         )
@@ -376,14 +398,19 @@
 
     def place(chunks, sides, us=0):
         old = [env["X"]] if "X" in env else []
-        spots = [(j, i) for j in chunks for i in sides]
-        n = len(spots)
+        spots, srcs = [], []
+        for j in chunks:
+            for i in sides:
+                for k, src in enumerate(env["F%d" % j][i]):
+                    spots.append((spans[j][0], k * src.shape[0], i))
+                    srcs.append(src)
+        n = len(srcs)
         (out,) = ordered(
-            functools.partial(place_kernel, [(spans[j][0], i) for j, i in spots]),
+            functools.partial(place_kernel, spots),
             [shape(features, outs, dtype=BF16)],
             [dmas(n)],
             [ANY] * (n + len(old)),
-            *[env["F%d" % j][i] for j, i in spots],
+            *srcs,
             *old,
             out_specs=[ANY],
             aliases={n + 1: 0} if old else None,
@@ -404,6 +431,10 @@
             env["X"] = place([int(c) for c in name[1:]], {"X": (0, 1), "Y": (0,), "Z": (1,)}[name[0]], us)
         elif name[0] == "G":
             gate(int(name[1]), us)
+        elif name[0] == "H":
+            env[name] = weight_of(int(name[1]), us, own=0)
+        elif name[0] == "K" and "H" + name[1] in env:
+            env[name] = weight_of(int(name[1]), us, parts=0) + env["H" + name[1]]
         elif name[0] in "KPF":
             env[name] = {"K": weight_of, "P": pair_of, "F": final_of}[name[0]](int(name[1]), us)
         else:

time: 195 us -> 187 us (0.959)
  waiting for transfers between devices: 71.9 us -> 64 us
    ppermute x2, waiting for transfers between devices: 2.84 us -> 14.1 us  [pair_of(): return (msg, lax.ppermute(msg, 'dp', FAR_SWAP))]
    ppermute x1, waiting for transfers between devices: 10.4 us -> 0.44 us  [second_of(): lax.ppermute(dn, 'col', Z_DOWN)]
    ppermute x2, waiting for transfers between devices: 9.08 us -> 0.01 us  [terms_of(): lax.ppermute(dn, 'col', Z_DOWN)]
    ppermute x1, waiting for transfers between devices: 1.57 us -> 10.5 us  [second_of(): lax.ppermute(up, 'col', Z_UP)]
    ppermute x8 -> x6, starting transfers between devices: 12.6 us -> 8.36 us  [the longest x3 4.58 us: weight_of(): lax.ppermute(give, 'dp', CORE_SWAP)]
    ppermute x1, waiting for transfers between devices: 10 us -> 7.36 us  [local(): far_hi = lax.ppermute(a_dn[h:], 'row', X_UP)]
    ppermute x2, starting transfers between devices: 0.38 us -> 2.99 us  [terms_of(): lax.ppermute(dn, 'col', Z_DOWN)]
    ppermute x8 -> x6, waiting for transfers between devices: 8.81 us -> 6.45 us  [the longest x3 5.04 us: weight_of(): lax.ppermute(give, 'dp', CORE_SWAP)]
  transfers between devices with their start and end apart: 28 -> 26, of which waited for: 15 -> 10; matrix products, arithmetic and copies ran while one was open for 1% -> 1% of each run, Pallas kernels for 36% -> 35%
where the time goes in v3:
time: 187 us
  Pallas kernels  73.9 us (40%)
  waiting for transfers between devices  64 us (34%)
  starting transfers between devices  39.9 us (21%)
  local copies, waits for them, and re-layouts  8.21 us (4%)
    pallas_call x15, Pallas kernels, ordered(): call(kernel, outs, scratch, [SMEM] + specs, **kw)  70.7 us
    ppermute x1, waiting for transfers between devices, local(): a_dn = lax.ppermute(a, 'row', X_UP)  23 us
    ppermute x2, waiting for transfers between devices, pair_of(): return (msg, lax.ppermute(msg, 'dp', FAR_SWAP))  14.1 us
    ppermute x1, waiting for transfers between devices, second_of(): lax.ppermute(up, 'col', Z_UP)  10.5 us
    ppermute x1, waiting for transfers between devices, local(): far_hi = lax.ppermute(a_dn[h:], 'row', X_UP)  7.36 us
    unnamed x30, local copies, waits for them, and re-layouts  7.17 us
    ppermute x3, waiting for transfers between devices, weight_of(): lax.ppermute(give, 'dp', CORE_SWAP)  5.04 us
    ppermute x3, starting transfers between devices, weight_of(): lax.ppermute(give, 'dp', CORE_SWAP)  4.58 us
  transfers between devices with their start and end apart: 26, of which 10 were waited for; matrix products, arithmetic and copies ran while one was open for 1% of the time, Pallas kernels for 35%

profile of v3, /device:TPU:1, one launch (start us, length us, event | category | flops | bytes accessed | tf_op | source)
XLA Modules:
  0.0 187.1 jit_solution(18173922782102393811)
XLA Ops:
  0.6 2.1 %collective-permute-start.2 = (bf16[256,2560]{1,0:T(8,128)(2,1)}, bf16[256,2560]{1,0:T(8,128)(2,1)S(1)}, u32[]{:S(2)}, u32[]{:S(2)}) collective-permute-start(bf16[256,2560]{1,0:T(8,128)(2,1)} %bitcast.9), channel_id=1, source_target_pairs={{0,32},{16,48},{32,64},{48,80},{64,96},{80,112},{96,0},{112,16},{1... | collective-permute-start | bytes 3932168 | tf_op jit(solution)/shard_map/ppermute | solution.py:290
  4.1 3.9 %collective-permute-start.4 = (bf16[512,1280]{1,0:T(8,128)(2,1)}, bf16[512,1280]{1,0:T(8,128)(2,1)S(1)}, u32[]{:S(2)}, u32[]{:S(2)}) collective-permute-start(bf16[512,1280]{1,0:T(8,128)(2,1)} %bitcast.15), channel_id=1, source_target_pairs={{0,12},{4,0},{8,4},{12,8},{1,13},{5,1},{9,5},{13,9},{2,14},{6,2},{... | collective-permute-start | bytes 3932168 | tf_op jit(solution)/shard_map/ppermute | solution.py:294
  9.3 23.0 %collective-permute-done.2.refs_4_ = bf16[256,2560]{1,0:T(8,128)(2,1)S(1)} collective-permute-done((bf16[256,2560]{1,0:T(8,128)(2,1)}, bf16[256,2560]{1,0:T(8,128)(2,1)S(1)}, u32[]{:S(2)}, u32[]{:S(2)}) %collective-permute-start.2) | collective-permute-done | bytes 1310752 | tf_op jit(solution)/shard_map/ppermute | solution.py:290
  32.9 2.3 %collective-permute-start.1 = (bf16[128,2560]{1,0:T(8,128)(2,1)S(1)}, bf16[128,2560]{1,0:T(8,128)(2,1)}, u32[]{:S(2)}, u32[]{:S(2)}) collective-permute-start(bf16[128,2560]{1,0:T(8,128)(2,1)S(1)} %slice.16), channel_id=1, source_target_pairs={{0,96},{16,112},{32,0},{48,16},{64,32},{80,48},{96,64},{112,80},{1... | collective-permute-start | bytes 1966088 | tf_op jit(solution)/shard_map/ppermute | solution.py:295
  36.3 4.1 %collective-permute-start.5 = (bf16[256,1280]{1,0:T(8,128)(2,1)S(1)}, bf16[256,1280]{1,0:T(8,128)(2,1)S(1)}, u32[]{:S(2)}, u32[]{:S(2)}) collective-permute-start(bf16[256,1280]{1,0:T(8,128)(2,1)S(1)} %slice.18), channel_id=1, source_target_pairs={{0,12},{4,0},{8,4},{12,8},{1,13},{5,1},{9,5},{13,9},{2,14},{6,2},{... | collective-permute-start | bytes 1966088 | tf_op jit(solution)/shard_map/ppermute | solution.py:299
  40.8 7.4 %collective-permute-done.3.refs_3_ = bf16[128,2560]{1,0:T(8,128)(2,1)S(1)} collective-permute-done((bf16[128,2560]{1,0:T(8,128)(2,1)S(1)}, bf16[128,2560]{1,0:T(8,128)(2,1)S(1)}, u32[]{:S(2)}, u32[]{:S(2)}) %collective-permute-start.3) | collective-permute-done | bytes 655392 | tf_op jit(solution)/shard_map/ppermute | solution.py:296
  50.1 2.1 %collective-permute-start.7 = (bf16[256,1280]{1,0:T(8,128)(2,1)}, bf16[256,1280]{1,0:T(8,128)(2,1)}, u32[]{:S(2)}, u32[]{:S(2)}) collective-permute-start(bf16[256,1280]{1,0:T(8,128)(2,1)} %slice.19), channel_id=1, source_target_pairs={{0,4},{4,8},{8,12},{12,0},{1,5},{5,9},{9,13},{13,1},{2,6},{6,10},{... | collective-permute-start | bytes 1966088 | tf_op jit(solution)/shard_map/ppermute | solution.py:300
  54.6 2.9 %copy-done = bf16[1280,2560]{1,0:T(8,128)(2,1)S(1)} copy-done((bf16[1280,2560]{1,0:T(8,128)(2,1)S(1)}, bf16[1280,2560]{1,0:T(8,128)(2,1)}, u32[]{:S(2)}) %copy-start) | copy-done | bytes 6553624
  58.8 11.6 %shard_map.50 = (bf16[272,1280]{1,0:T(8,128)(2,1)S(1)}, bf16[272,1280]{1,0:T(8,128)(2,1)S(1)}, f32[4,256,1280]{2,1,0:T(8,128)S(1)}) custom-call(s32[4]{0:T(128)S(1)} %pad_add_fusion.at, bf16[1280,2560]{1,0:T(8,128)(2,1)S(1)} %copy-done, bf16[256,2560]{1,0:T(8,128)(2,1)S(1)} %bitcast.12, bf16[256,2560]{1,0:T(8,128)(2,1)S(1)} %collective-permute-done.refs_1_, ...), custom_call_target="tpu_custom_call" | custom-call | flops 1 | bytes 1 | tf_op jit(solution)/shard_map/pallas_call | solution.py:315
  72.1 2.0 %collective-permute-start.14 = (bf16[272,1280]{1,0:T(8,128)(2,1)S(1)}, bf16[272,1280]{1,0:T(8,128)(2,1)S(1)}, u32[]{:S(2)}, u32[]{:S(2)}) collective-permute-start(bf16[272,1280]{1,0:T(8,128)(2,1)S(1)} %get-tuple-element.38), channel_id=1, source_target_pairs={{0,12},{4,0},{8,4},{12,8},{1,13},{5,1},{9,5},{13,9},{2,14},{6,2},{... | collective-permute-start | bytes 2088968 | tf_op jit(solution)/shard_map/ppermute | solution.py:331
  74.1 3.6 %shard_map.51.inputs = bf16[1280,2048]{1,0:T(8,128)(2,1)S(1)} custom-call(s32[4]{0:T(128)S(1)} %pad_add_fusion.at, bf16[512,1280]{1,0:T(8,128)(2,1)S(1)} %bitcast.17, bf16[512,1280]{1,0:T(8,128)(2,1)S(1)} %copy-done.7, bf16[256,1280]{1,0:T(8,128)(2,1)S(1)} %copy-done.12, bf16[256,1280]{1,0:T(8,128)(2,1)} %collective-permute-done.7.refs_3_, ...), custom_call_target="tpu_custom_call" | custom-call | flops 1 | bytes 1 | tf_op jit(solution)/shard_map/pallas_call | solution.py:315
  77.7 2.1 %collective-permute-done.10.refs_7_.refs_2_ = bf16[128,2560]{1,0:T(8,128)(2,1)} collective-permute-done((bf16[128,2560]{1,0:T(8,128)(2,1)}, bf16[128,2560]{1,0:T(8,128)(2,1)}, u32[]{:S(2)}, u32[]{:S(2)}) %collective-permute-start.10) | collective-permute-done | bytes 655392 | tf_op jit(solution)/shard_map/ppermute | solution.py:301
  79.9 9.5 %shard_map.52 = (f32[640,1280]{1,0:T(8,128)}, f32[640,1280]{1,0:T(8,128)S(1)}) custom-call(s32[4]{0:T(128)S(1)} %pad_add_fusion.at, bf16[1280,2048]{1,0:T(8,128)(2,1)S(1)} %shard_map.51.inputs, bf16[256,2560]{1,0:T(8,128)(2,1)S(1)} %bitcast.13, bf16[256,2560]{1,0:T(8,128)(2,1)S(1)} %collective-permute-done.refs_1_, ...), custom_call_target="tpu_custom_call" | custom-call | flops 6000000000 | bytes 1 | tf_op jit(solution)/shard_map/pallas_call | solution.py:315
  89.4 3.8 %collective-permute-start.15 = (f32[640,1280]{1,0:T(8,128)}, f32[640,1280]{1,0:T(8,128)}, u32[]{:S(2)}, u32[]{:S(2)}) collective-permute-start(f32[640,1280]{1,0:T(8,128)} %get-tuple-element.35), channel_id=1, source_target_pairs={{0,1},{1,0},{2,3},{3,2},{4,5},{5,4},{6,7},{7,6},{8,9},{9,8},{10,11... | collective-permute-start | bytes 9830408 | tf_op jit(solution)/shard_map/ppermute | solution.py:347
  93.2 1.9 shard_map.53.sums_a
  95.0 3.9 %collective-permute-done.15.refs_0_ = f32[640,1280]{1,0:T(8,128)} collective-permute-done((f32[640,1280]{1,0:T(8,128)}, f32[640,1280]{1,0:T(8,128)}, u32[]{:S(2)}, u32[]{:S(2)}) %collective-permute-start.15) | collective-permute-done | bytes 3276832 | tf_op jit(solution)/shard_map/ppermute | solution.py:347
  99.0 3.7 %shard_map.54.msg = bf16[656,1280]{1,0:T(8,128)(2,1)S(1)} custom-call(s32[4]{0:T(128)S(1)} %pad_add_fusion.at, f32[640,1280]{1,0:T(8,128)S(1)} %get-tuple-element.40.keep, f32[640,1280]{1,0:T(8,128)} %collective-permute-done.15.refs_0_), custom_call_target="tpu_custom_call" | custom-call | flops 1 | bytes 1 | tf_op jit(solution)/shard_map/pallas_call | solution.py:315
  102.7 3.2 %collective-permute-start.18 = (bf16[656,1280]{1,0:T(8,128)(2,1)S(1)}, bf16[656,1280]{1,0:T(8,128)(2,1)S(1)}, u32[]{:S(2)}, u32[]{:S(2)}) collective-permute-start(bf16[656,1280]{1,0:T(8,128)(2,1)S(1)} %shard_map.54.msg), channel_id=1, source_target_pairs={{0,2},{1,3},{2,0},{3,1},{4,6},{5,7},{6,4},{7,5},{8,10},{9,11},{10,... | collective-permute-start | bytes 5038088 | tf_op jit(solution)/shard_map/ppermute | solution.py:360
  105.9 12.5 %shard_map.55 = (bf16[272,1280]{1,0:T(8,128)(2,1)S(1)}, bf16[272,1280]{1,0:T(8,128)(2,1)S(1)}, f32[4,256,1280]{2,1,0:T(8,128)S(1)}) custom-call(s32[4]{0:T(128)S(1)} %pad_add_fusion.at, bf16[1280,2560]{1,0:T(8,128)(2,1)S(1)} %copy-done.1, bf16[256,2560]{1,0:T(8,128)(2,1)} %collective-permute-done.8.refs_5_.refs_0_, ...), custom_call_target="tpu_custom_call" | custom-call | flops 1 | bytes 1 | tf_op jit(solution)/shard_map/pallas_call | solution.py:315
  118.4 9.2 %shard_map.56 = (f32[320,1280]{1,0:T(8,128)S(1)}, f32[320,1280]{1,0:T(8,128)S(1)}, f32[640,1280]{1,0:T(8,128)S(1)}) custom-call(s32[4]{0:T(128)S(1)} %pad_add_fusion.at, bf16[1280,2048]{1,0:T(8,128)(2,1)S(1)} %bitcast.8, bf16[256,2560]{1,0:T(8,128)(2,1)S(1)} %bitcast.14, bf16[256,2560]{1,0:T(8,128)(2,1)S(1)} %collective-permute-done.refs_1_, ...), custom_call_target="tpu_custom_call" | custom-call | flops 1 | bytes 1 | tf_op jit(solution)/shard_map/pallas_call | solution.py:315
  133.8 2.1 %shard_map.57.msg = bf16[656,1280]{1,0:T(8,128)(2,1)S(1)} custom-call(s32[4]{0:T(128)S(1)} %pad_add_fusion.at, f32[640,1280]{1,0:T(8,128)S(1)} %get-tuple-element.46.keep, f32[320,1280]{1,0:T(8,128)S(1)} %collective-permute-done.16.refs_0_, f32[320,1280]{1,0:T(8,128)S(1)} %collective-permute-done.17.refs_1_), custom_call_target="tpu_custom_call" | custom-call | flops 1 | bytes 1 | tf_op jit(solution)/shard_map/pallas_call | solution.py:315
  136.0 6.3 %collective-permute-done.18.got = bf16[656,1280]{1,0:T(8,128)(2,1)S(1)} collective-permute-done((bf16[656,1280]{1,0:T(8,128)(2,1)S(1)}, bf16[656,1280]{1,0:T(8,128)(2,1)S(1)}, u32[]{:S(2)}, u32[]{:S(2)}) %collective-permute-start.18) | collective-permute-done | bytes 1679392 | tf_op jit(solution)/shard_map/ppermute | solution.py:360
  142.4 2.4 %shard_map.59.refs_0_ = bf16[640,1280]{1,0:T(8,128)(2,1)S(1)} custom-call(s32[4]{0:T(128)S(1)} %pad_add_fusion.at, f32[640,1280]{1,0:T(8,128)S(1)} %shard_map.58.mine, bf16[656,1280]{1,0:T(8,128)(2,1)S(1)} %collective-permute-done.18.got), custom_call_target="tpu_custom_call" | custom-call | flops 1 | bytes 1 | tf_op jit(solution)/shard_map/pallas_call | solution.py:315
  144.8 2.1 %collective-permute-start.21 = (bf16[640,1280]{1,0:T(8,128)(2,1)S(1)}, bf16[640,1280]{1,0:T(8,128)(2,1)S(1)}, u32[]{:S(2)}, u32[]{:S(2)}) collective-permute-start(bf16[640,1280]{1,0:T(8,128)(2,1)S(1)} %shard_map.59.refs_0_), channel_id=1, source_target_pairs={{0,1},{1,0},{2,3},{3,2},{4,5},{5,4},{6,7},{7,6},{8,9},{9,8},{10,11... | collective-permute-start | bytes 4915208 | tf_op jit(solution)/shard_map/ppermute | solution.py:370
  146.9 3.1 %shard_map.60 = (bf16[272,1280]{1,0:T(8,128)(2,1)S(1)}, bf16[272,1280]{1,0:T(8,128)(2,1)S(1)}, f32[512,1280]{1,0:T(8,128)S(1)}) custom-call(s32[4]{0:T(128)S(1)} %pad_add_fusion.at, f32[512,1280]{1,0:T(8,128)S(1)} %shard_map.53.sums_a, f32[4,256,1280]{2,1,0:T(8,128)S(1)} %get-tuple-element.50.terms, bf16[272,1280]{1,0:T(8,128)(2,1)S(1)} %collective-permute-done.19.from_dn, ...), custom_call_target="tpu_custom_call" | custom-call | flops 30000001024 | bytes 1 | tf_op jit(solution)/shard_map/pallas_call | solution.py:315
  154.3 2.3 %shard_map.61.refs_1_ = bf16[1280,2560]{1,0:T(8,128)(2,1)} custom-call(s32[4]{0:T(128)S(1)} %pad_add_fusion.at, bf16[640,1280]{1,0:T(8,128)(2,1)S(1)} %shard_map.59.refs_0_, bf16[640,1280]{1,0:T(8,128)(2,1)S(1)} %collective-permute-done.21.refs_1_), custom_call_target="tpu_custom_call" | custom-call | flops 1 | bytes 1 | tf_op jit(solution)/shard_map/pallas_call | solution.py:315
  156.6 10.5 %collective-permute-done.22.second_dn = bf16[272,1280]{1,0:T(8,128)(2,1)S(1)} collective-permute-done((bf16[272,1280]{1,0:T(8,128)(2,1)S(1)}, bf16[272,1280]{1,0:T(8,128)(2,1)S(1)}, u32[]{:S(2)}, u32[]{:S(2)}) %collective-permute-start.22) | collective-permute-done | bytes 696352 | tf_op jit(solution)/shard_map/ppermute | solution.py:392
  167.6 3.0 %shard_map.62 = bf16[512,1280]{1,0:T(8,128)(2,1)} custom-call(s32[4]{0:T(128)S(1)} %pad_add_fusion.at, f32[512,1280]{1,0:T(8,128)S(1)} %shard_map.53.sums_a, f32[512,1280]{1,0:T(8,128)S(1)} %get-tuple-element.55.sums_b, bf16[272,1280]{1,0:T(8,128)(2,1)S(1)} %collective-permute-done.22.second_dn, bf16[272,1280]{1,0:T(8,128)(2,1)S(1)} %collective-permute-done.23.second_up), custom_call_target="tpu_custom_call" | custom-call | flops 1 | bytes 1 | tf_op jit(solution)/shard_map/pallas_call | solution.py:315
  170.6 7.7 %collective-permute-done.24.got = bf16[656,1280]{1,0:T(8,128)(2,1)S(1)} collective-permute-done((bf16[656,1280]{1,0:T(8,128)(2,1)S(1)}, bf16[656,1280]{1,0:T(8,128)(2,1)S(1)}, u32[]{:S(2)}, u32[]{:S(2)}) %collective-permute-start.24) | collective-permute-done | bytes 1679392 | tf_op jit(solution)/shard_map/ppermute | solution.py:360
  178.4 2.4 %shard_map.64.refs_0_ = bf16[640,1280]{1,0:T(8,128)(2,1)S(1)} custom-call(s32[4]{0:T(128)S(1)} %pad_add_fusion.at, f32[640,1280]{1,0:T(8,128)S(1)} %shard_map.63.mine, bf16[656,1280]{1,0:T(8,128)(2,1)S(1)} %collective-permute-done.24.got), custom_call_target="tpu_custom_call" | custom-call | flops 1 | bytes 1 | tf_op jit(solution)/shard_map/pallas_call | solution.py:315
  182.1 1.7 shard_map.65.refs_1_
  185.2 1.7 shard_map.66
  (73 shorter events, 26.0 us)
Async XLA Ops:
  0.6 31.6 %collective-permute-start.2 = (bf16[256,2560]{1,0:T(8,128)(2,1)}, bf16[256,2560]{1,0:T(8,128)(2,1)S(1)}, u32[]{:S(2)}, u32[]{:S(2)}) collective-permute-start(bf16[256,2560]{1,0:T(8,128)(2,1)} %bitcast.9), channel_id=1, source_target_pairs={{0,32},{16,48},{32,64},{48,80},{64,96},{80,112},{96,0},{112,16},{1... | collective-permute-start | bytes 3932168 | tf_op jit(solution)/shard_map/ppermute | solution.py:290
  2.7 30.1 %collective-permute-start = (bf16[256,2560]{1,0:T(8,128)(2,1)}, bf16[256,2560]{1,0:T(8,128)(2,1)S(1)}, u32[]{:S(2)}, u32[]{:S(2)}) collective-permute-start(bf16[256,2560]{1,0:T(8,128)(2,1)} %bitcast.10), channel_id=1, source_target_pairs={{0,96},{16,112},{32,0},{48,16},{64,32},{80,48},{96,64},{112,80},{1... | collective-permute-start | bytes 3932168 | tf_op jit(solution)/shard_map/ppermute | solution.py:291
  4.1 31.1 %collective-permute-start.4 = (bf16[512,1280]{1,0:T(8,128)(2,1)}, bf16[512,1280]{1,0:T(8,128)(2,1)S(1)}, u32[]{:S(2)}, u32[]{:S(2)}) collective-permute-start(bf16[512,1280]{1,0:T(8,128)(2,1)} %bitcast.15), channel_id=1, source_target_pairs={{0,12},{4,0},{8,4},{12,8},{1,13},{5,1},{9,5},{13,9},{2,14},{6,2},{... | collective-permute-start | bytes 3932168 | tf_op jit(solution)/shard_map/ppermute | solution.py:294
  8.0 32.4 %collective-permute-start.8 = (bf16[256,2560]{1,0:T(8,128)(2,1)}, bf16[256,2560]{1,0:T(8,128)(2,1)}, u32[]{:S(2)}, u32[]{:S(2)}) collective-permute-start(bf16[256,2560]{1,0:T(8,128)(2,1)} %bitcast.11), channel_id=1, source_target_pairs={{0,16},{16,0},{32,48},{48,32},{64,80},{80,64},{96,112},{112,96},{1... | collective-permute-start | bytes 3932168 | tf_op jit(solution)/shard_map/ppermute | solution.py:292
  9.3 38.9 %collective-permute-start.6 = (bf16[512,1280]{1,0:T(8,128)(2,1)}, bf16[512,1280]{1,0:T(8,128)(2,1)S(1)}, u32[]{:S(2)}, u32[]{:S(2)}) collective-permute-start(bf16[512,1280]{1,0:T(8,128)(2,1)} %bitcast.16), channel_id=1, source_target_pairs={{0,4},{4,8},{8,12},{12,0},{1,5},{5,9},{9,13},{13,1},{2,6},{6,10},{... | collective-permute-start | bytes 3932168 | tf_op jit(solution)/shard_map/ppermute | solution.py:293
  32.3 15.8 %collective-permute-start.3 = (bf16[128,2560]{1,0:T(8,128)(2,1)S(1)}, bf16[128,2560]{1,0:T(8,128)(2,1)S(1)}, u32[]{:S(2)}, u32[]{:S(2)}) collective-permute-start(bf16[128,2560]{1,0:T(8,128)(2,1)S(1)} %slice.17), channel_id=1, source_target_pairs={{0,32},{16,48},{32,64},{48,80},{64,96},{80,112},{96,0},{112,16},{1... | collective-permute-start | bytes 1966088 | tf_op jit(solution)/shard_map/ppermute | solution.py:296
  32.9 19.4 %collective-permute-start.1 = (bf16[128,2560]{1,0:T(8,128)(2,1)S(1)}, bf16[128,2560]{1,0:T(8,128)(2,1)}, u32[]{:S(2)}, u32[]{:S(2)}) collective-permute-start(bf16[128,2560]{1,0:T(8,128)(2,1)S(1)} %slice.16), channel_id=1, source_target_pairs={{0,96},{16,112},{32,0},{48,16},{64,32},{80,48},{96,64},{112,80},{1... | collective-permute-start | bytes 1966088 | tf_op jit(solution)/shard_map/ppermute | solution.py:295
  36.3 17.2 %collective-permute-start.5 = (bf16[256,1280]{1,0:T(8,128)(2,1)S(1)}, bf16[256,1280]{1,0:T(8,128)(2,1)S(1)}, u32[]{:S(2)}, u32[]{:S(2)}) collective-permute-start(bf16[256,1280]{1,0:T(8,128)(2,1)S(1)} %slice.18), channel_id=1, source_target_pairs={{0,12},{4,0},{8,4},{12,8},{1,13},{5,1},{9,5},{13,9},{2,14},{6,2},{... | collective-permute-start | bytes 1966088 | tf_op jit(solution)/shard_map/ppermute | solution.py:299
  40.4 39.5 %collective-permute-start.9 = (bf16[256,2560]{1,0:T(8,128)(2,1)}, bf16[256,2560]{1,0:T(8,128)(2,1)}, u32[]{:S(2)}, u32[]{:S(2)}) collective-permute-start(bf16[256,2560]{1,0:T(8,128)(2,1)} %collective-permute-done.8.refs_5_.refs_0_), channel_id=1, source_target_pairs={{0,96},{16,112},{32,0},{48,16},{64,32},{80,48},{96,64},{112,80},{1... | collective-permute-start | bytes 3932168 | tf_op jit(solution)/shard_map/ppermute | solution.py:298
  48.2 31.7 %collective-permute-start.12 = (bf16[256,2560]{1,0:T(8,128)(2,1)}, bf16[256,2560]{1,0:T(8,128)(2,1)}, u32[]{:S(2)}, u32[]{:S(2)}) collective-permute-start(bf16[256,2560]{1,0:T(8,128)(2,1)} %collective-permute-done.8.refs_5_.refs_0_), channel_id=1, source_target_pairs={{0,32},{16,48},{32,64},{48,80},{64,96},{80,112},{96,0},{112,16},{1... | collective-permute-start | bytes 3932168 | tf_op jit(solution)/shard_map/ppermute | solution.py:297
  50.1 20.3 %collective-permute-start.7 = (bf16[256,1280]{1,0:T(8,128)(2,1)}, bf16[256,1280]{1,0:T(8,128)(2,1)}, u32[]{:S(2)}, u32[]{:S(2)}) collective-permute-start(bf16[256,1280]{1,0:T(8,128)(2,1)} %slice.19), channel_id=1, source_target_pairs={{0,4},{4,8},{8,12},{12,0},{1,5},{5,9},{9,13},{13,1},{2,6},{6,10},{... | collective-permute-start | bytes 1966088 | tf_op jit(solution)/shard_map/ppermute | solution.py:300
  52.2 19.9 %collective-permute-start.11 = (bf16[128,2560]{1,0:T(8,128)(2,1)S(1)}, bf16[128,2560]{1,0:T(8,128)(2,1)}, u32[]{:S(2)}, u32[]{:S(2)}) collective-permute-start(bf16[128,2560]{1,0:T(8,128)(2,1)S(1)} %collective-permute-done.3.refs_3_), channel_id=1, source_target_pairs={{0,16},{16,0},{32,48},{48,32},{64,80},{80,64},{96,112},{112,96},{1... | collective-permute-start | bytes 1966088 | tf_op jit(solution)/shard_map/ppermute | solution.py:302
  54.4 25.5 %collective-permute-start.10 = (bf16[128,2560]{1,0:T(8,128)(2,1)}, bf16[128,2560]{1,0:T(8,128)(2,1)}, u32[]{:S(2)}, u32[]{:S(2)}) collective-permute-start(bf16[128,2560]{1,0:T(8,128)(2,1)} %collective-permute-done.1.refs_2_), channel_id=1, source_target_pairs={{0,16},{16,0},{32,48},{48,32},{64,80},{80,64},{96,112},{112,96},{1... | collective-permute-start | bytes 1966088 | tf_op jit(solution)/shard_map/ppermute | solution.py:301
  58.8 15.3 %copy-start.9 = (bf16[512,1280]{1,0:T(8,128)(2,1)S(1)}, bf16[512,1280]{1,0:T(8,128)(2,1)}, u32[]{:S(2)}) copy-start(bf16[512,1280]{1,0:T(8,128)(2,1)} %copy-done.8) | copy-start | bytes 3932164
  58.8 15.3 %copy-start.10 = (bf16[1,512,1280]{2,1,0:T(8,128)(2,1)S(1)}, bf16[1,512,1280]{2,1,0:T(8,128)(2,1)}, u32[]{:S(2)}) copy-start(bf16[1,512,1280]{2,1,0:T(8,128)(2,1)} %param.3) | copy-start | bytes 3932164
  58.8 15.3 %copy-start.12 = (bf16[256,1280]{1,0:T(8,128)(2,1)S(1)}, bf16[256,1280]{1,0:T(8,128)(2,1)}, u32[]{:S(2)}) copy-start(bf16[256,1280]{1,0:T(8,128)(2,1)} %copy-done.11) | copy-start | bytes 1966084
  70.4 22.7 %collective-permute-start.13 = (bf16[272,1280]{1,0:T(8,128)(2,1)S(1)}, bf16[272,1280]{1,0:T(8,128)(2,1)S(1)}, u32[]{:S(2)}, u32[]{:S(2)}) collective-permute-start(bf16[272,1280]{1,0:T(8,128)(2,1)S(1)} %get-tuple-element.31), channel_id=1, source_target_pairs={{0,4},{4,8},{8,12},{12,0},{1,5},{5,9},{9,13},{13,1},{2,6},{6,10},{... | collective-permute-start | bytes 2088968 | tf_op jit(solution)/shard_map/ppermute | solution.py:331
  72.1 21.0 %collective-permute-start.14 = (bf16[272,1280]{1,0:T(8,128)(2,1)S(1)}, bf16[272,1280]{1,0:T(8,128)(2,1)S(1)}, u32[]{:S(2)}, u32[]{:S(2)}) collective-permute-start(bf16[272,1280]{1,0:T(8,128)(2,1)S(1)} %get-tuple-element.38), channel_id=1, source_target_pairs={{0,12},{4,0},{8,4},{12,8},{1,13},{5,1},{9,5},{13,9},{2,14},{6,2},{... | collective-permute-start | bytes 2088968 | tf_op jit(solution)/shard_map/ppermute | solution.py:331
  89.4 9.6 %collective-permute-start.15 = (f32[640,1280]{1,0:T(8,128)}, f32[640,1280]{1,0:T(8,128)}, u32[]{:S(2)}, u32[]{:S(2)}) collective-permute-start(f32[640,1280]{1,0:T(8,128)} %get-tuple-element.35), channel_id=1, source_target_pairs={{0,1},{1,0},{2,3},{3,2},{4,5},{5,4},{6,7},{7,6},{8,9},{9,8},{10,11... | collective-permute-start | bytes 9830408 | tf_op jit(solution)/shard_map/ppermute | solution.py:347
  99.0 19.4 %slice-start = ((s8[5242880]{0:T(1024)(128)(4,1)}), s8[4194304]{0:T(1024)(128)(4,1)S(1)}, s32[]{:S(2)}) async-start(s8[5242880]{0:T(1024)(128)(4,1)} %bitcast.7), calls=%async_computation | async-start | bytes 8388608
  102.6 15.7 %slice-start.1 = ((s8[5242880]{0:T(1024)(128)(4,1)}), s8[1048576]{0:T(1024)(128)(4,1)S(1)}, s32[]{:S(2)}) async-start(s8[5242880]{0:T(1024)(128)(4,1)} %bitcast.7), calls=%async_computation.1 | async-start | bytes 2097152
  102.7 15.7 %copy-start.5 = (bf16[1,256,2560]{2,1,0:T(8,128)(2,1)S(1)}, bf16[1,256,2560]{2,1,0:T(8,128)(2,1)}, u32[]{:S(2)}) copy-start(bf16[1,256,2560]{2,1,0:T(8,128)(2,1)} %param.4) | copy-start | bytes 3932164
  102.7 39.7 %collective-permute-start.18 = (bf16[656,1280]{1,0:T(8,128)(2,1)S(1)}, bf16[656,1280]{1,0:T(8,128)(2,1)S(1)}, u32[]{:S(2)}, u32[]{:S(2)}) collective-permute-start(bf16[656,1280]{1,0:T(8,128)(2,1)S(1)} %shard_map.54.msg), channel_id=1, source_target_pairs={{0,2},{1,3},{2,0},{3,1},{4,6},{5,7},{6,4},{7,5},{8,10},{9,11},{10,... | collective-permute-start | bytes 5038088 | tf_op jit(solution)/shard_map/ppermute | solution.py:360
  127.6 5.1 %collective-permute-start.16 = (f32[320,1280]{1,0:T(8,128)S(1)}, f32[320,1280]{1,0:T(8,128)S(1)}, u32[]{:S(2)}, u32[]{:S(2)}) collective-permute-start(f32[320,1280]{1,0:T(8,128)S(1)} %get-tuple-element.44), channel_id=1, source_target_pairs={{0,1},{1,0},{2,3},{3,2},{4,5},{5,4},{6,7},{7,6},{8,9},{9,8},{10,11... | collective-permute-start | bytes 4915208 | tf_op jit(solution)/shard_map/ppermute | solution.py:347
  128.3 5.5 %collective-permute-start.17 = (f32[320,1280]{1,0:T(8,128)S(1)}, f32[320,1280]{1,0:T(8,128)S(1)}, u32[]{:S(2)}, u32[]{:S(2)}) collective-permute-start(f32[320,1280]{1,0:T(8,128)S(1)} %get-tuple-element.47), channel_id=1, source_target_pairs={{0,1},{1,0},{2,3},{3,2},{4,5},{5,4},{6,7},{7,6},{8,9},{9,8},{10,11... | collective-permute-start | bytes 4915208 | tf_op jit(solution)/shard_map/ppermute | solution.py:347
  128.4 18.4 %collective-permute-start.19 = (bf16[272,1280]{1,0:T(8,128)(2,1)S(1)}, bf16[272,1280]{1,0:T(8,128)(2,1)S(1)}, u32[]{:S(2)}, u32[]{:S(2)}) collective-permute-start(bf16[272,1280]{1,0:T(8,128)(2,1)S(1)} %get-tuple-element.42), channel_id=1, source_target_pairs={{0,4},{4,8},{8,12},{12,0},{1,5},{5,9},{9,13},{13,1},{2,6},{6,10},{... | collective-permute-start | bytes 2088968 | tf_op jit(solution)/shard_map/ppermute | solution.py:331
  130.1 16.8 %collective-permute-start.20 = (bf16[272,1280]{1,0:T(8,128)(2,1)S(1)}, bf16[272,1280]{1,0:T(8,128)(2,1)S(1)}, u32[]{:S(2)}, u32[]{:S(2)}) collective-permute-start(bf16[272,1280]{1,0:T(8,128)(2,1)S(1)} %get-tuple-element.51), channel_id=1, source_target_pairs={{0,12},{4,0},{8,4},{12,8},{1,13},{5,1},{9,5},{13,9},{2,14},{6,2},{... | collective-permute-start | bytes 2088968 | tf_op jit(solution)/shard_map/ppermute | solution.py:331
  135.9 42.5 %collective-permute-start.24 = (bf16[656,1280]{1,0:T(8,128)(2,1)S(1)}, bf16[656,1280]{1,0:T(8,128)(2,1)S(1)}, u32[]{:S(2)}, u32[]{:S(2)}) collective-permute-start(bf16[656,1280]{1,0:T(8,128)(2,1)S(1)} %shard_map.57.msg), channel_id=1, source_target_pairs={{0,2},{1,3},{2,0},{3,1},{4,6},{5,7},{6,4},{7,5},{8,10},{9,11},{10,... | collective-permute-start | bytes 5038088 | tf_op jit(solution)/shard_map/ppermute | solution.py:360
  144.8 9.6 %collective-permute-start.21 = (bf16[640,1280]{1,0:T(8,128)(2,1)S(1)}, bf16[640,1280]{1,0:T(8,128)(2,1)S(1)}, u32[]{:S(2)}, u32[]{:S(2)}) collective-permute-start(bf16[640,1280]{1,0:T(8,128)(2,1)S(1)} %shard_map.59.refs_0_), channel_id=1, source_target_pairs={{0,1},{1,0},{2,3},{3,2},{4,5},{5,4},{6,7},{7,6},{8,9},{9,8},{10,11... | collective-permute-start | bytes 4915208 | tf_op jit(solution)/shard_map/ppermute | solution.py:370
  150.0 17.1 %collective-permute-start.22 = (bf16[272,1280]{1,0:T(8,128)(2,1)S(1)}, bf16[272,1280]{1,0:T(8,128)(2,1)S(1)}, u32[]{:S(2)}, u32[]{:S(2)}) collective-permute-start(bf16[272,1280]{1,0:T(8,128)(2,1)S(1)} %get-tuple-element.52), channel_id=1, source_target_pairs={{0,4},{4,8},{8,12},{12,0},{1,5},{5,9},{9,13},{13,1},{2,6},{6,10},{... | collective-permute-start | bytes 2088968 | tf_op jit(solution)/shard_map/ppermute | solution.py:392
  151.7 15.9 %collective-permute-start.23 = (bf16[272,1280]{1,0:T(8,128)(2,1)S(1)}, bf16[272,1280]{1,0:T(8,128)(2,1)S(1)}, u32[]{:S(2)}, u32[]{:S(2)}) collective-permute-start(bf16[272,1280]{1,0:T(8,128)(2,1)S(1)} %get-tuple-element.56), channel_id=1, source_target_pairs={{0,12},{4,0},{8,4},{12,8},{1,13},{5,1},{9,5},{13,9},{2,14},{6,2},{... | collective-permute-start | bytes 2088968 | tf_op jit(solution)/shard_map/ppermute | solution.py:392
  180.8 4.4 %collective-permute-start.25 = (bf16[640,1280]{1,0:T(8,128)(2,1)S(1)}, bf16[640,1280]{1,0:T(8,128)(2,1)S(1)}, u32[]{:S(2)}, u32[]{:S(2)}) collective-permute-start(bf16[640,1280]{1,0:T(8,128)(2,1)S(1)} %shard_map.64.refs_0_), channel_id=1, source_target_pairs={{0,1},{1,0},{2,3},{3,2},{4,5},{5,4},{6,7},{7,6},{8,9},{9,8},{10,11... | collective-permute-start | bytes 4915208 | tf_op jit(solution)/shard_map/ppermute | solution.py:370
  (9 other events, 48.7 us)

commit v4 on v3

--- a/solution.py
+++ b/solution.py
@@ -27,7 +27,6 @@
     ("K1", 0), ("P1", 0), ("F0", 0), ("S", 30), ("X0", 0), ("L", 0),
     ("F1", 0), ("Y1", 0), ("Z1", 0),
 )
-HALVES = (1, 1)
 TAIL = 16
 STEP = 32
 
@@ -50,7 +49,7 @@
 
 
 def encode(srcs, dst):
-    c = dst.shape[1]
+    c = srcs[0].shape[1]
     m = jnp.zeros((8, c), F32)
     for src in srcs:
 
@@ -66,7 +65,8 @@
 
 
 def encode_with(m, srcs, dst):
-    c = dst.shape[1]
+    c = m.shape[1]
+    n = sum(src.shape[0] for src in srcs)
     e = jnp.ceil(jnp.log2(jnp.clip(jnp.max(m, keepdims=True), 2.0**-118, 2.0**120)))
     scale = jnp.exp2(8.0 - e)
     first = 0
@@ -78,15 +78,25 @@
             v = src[pl.ds(at, STEP), :] * scale
             v2 = v * v
             v4 = v2 * v2
-            dst[pl.ds(first + at, STEP), :] = ((v4 * v4) * v4 * (v2 * v)).astype(BF16)
+            code = ((v4 * v4) * v4 * (v2 * v)).astype(BF16)
+            for q in range(c // 128):
+                dst[pl.ds(q * n + first + at, STEP), :] = code[:, 128 * q : 128 * (q + 1)]
 
         first += src.shape[0]
-    dst[first:, :] = jnp.broadcast_to(e, (TAIL, c)).astype(BF16)
+    dst[n * c // 128 :, :] = jnp.broadcast_to(e, (TAIL, 128)).astype(BF16)
+
+
+def message(n, c):
+    return jax.ShapeDtypeStruct((n * c // 128 + TAIL, 128), BF16)
+
+
+def part_of(msg, n, c, i):
+    return jnp.concatenate([msg[pl.ds(q * n + i, STEP), :] for q in range(c // 128)], axis=1)
 
 
 def scale_of(msg):
     n = msg.shape[0] - TAIL
-    return jnp.exp2(msg[n:, 0:128].astype(F32)[0:1, 0:1] - 8.0)
+    return jnp.exp2(msg[n:, :].astype(F32)[0:1, 0:1] - 8.0)
 
 
 def decode(y, scale):
@@ -176,17 +186,17 @@
     s = scale_of(msg)
 
     def one(i):
-        out[pl.ds(i, STEP), :] = decode(msg[pl.ds(i, STEP), :], s)
+        out[pl.ds(i, STEP), :] = decode(part_of(msg, *out.shape, i), s)
 
     looped(out.shape[0], one)
 
 
-def final_kernel(first, at, mine, got, out):
+def final_kernel(at, mine, got, out):
     s = scale_of(got)
 
     def add(i):
-        rows = pl.ds(first + i, STEP)
-        out[pl.ds(i, STEP), :] = (mine[rows, :] + decode(got[rows, :], s)).astype(BF16)
+        rows = pl.ds(i, STEP)
+        out[rows, :] = (mine[rows, :] + decode(part_of(got, *out.shape, i), s)).astype(BF16)
 
     looped(out.shape[0], add)
 
@@ -234,14 +244,15 @@
 
 def meet(terms, from_dn, from_up, sums):
     h = terms.shape[1] // 2
+    n, c = terms.shape[1:]
     dn, up = scale_of(from_dn), scale_of(from_up)
 
     def add(i):
         lo, hi = pl.ds(i, STEP), pl.ds(h + i, STEP)
-        sums[lo, :] = terms[1, lo, :] + decode(from_dn[lo, :], dn)
-        sums[hi, :] = terms[3, hi, :] + decode(from_up[hi, :], up)
-        sums[pl.ds(2 * h + i, STEP), :] = terms[0, lo, :] + decode(from_up[lo, :], up)
-        sums[pl.ds(3 * h + i, STEP), :] = terms[0, hi, :] + decode(from_dn[hi, :], dn)
+        sums[lo, :] = terms[1, lo, :] + decode(part_of(from_dn, n, c, i), dn)
+        sums[hi, :] = terms[3, hi, :] + decode(part_of(from_up, n, c, h + i), up)
+        sums[pl.ds(2 * h + i, STEP), :] = terms[0, lo, :] + decode(part_of(from_up, n, c, i), up)
+        sums[pl.ds(3 * h + i, STEP), :] = terms[0, hi, :] + decode(part_of(from_dn, n, c, h + i), dn)
 
     looped(h, add)
 
@@ -259,14 +270,13 @@
 
 def last_kernel(at, sums_a, sums_b, second_dn, second_up, out):
     dn, up = scale_of(second_dn), scale_of(second_up)
-    h = sums_a.shape[0] // 4
+    h, c = sums_a.shape[0] // 4, sums_a.shape[1]
     for k, sums in enumerate((sums_a, sums_b)):
         first = lax.rem(at[1] + k, 2) * (2 * h)
 
         def add(i):
-            msg = pl.ds(k * h + i, STEP)
-            a = sums[pl.ds(2 * h + i, STEP), :] + decode(second_dn[msg, :], dn)
-            b = sums[pl.ds(3 * h + i, STEP), :] + decode(second_up[msg, :], up)
+            a = sums[pl.ds(2 * h + i, STEP), :] + decode(part_of(second_dn, 2 * h, c, k * h + i), dn)
+            b = sums[pl.ds(3 * h + i, STEP), :] + decode(part_of(second_up, 2 * h, c, k * h + i), up)
             out[pl.ds(pl.multiple_of(first + i, STEP), STEP), :] = a.astype(BF16)
             out[pl.ds(pl.multiple_of(first + h + i, STEP), STEP), :] = b.astype(BF16)
 
@@ -317,7 +327,7 @@
         return results
 
     def terms_of(side, us=0):
-        msg = shape(rows + TAIL, features, dtype=BF16)
+        msg = message(rows, features)
         up, dn, terms = ordered(
             term_kernel,
             [msg, msg, shape(4, rows, features)],
@@ -351,7 +361,7 @@
         parts = env["K%d" % j]
         (msg,) = ordered(
             pair_kernel,
-            [shape(half + TAIL, width, dtype=BF16)],
+            [message(half, width)],
             [pltpu.VMEM((half, width), F32)],
             [VMEM] * len(parts),
             *parts,
@@ -363,11 +373,8 @@
         width = spans[j][1]
         sent, got = env["P%d" % j]
         (mine,) = call(decode_kernel, [shape(half, width)], (), [VMEM])(sent)
-        own, n = [], half // HALVES[j]
-        for first in range(0, half, n):
-            kernel = functools.partial(final_kernel, first)
-            own += ordered(kernel, [shape(n, width, dtype=BF16)], (), [VMEM] * 2, mine, got, us=us)
-        return own, [lax.ppermute(v, "dp", CORE_SWAP) for v in own]
+        own = ordered(final_kernel, [shape(half, width, dtype=BF16)], (), [VMEM] * 2, mine, got, us=us)
+        return list(own), [lax.ppermute(v, "dp", CORE_SWAP) for v in own]
 
     def turn(us=0):
         (turned,) = ordered(
@@ -385,7 +392,7 @@
         return sums
 
     def second_of(us=0):
-        msg = shape(rows + TAIL, features, dtype=BF16)
+        msg = message(rows, features)
         up, dn, sums = ordered(
             second_kernel, [msg, msg, shape(2 * rows, features)], (), [VMEM] * 4, env["M"], *env["B"], mib=18, us=us
         )

time: 187 us -> 186 us (level)
  transfers between devices with their start and end apart: 26 -> 26, of which waited for: 10 -> 10; matrix products, arithmetic and copies ran while one was open for 1% -> 1% of each run, Pallas kernels for 35% -> 36%
where the time goes in v4:
time: 186 us
  Pallas kernels  74.1 us (40%)
  waiting for transfers between devices  62.3 us (33%)
  starting transfers between devices  39.9 us (21%)
  local copies, waits for them, and re-layouts  8.21 us (4%)
    pallas_call x15, Pallas kernels, ordered(): call(kernel, outs, scratch, [SMEM] + specs, **kw)  70.8 us
    ppermute x1, waiting for transfers between devices, local(): a_dn = lax.ppermute(a, 'row', X_UP)  23 us
    ppermute x2, waiting for transfers between devices, pair_of(): return (msg, lax.ppermute(msg, 'dp', FAR_SWAP))  13.2 us
    ppermute x1, waiting for transfers between devices, second_of(): lax.ppermute(up, 'col', Z_UP)  9.75 us
    ppermute x1, waiting for transfers between devices, local(): far_hi = lax.ppermute(a_dn[h:], 'row', X_UP)  7.36 us
    unnamed x30, local copies, waits for them, and re-layouts  7.17 us
    ppermute x3, waiting for transfers between devices, weight_of(): lax.ppermute(give, 'dp', CORE_SWAP)  4.95 us
    ppermute x3, starting transfers between devices, weight_of(): lax.ppermute(give, 'dp', CORE_SWAP)  4.58 us
  transfers between devices with their start and end apart: 26, of which 10 were waited for; matrix products, arithmetic and copies ran while one was open for 1% of the time, Pallas kernels for 36%

profile of v4, /device:TPU:1, one launch (start us, length us, event | category | flops | bytes accessed | tf_op | source)
XLA Modules:
  0.0 185.6 jit_solution(12718322151245038048)
XLA Ops:
  0.6 2.1 %collective-permute-start.2 = (bf16[256,2560]{1,0:T(8,128)(2,1)}, bf16[256,2560]{1,0:T(8,128)(2,1)S(1)}, u32[]{:S(2)}, u32[]{:S(2)}) collective-permute-start(bf16[256,2560]{1,0:T(8,128)(2,1)} %bitcast.9), channel_id=1, source_target_pairs={{0,32},{16,48},{32,64},{48,80},{64,96},{80,112},{96,0},{112,16},{1... | collective-permute-start | bytes 3932168 | tf_op jit(solution)/shard_map/ppermute | solution.py:300
  4.1 3.9 %collective-permute-start.4 = (bf16[512,1280]{1,0:T(8,128)(2,1)}, bf16[512,1280]{1,0:T(8,128)(2,1)S(1)}, u32[]{:S(2)}, u32[]{:S(2)}) collective-permute-start(bf16[512,1280]{1,0:T(8,128)(2,1)} %bitcast.15), channel_id=1, source_target_pairs={{0,12},{4,0},{8,4},{12,8},{1,13},{5,1},{9,5},{13,9},{2,14},{6,2},{... | collective-permute-start | bytes 3932168 | tf_op jit(solution)/shard_map/ppermute | solution.py:304
  9.3 23.0 %collective-permute-done.2.refs_4_ = bf16[256,2560]{1,0:T(8,128)(2,1)S(1)} collective-permute-done((bf16[256,2560]{1,0:T(8,128)(2,1)}, bf16[256,2560]{1,0:T(8,128)(2,1)S(1)}, u32[]{:S(2)}, u32[]{:S(2)}) %collective-permute-start.2) | collective-permute-done | bytes 1310752 | tf_op jit(solution)/shard_map/ppermute | solution.py:300
  32.9 2.3 %collective-permute-start.1 = (bf16[128,2560]{1,0:T(8,128)(2,1)S(1)}, bf16[128,2560]{1,0:T(8,128)(2,1)}, u32[]{:S(2)}, u32[]{:S(2)}) collective-permute-start(bf16[128,2560]{1,0:T(8,128)(2,1)S(1)} %slice.16), channel_id=1, source_target_pairs={{0,96},{16,112},{32,0},{48,16},{64,32},{80,48},{96,64},{112,80},{1... | collective-permute-start | bytes 1966088 | tf_op jit(solution)/shard_map/ppermute | solution.py:305
  36.3 4.1 %collective-permute-start.5 = (bf16[256,1280]{1,0:T(8,128)(2,1)S(1)}, bf16[256,1280]{1,0:T(8,128)(2,1)S(1)}, u32[]{:S(2)}, u32[]{:S(2)}) collective-permute-start(bf16[256,1280]{1,0:T(8,128)(2,1)S(1)} %slice.18), channel_id=1, source_target_pairs={{0,12},{4,0},{8,4},{12,8},{1,13},{5,1},{9,5},{13,9},{2,14},{6,2},{... | collective-permute-start | bytes 1966088 | tf_op jit(solution)/shard_map/ppermute | solution.py:309
  40.8 7.4 %collective-permute-done.3.refs_3_ = bf16[128,2560]{1,0:T(8,128)(2,1)S(1)} collective-permute-done((bf16[128,2560]{1,0:T(8,128)(2,1)S(1)}, bf16[128,2560]{1,0:T(8,128)(2,1)S(1)}, u32[]{:S(2)}, u32[]{:S(2)}) %collective-permute-start.3) | collective-permute-done | bytes 655392 | tf_op jit(solution)/shard_map/ppermute | solution.py:306
  50.1 2.1 %collective-permute-start.7 = (bf16[256,1280]{1,0:T(8,128)(2,1)}, bf16[256,1280]{1,0:T(8,128)(2,1)}, u32[]{:S(2)}, u32[]{:S(2)}) collective-permute-start(bf16[256,1280]{1,0:T(8,128)(2,1)} %slice.19), channel_id=1, source_target_pairs={{0,4},{4,8},{8,12},{12,0},{1,5},{5,9},{9,13},{13,1},{2,6},{6,10},{... | collective-permute-start | bytes 1966088 | tf_op jit(solution)/shard_map/ppermute | solution.py:310
  54.6 2.9 %copy-done = bf16[1280,2560]{1,0:T(8,128)(2,1)S(1)} copy-done((bf16[1280,2560]{1,0:T(8,128)(2,1)S(1)}, bf16[1280,2560]{1,0:T(8,128)(2,1)}, u32[]{:S(2)}) %copy-start) | copy-done | bytes 6553624
  58.8 11.6 %shard_map.50 = (bf16[2576,128]{1,0:T(8,128)(2,1)S(1)}, bf16[2576,128]{1,0:T(8,128)(2,1)S(1)}, f32[4,256,1280]{2,1,0:T(8,128)S(1)}) custom-call(s32[4]{0:T(128)S(1)} %pad_add_fusion.at, bf16[1280,2560]{1,0:T(8,128)(2,1)S(1)} %copy-done, bf16[256,2560]{1,0:T(8,128)(2,1)S(1)} %bitcast.12, bf16[256,2560]{1,0:T(8,128)(2,1)S(1)} %collective-permute-done.refs_1_, ...), custom_call_target="tpu_custom_call" | custom-call | flops 1 | bytes 1 | tf_op jit(solution)/shard_map/pallas_call | solution.py:325
  72.1 2.0 %collective-permute-start.14 = (bf16[2576,128]{1,0:T(8,128)(2,1)S(1)}, bf16[2576,128]{1,0:T(8,128)(2,1)S(1)}, u32[]{:S(2)}, u32[]{:S(2)}) collective-permute-start(bf16[2576,128]{1,0:T(8,128)(2,1)S(1)} %get-tuple-element.38), channel_id=1, source_target_pairs={{0,12},{4,0},{8,4},{12,8},{1,13},{5,1},{9,5},{13,9},{2,14},{6,2},{... | collective-permute-start | bytes 1978376 | tf_op jit(solution)/shard_map/ppermute | solution.py:341
  74.1 3.6 %shard_map.51.inputs = bf16[1280,2048]{1,0:T(8,128)(2,1)S(1)} custom-call(s32[4]{0:T(128)S(1)} %pad_add_fusion.at, bf16[512,1280]{1,0:T(8,128)(2,1)S(1)} %bitcast.17, bf16[512,1280]{1,0:T(8,128)(2,1)S(1)} %copy-done.7, bf16[256,1280]{1,0:T(8,128)(2,1)S(1)} %copy-done.12, bf16[256,1280]{1,0:T(8,128)(2,1)} %collective-permute-done.7.refs_3_, ...), custom_call_target="tpu_custom_call" | custom-call | flops 1 | bytes 1 | tf_op jit(solution)/shard_map/pallas_call | solution.py:325
  77.7 2.1 %collective-permute-done.10.refs_7_.refs_2_ = bf16[128,2560]{1,0:T(8,128)(2,1)} collective-permute-done((bf16[128,2560]{1,0:T(8,128)(2,1)}, bf16[128,2560]{1,0:T(8,128)(2,1)}, u32[]{:S(2)}, u32[]{:S(2)}) %collective-permute-start.10) | collective-permute-done | bytes 655392 | tf_op jit(solution)/shard_map/ppermute | solution.py:311
  79.9 9.5 %shard_map.52 = (f32[640,1280]{1,0:T(8,128)}, f32[640,1280]{1,0:T(8,128)S(1)}) custom-call(s32[4]{0:T(128)S(1)} %pad_add_fusion.at, bf16[1280,2048]{1,0:T(8,128)(2,1)S(1)} %shard_map.51.inputs, bf16[256,2560]{1,0:T(8,128)(2,1)S(1)} %bitcast.13, bf16[256,2560]{1,0:T(8,128)(2,1)S(1)} %collective-permute-done.refs_1_, ...), custom_call_target="tpu_custom_call" | custom-call | flops 6000000000 | bytes 1 | tf_op jit(solution)/shard_map/pallas_call | solution.py:325
  89.4 3.8 %collective-permute-start.15 = (f32[640,1280]{1,0:T(8,128)}, f32[640,1280]{1,0:T(8,128)}, u32[]{:S(2)}, u32[]{:S(2)}) collective-permute-start(f32[640,1280]{1,0:T(8,128)} %get-tuple-element.35), channel_id=1, source_target_pairs={{0,1},{1,0},{2,3},{3,2},{4,5},{5,4},{6,7},{7,6},{8,9},{9,8},{10,11... | collective-permute-start | bytes 9830408 | tf_op jit(solution)/shard_map/ppermute | solution.py:357
  93.2 1.9 %shard_map.53.sums_a = f32[512,1280]{1,0:T(8,128)S(1)} custom-call(s32[4]{0:T(128)S(1)} %pad_add_fusion.at, f32[4,256,1280]{2,1,0:T(8,128)S(1)} %get-tuple-element.37.terms, bf16[2576,128]{1,0:T(8,128)(2,1)S(1)} %collective-permute-done.13.from_dn, bf16[2576,128]{1,0:T(8,128)(2,1)S(1)} %collective-permute-done.14.from_up), custom_call_target="tpu_custom_call" | custom-call | flops 149999992832 | bytes 1 | tf_op jit(solution)/shard_map/pallas_call | solution.py:325
  95.1 3.9 %collective-permute-done.15.refs_0_ = f32[640,1280]{1,0:T(8,128)} collective-permute-done((f32[640,1280]{1,0:T(8,128)}, f32[640,1280]{1,0:T(8,128)}, u32[]{:S(2)}, u32[]{:S(2)}) %collective-permute-start.15) | collective-permute-done | bytes 3276832 | tf_op jit(solution)/shard_map/ppermute | solution.py:357
  99.0 3.7 %shard_map.54.msg = bf16[6416,128]{1,0:T(8,128)(2,1)S(1)} custom-call(s32[4]{0:T(128)S(1)} %pad_add_fusion.at, f32[640,1280]{1,0:T(8,128)S(1)} %get-tuple-element.40.keep, f32[640,1280]{1,0:T(8,128)} %collective-permute-done.15.refs_0_), custom_call_target="tpu_custom_call" | custom-call | flops 1 | bytes 1 | tf_op jit(solution)/shard_map/pallas_call | solution.py:325
  102.7 3.2 %collective-permute-start.18 = (bf16[6416,128]{1,0:T(8,128)(2,1)S(1)}, bf16[6416,128]{1,0:T(8,128)(2,1)S(1)}, u32[]{:S(2)}, u32[]{:S(2)}) collective-permute-start(bf16[6416,128]{1,0:T(8,128)(2,1)S(1)} %shard_map.54.msg), channel_id=1, source_target_pairs={{0,2},{1,3},{2,0},{3,1},{4,6},{5,7},{6,4},{7,5},{8,10},{9,11},{10,... | collective-permute-start | bytes 4927496 | tf_op jit(solution)/shard_map/ppermute | solution.py:370
  105.9 12.5 %shard_map.55 = (bf16[2576,128]{1,0:T(8,128)(2,1)S(1)}, bf16[2576,128]{1,0:T(8,128)(2,1)S(1)}, f32[4,256,1280]{2,1,0:T(8,128)S(1)}) custom-call(s32[4]{0:T(128)S(1)} %pad_add_fusion.at, bf16[1280,2560]{1,0:T(8,128)(2,1)S(1)} %copy-done.1, bf16[256,2560]{1,0:T(8,128)(2,1)} %collective-permute-done.8.refs_5_.refs_0_, ...), custom_call_target="tpu_custom_call" | custom-call | flops 1 | bytes 1 | tf_op jit(solution)/shard_map/pallas_call | solution.py:325
  118.4 9.2 %shard_map.56 = (f32[320,1280]{1,0:T(8,128)S(1)}, f32[320,1280]{1,0:T(8,128)S(1)}, f32[640,1280]{1,0:T(8,128)S(1)}) custom-call(s32[4]{0:T(128)S(1)} %pad_add_fusion.at, bf16[1280,2048]{1,0:T(8,128)(2,1)S(1)} %bitcast.8, bf16[256,2560]{1,0:T(8,128)(2,1)S(1)} %bitcast.14, bf16[256,2560]{1,0:T(8,128)(2,1)S(1)} %collective-permute-done.refs_1_, ...), custom_call_target="tpu_custom_call" | custom-call | flops 1 | bytes 1 | tf_op jit(solution)/shard_map/pallas_call | solution.py:325
  133.8 2.1 %shard_map.57.msg = bf16[6416,128]{1,0:T(8,128)(2,1)S(1)} custom-call(s32[4]{0:T(128)S(1)} %pad_add_fusion.at, f32[640,1280]{1,0:T(8,128)S(1)} %get-tuple-element.46.keep, f32[320,1280]{1,0:T(8,128)S(1)} %collective-permute-done.16.refs_0_, f32[320,1280]{1,0:T(8,128)S(1)} %collective-permute-done.17.refs_1_), custom_call_target="tpu_custom_call" | custom-call | flops 1 | bytes 1 | tf_op jit(solution)/shard_map/pallas_call | solution.py:325
  136.0 5.5 %collective-permute-done.18.got = bf16[6416,128]{1,0:T(8,128)(2,1)S(1)} collective-permute-done((bf16[6416,128]{1,0:T(8,128)(2,1)S(1)}, bf16[6416,128]{1,0:T(8,128)(2,1)S(1)}, u32[]{:S(2)}, u32[]{:S(2)}) %collective-permute-start.18) | collective-permute-done | bytes 1642528 | tf_op jit(solution)/shard_map/ppermute | solution.py:370
  141.6 2.5 %shard_map.59.refs_0_ = bf16[640,1280]{1,0:T(8,128)(2,1)S(1)} custom-call(s32[4]{0:T(128)S(1)} %pad_add_fusion.at, f32[640,1280]{1,0:T(8,128)S(1)} %shard_map.58.mine, bf16[6416,128]{1,0:T(8,128)(2,1)S(1)} %collective-permute-done.18.got), custom_call_target="tpu_custom_call" | custom-call | flops 1 | bytes 1 | tf_op jit(solution)/shard_map/pallas_call | solution.py:325
  144.1 2.1 %collective-permute-start.21 = (bf16[640,1280]{1,0:T(8,128)(2,1)S(1)}, bf16[640,1280]{1,0:T(8,128)(2,1)S(1)}, u32[]{:S(2)}, u32[]{:S(2)}) collective-permute-start(bf16[640,1280]{1,0:T(8,128)(2,1)S(1)} %shard_map.59.refs_0_), channel_id=1, source_target_pairs={{0,1},{1,0},{2,3},{3,2},{4,5},{5,4},{6,7},{7,6},{8,9},{9,8},{10,11... | collective-permute-start | bytes 4915208 | tf_op jit(solution)/shard_map/ppermute | solution.py:377
  146.2 3.1 %shard_map.60 = (bf16[2576,128]{1,0:T(8,128)(2,1)S(1)}, bf16[2576,128]{1,0:T(8,128)(2,1)S(1)}, f32[512,1280]{1,0:T(8,128)S(1)}) custom-call(s32[4]{0:T(128)S(1)} %pad_add_fusion.at, f32[512,1280]{1,0:T(8,128)S(1)} %shard_map.53.sums_a, f32[4,256,1280]{2,1,0:T(8,128)S(1)} %get-tuple-element.50.terms, bf16[2576,128]{1,0:T(8,128)(2,1)S(1)} %collective-permute-done.19.from_dn, ...), custom_call_target="tpu_custom_call" | custom-call | flops 30000001024 | bytes 1 | tf_op jit(solution)/shard_map/pallas_call | solution.py:325
  153.7 2.3 %shard_map.61.refs_1_ = bf16[1280,2560]{1,0:T(8,128)(2,1)} custom-call(s32[4]{0:T(128)S(1)} %pad_add_fusion.at, bf16[640,1280]{1,0:T(8,128)(2,1)S(1)} %shard_map.59.refs_0_, bf16[640,1280]{1,0:T(8,128)(2,1)S(1)} %collective-permute-done.21.refs_1_), custom_call_target="tpu_custom_call" | custom-call | flops 1 | bytes 1 | tf_op jit(solution)/shard_map/pallas_call | solution.py:325
  155.9 9.7 %collective-permute-done.22.second_dn = bf16[2576,128]{1,0:T(8,128)(2,1)S(1)} collective-permute-done((bf16[2576,128]{1,0:T(8,128)(2,1)S(1)}, bf16[2576,128]{1,0:T(8,128)(2,1)S(1)}, u32[]{:S(2)}, u32[]{:S(2)}) %collective-permute-start.22) | collective-permute-done | bytes 659488 | tf_op jit(solution)/shard_map/ppermute | solution.py:399
  166.1 3.0 %shard_map.62 = bf16[512,1280]{1,0:T(8,128)(2,1)} custom-call(s32[4]{0:T(128)S(1)} %pad_add_fusion.at, f32[512,1280]{1,0:T(8,128)S(1)} %shard_map.53.sums_a, f32[512,1280]{1,0:T(8,128)S(1)} %get-tuple-element.55.sums_b, bf16[2576,128]{1,0:T(8,128)(2,1)S(1)} %collective-permute-done.22.second_dn, bf16[2576,128]{1,0:T(8,128)(2,1)S(1)} %collective-permute-done.23.second_up), custom_call_target="tpu_custom_call" | custom-call | flops 1 | bytes 1 | tf_op jit(solution)/shard_map/pallas_call | solution.py:325
  169.1 7.6 %collective-permute-done.24.got = bf16[6416,128]{1,0:T(8,128)(2,1)S(1)} collective-permute-done((bf16[6416,128]{1,0:T(8,128)(2,1)S(1)}, bf16[6416,128]{1,0:T(8,128)(2,1)S(1)}, u32[]{:S(2)}, u32[]{:S(2)}) %collective-permute-start.24) | collective-permute-done | bytes 1642528 | tf_op jit(solution)/shard_map/ppermute | solution.py:370
  176.8 2.5 %shard_map.64.refs_0_ = bf16[640,1280]{1,0:T(8,128)(2,1)S(1)} custom-call(s32[4]{0:T(128)S(1)} %pad_add_fusion.at, f32[640,1280]{1,0:T(8,128)S(1)} %shard_map.63.mine, bf16[6416,128]{1,0:T(8,128)(2,1)S(1)} %collective-permute-done.24.got), custom_call_target="tpu_custom_call" | custom-call | flops 1 | bytes 1 | tf_op jit(solution)/shard_map/pallas_call | solution.py:325
  180.5 1.7 shard_map.65.refs_1_
  183.7 1.7 shard_map.66
  (73 shorter events, 26.1 us)
Async XLA Ops:
  0.6 31.6 %collective-permute-start.2 = (bf16[256,2560]{1,0:T(8,128)(2,1)}, bf16[256,2560]{1,0:T(8,128)(2,1)S(1)}, u32[]{:S(2)}, u32[]{:S(2)}) collective-permute-start(bf16[256,2560]{1,0:T(8,128)(2,1)} %bitcast.9), channel_id=1, source_target_pairs={{0,32},{16,48},{32,64},{48,80},{64,96},{80,112},{96,0},{112,16},{1... | collective-permute-start | bytes 3932168 | tf_op jit(solution)/shard_map/ppermute | solution.py:300
  2.7 30.1 %collective-permute-start = (bf16[256,2560]{1,0:T(8,128)(2,1)}, bf16[256,2560]{1,0:T(8,128)(2,1)S(1)}, u32[]{:S(2)}, u32[]{:S(2)}) collective-permute-start(bf16[256,2560]{1,0:T(8,128)(2,1)} %bitcast.10), channel_id=1, source_target_pairs={{0,96},{16,112},{32,0},{48,16},{64,32},{80,48},{96,64},{112,80},{1... | collective-permute-start | bytes 3932168 | tf_op jit(solution)/shard_map/ppermute | solution.py:301
  4.1 31.1 %collective-permute-start.4 = (bf16[512,1280]{1,0:T(8,128)(2,1)}, bf16[512,1280]{1,0:T(8,128)(2,1)S(1)}, u32[]{:S(2)}, u32[]{:S(2)}) collective-permute-start(bf16[512,1280]{1,0:T(8,128)(2,1)} %bitcast.15), channel_id=1, source_target_pairs={{0,12},{4,0},{8,4},{12,8},{1,13},{5,1},{9,5},{13,9},{2,14},{6,2},{... | collective-permute-start | bytes 3932168 | tf_op jit(solution)/shard_map/ppermute | solution.py:304
  8.0 32.4 %collective-permute-start.8 = (bf16[256,2560]{1,0:T(8,128)(2,1)}, bf16[256,2560]{1,0:T(8,128)(2,1)}, u32[]{:S(2)}, u32[]{:S(2)}) collective-permute-start(bf16[256,2560]{1,0:T(8,128)(2,1)} %bitcast.11), channel_id=1, source_target_pairs={{0,16},{16,0},{32,48},{48,32},{64,80},{80,64},{96,112},{112,96},{1... | collective-permute-start | bytes 3932168 | tf_op jit(solution)/shard_map/ppermute | solution.py:302
  9.3 38.9 %collective-permute-start.6 = (bf16[512,1280]{1,0:T(8,128)(2,1)}, bf16[512,1280]{1,0:T(8,128)(2,1)S(1)}, u32[]{:S(2)}, u32[]{:S(2)}) collective-permute-start(bf16[512,1280]{1,0:T(8,128)(2,1)} %bitcast.16), channel_id=1, source_target_pairs={{0,4},{4,8},{8,12},{12,0},{1,5},{5,9},{9,13},{13,1},{2,6},{6,10},{... | collective-permute-start | bytes 3932168 | tf_op jit(solution)/shard_map/ppermute | solution.py:303
  32.3 15.8 %collective-permute-start.3 = (bf16[128,2560]{1,0:T(8,128)(2,1)S(1)}, bf16[128,2560]{1,0:T(8,128)(2,1)S(1)}, u32[]{:S(2)}, u32[]{:S(2)}) collective-permute-start(bf16[128,2560]{1,0:T(8,128)(2,1)S(1)} %slice.17), channel_id=1, source_target_pairs={{0,32},{16,48},{32,64},{48,80},{64,96},{80,112},{96,0},{112,16},{1... | collective-permute-start | bytes 1966088 | tf_op jit(solution)/shard_map/ppermute | solution.py:306
  32.9 19.4 %collective-permute-start.1 = (bf16[128,2560]{1,0:T(8,128)(2,1)S(1)}, bf16[128,2560]{1,0:T(8,128)(2,1)}, u32[]{:S(2)}, u32[]{:S(2)}) collective-permute-start(bf16[128,2560]{1,0:T(8,128)(2,1)S(1)} %slice.16), channel_id=1, source_target_pairs={{0,96},{16,112},{32,0},{48,16},{64,32},{80,48},{96,64},{112,80},{1... | collective-permute-start | bytes 1966088 | tf_op jit(solution)/shard_map/ppermute | solution.py:305
  36.3 17.2 %collective-permute-start.5 = (bf16[256,1280]{1,0:T(8,128)(2,1)S(1)}, bf16[256,1280]{1,0:T(8,128)(2,1)S(1)}, u32[]{:S(2)}, u32[]{:S(2)}) collective-permute-start(bf16[256,1280]{1,0:T(8,128)(2,1)S(1)} %slice.18), channel_id=1, source_target_pairs={{0,12},{4,0},{8,4},{12,8},{1,13},{5,1},{9,5},{13,9},{2,14},{6,2},{... | collective-permute-start | bytes 1966088 | tf_op jit(solution)/shard_map/ppermute | solution.py:309
  40.4 39.5 %collective-permute-start.9 = (bf16[256,2560]{1,0:T(8,128)(2,1)}, bf16[256,2560]{1,0:T(8,128)(2,1)}, u32[]{:S(2)}, u32[]{:S(2)}) collective-permute-start(bf16[256,2560]{1,0:T(8,128)(2,1)} %collective-permute-done.8.refs_5_.refs_0_), channel_id=1, source_target_pairs={{0,96},{16,112},{32,0},{48,16},{64,32},{80,48},{96,64},{112,80},{1... | collective-permute-start | bytes 3932168 | tf_op jit(solution)/shard_map/ppermute | solution.py:308
  48.2 31.7 %collective-permute-start.12 = (bf16[256,2560]{1,0:T(8,128)(2,1)}, bf16[256,2560]{1,0:T(8,128)(2,1)}, u32[]{:S(2)}, u32[]{:S(2)}) collective-permute-start(bf16[256,2560]{1,0:T(8,128)(2,1)} %collective-permute-done.8.refs_5_.refs_0_), channel_id=1, source_target_pairs={{0,32},{16,48},{32,64},{48,80},{64,96},{80,112},{96,0},{112,16},{1... | collective-permute-start | bytes 3932168 | tf_op jit(solution)/shard_map/ppermute | solution.py:307
  50.1 20.3 %collective-permute-start.7 = (bf16[256,1280]{1,0:T(8,128)(2,1)}, bf16[256,1280]{1,0:T(8,128)(2,1)}, u32[]{:S(2)}, u32[]{:S(2)}) collective-permute-start(bf16[256,1280]{1,0:T(8,128)(2,1)} %slice.19), channel_id=1, source_target_pairs={{0,4},{4,8},{8,12},{12,0},{1,5},{5,9},{9,13},{13,1},{2,6},{6,10},{... | collective-permute-start | bytes 1966088 | tf_op jit(solution)/shard_map/ppermute | solution.py:310
  52.2 19.9 %collective-permute-start.11 = (bf16[128,2560]{1,0:T(8,128)(2,1)S(1)}, bf16[128,2560]{1,0:T(8,128)(2,1)}, u32[]{:S(2)}, u32[]{:S(2)}) collective-permute-start(bf16[128,2560]{1,0:T(8,128)(2,1)S(1)} %collective-permute-done.3.refs_3_), channel_id=1, source_target_pairs={{0,16},{16,0},{32,48},{48,32},{64,80},{80,64},{96,112},{112,96},{1... | collective-permute-start | bytes 1966088 | tf_op jit(solution)/shard_map/ppermute | solution.py:312
  54.4 25.5 %collective-permute-start.10 = (bf16[128,2560]{1,0:T(8,128)(2,1)}, bf16[128,2560]{1,0:T(8,128)(2,1)}, u32[]{:S(2)}, u32[]{:S(2)}) collective-permute-start(bf16[128,2560]{1,0:T(8,128)(2,1)} %collective-permute-done.1.refs_2_), channel_id=1, source_target_pairs={{0,16},{16,0},{32,48},{48,32},{64,80},{80,64},{96,112},{112,96},{1... | collective-permute-start | bytes 1966088 | tf_op jit(solution)/shard_map/ppermute | solution.py:311
  58.8 15.3 %copy-start.9 = (bf16[512,1280]{1,0:T(8,128)(2,1)S(1)}, bf16[512,1280]{1,0:T(8,128)(2,1)}, u32[]{:S(2)}) copy-start(bf16[512,1280]{1,0:T(8,128)(2,1)} %copy-done.8) | copy-start | bytes 3932164
  58.8 15.3 %copy-start.10 = (bf16[1,512,1280]{2,1,0:T(8,128)(2,1)S(1)}, bf16[1,512,1280]{2,1,0:T(8,128)(2,1)}, u32[]{:S(2)}) copy-start(bf16[1,512,1280]{2,1,0:T(8,128)(2,1)} %param.3) | copy-start | bytes 3932164
  58.8 15.3 %copy-start.12 = (bf16[256,1280]{1,0:T(8,128)(2,1)S(1)}, bf16[256,1280]{1,0:T(8,128)(2,1)}, u32[]{:S(2)}) copy-start(bf16[256,1280]{1,0:T(8,128)(2,1)} %copy-done.11) | copy-start | bytes 1966084
  70.4 22.7 %collective-permute-start.13 = (bf16[2576,128]{1,0:T(8,128)(2,1)S(1)}, bf16[2576,128]{1,0:T(8,128)(2,1)S(1)}, u32[]{:S(2)}, u32[]{:S(2)}) collective-permute-start(bf16[2576,128]{1,0:T(8,128)(2,1)S(1)} %get-tuple-element.31), channel_id=1, source_target_pairs={{0,4},{4,8},{8,12},{12,0},{1,5},{5,9},{9,13},{13,1},{2,6},{6,10},{... | collective-permute-start | bytes 1978376 | tf_op jit(solution)/shard_map/ppermute | solution.py:341
  72.1 21.0 %collective-permute-start.14 = (bf16[2576,128]{1,0:T(8,128)(2,1)S(1)}, bf16[2576,128]{1,0:T(8,128)(2,1)S(1)}, u32[]{:S(2)}, u32[]{:S(2)}) collective-permute-start(bf16[2576,128]{1,0:T(8,128)(2,1)S(1)} %get-tuple-element.38), channel_id=1, source_target_pairs={{0,12},{4,0},{8,4},{12,8},{1,13},{5,1},{9,5},{13,9},{2,14},{6,2},{... | collective-permute-start | bytes 1978376 | tf_op jit(solution)/shard_map/ppermute | solution.py:341
  89.4 9.6 %collective-permute-start.15 = (f32[640,1280]{1,0:T(8,128)}, f32[640,1280]{1,0:T(8,128)}, u32[]{:S(2)}, u32[]{:S(2)}) collective-permute-start(f32[640,1280]{1,0:T(8,128)} %get-tuple-element.35), channel_id=1, source_target_pairs={{0,1},{1,0},{2,3},{3,2},{4,5},{5,4},{6,7},{7,6},{8,9},{9,8},{10,11... | collective-permute-start | bytes 9830408 | tf_op jit(solution)/shard_map/ppermute | solution.py:357
  99.0 19.4 %slice-start = ((s8[5242880]{0:T(1024)(128)(4,1)}), s8[4194304]{0:T(1024)(128)(4,1)S(1)}, s32[]{:S(2)}) async-start(s8[5242880]{0:T(1024)(128)(4,1)} %bitcast.7), calls=%async_computation | async-start | bytes 8388608
  102.6 15.7 %slice-start.1 = ((s8[5242880]{0:T(1024)(128)(4,1)}), s8[1048576]{0:T(1024)(128)(4,1)S(1)}, s32[]{:S(2)}) async-start(s8[5242880]{0:T(1024)(128)(4,1)} %bitcast.7), calls=%async_computation.1 | async-start | bytes 2097152
  102.7 15.7 %copy-start.5 = (bf16[1,256,2560]{2,1,0:T(8,128)(2,1)S(1)}, bf16[1,256,2560]{2,1,0:T(8,128)(2,1)}, u32[]{:S(2)}) copy-start(bf16[1,256,2560]{2,1,0:T(8,128)(2,1)} %param.4) | copy-start | bytes 3932164
  102.7 38.9 %collective-permute-start.18 = (bf16[6416,128]{1,0:T(8,128)(2,1)S(1)}, bf16[6416,128]{1,0:T(8,128)(2,1)S(1)}, u32[]{:S(2)}, u32[]{:S(2)}) collective-permute-start(bf16[6416,128]{1,0:T(8,128)(2,1)S(1)} %shard_map.54.msg), channel_id=1, source_target_pairs={{0,2},{1,3},{2,0},{3,1},{4,6},{5,7},{6,4},{7,5},{8,10},{9,11},{10,... | collective-permute-start | bytes 4927496 | tf_op jit(solution)/shard_map/ppermute | solution.py:370
  127.6 5.2 %collective-permute-start.16 = (f32[320,1280]{1,0:T(8,128)S(1)}, f32[320,1280]{1,0:T(8,128)S(1)}, u32[]{:S(2)}, u32[]{:S(2)}) collective-permute-start(f32[320,1280]{1,0:T(8,128)S(1)} %get-tuple-element.44), channel_id=1, source_target_pairs={{0,1},{1,0},{2,3},{3,2},{4,5},{5,4},{6,7},{7,6},{8,9},{9,8},{10,11... | collective-permute-start | bytes 4915208 | tf_op jit(solution)/shard_map/ppermute | solution.py:357
  128.3 5.5 %collective-permute-start.17 = (f32[320,1280]{1,0:T(8,128)S(1)}, f32[320,1280]{1,0:T(8,128)S(1)}, u32[]{:S(2)}, u32[]{:S(2)}) collective-permute-start(f32[320,1280]{1,0:T(8,128)S(1)} %get-tuple-element.47), channel_id=1, source_target_pairs={{0,1},{1,0},{2,3},{3,2},{4,5},{5,4},{6,7},{7,6},{8,9},{9,8},{10,11... | collective-permute-start | bytes 4915208 | tf_op jit(solution)/shard_map/ppermute | solution.py:357
  128.4 17.7 %collective-permute-start.19 = (bf16[2576,128]{1,0:T(8,128)(2,1)S(1)}, bf16[2576,128]{1,0:T(8,128)(2,1)S(1)}, u32[]{:S(2)}, u32[]{:S(2)}) collective-permute-start(bf16[2576,128]{1,0:T(8,128)(2,1)S(1)} %get-tuple-element.42), channel_id=1, source_target_pairs={{0,4},{4,8},{8,12},{12,0},{1,5},{5,9},{9,13},{13,1},{2,6},{6,10},{... | collective-permute-start | bytes 1978376 | tf_op jit(solution)/shard_map/ppermute | solution.py:341
  130.1 16.1 %collective-permute-start.20 = (bf16[2576,128]{1,0:T(8,128)(2,1)S(1)}, bf16[2576,128]{1,0:T(8,128)(2,1)S(1)}, u32[]{:S(2)}, u32[]{:S(2)}) collective-permute-start(bf16[2576,128]{1,0:T(8,128)(2,1)S(1)} %get-tuple-element.51), channel_id=1, source_target_pairs={{0,12},{4,0},{8,4},{12,8},{1,13},{5,1},{9,5},{13,9},{2,14},{6,2},{... | collective-permute-start | bytes 1978376 | tf_op jit(solution)/shard_map/ppermute | solution.py:341
  135.9 40.9 %collective-permute-start.24 = (bf16[6416,128]{1,0:T(8,128)(2,1)S(1)}, bf16[6416,128]{1,0:T(8,128)(2,1)S(1)}, u32[]{:S(2)}, u32[]{:S(2)}) collective-permute-start(bf16[6416,128]{1,0:T(8,128)(2,1)S(1)} %shard_map.57.msg), channel_id=1, source_target_pairs={{0,2},{1,3},{2,0},{3,1},{4,6},{5,7},{6,4},{7,5},{8,10},{9,11},{10,... | collective-permute-start | bytes 4927496 | tf_op jit(solution)/shard_map/ppermute | solution.py:370
  144.1 9.6 %collective-permute-start.21 = (bf16[640,1280]{1,0:T(8,128)(2,1)S(1)}, bf16[640,1280]{1,0:T(8,128)(2,1)S(1)}, u32[]{:S(2)}, u32[]{:S(2)}) collective-permute-start(bf16[640,1280]{1,0:T(8,128)(2,1)S(1)} %shard_map.59.refs_0_), channel_id=1, source_target_pairs={{0,1},{1,0},{2,3},{3,2},{4,5},{5,4},{6,7},{7,6},{8,9},{9,8},{10,11... | collective-permute-start | bytes 4915208 | tf_op jit(solution)/shard_map/ppermute | solution.py:377
  149.2 16.4 %collective-permute-start.22 = (bf16[2576,128]{1,0:T(8,128)(2,1)S(1)}, bf16[2576,128]{1,0:T(8,128)(2,1)S(1)}, u32[]{:S(2)}, u32[]{:S(2)}) collective-permute-start(bf16[2576,128]{1,0:T(8,128)(2,1)S(1)} %get-tuple-element.52), channel_id=1, source_target_pairs={{0,4},{4,8},{8,12},{12,0},{1,5},{5,9},{9,13},{13,1},{2,6},{6,10},{... | collective-permute-start | bytes 1978376 | tf_op jit(solution)/shard_map/ppermute | solution.py:399
  151.0 15.2 %collective-permute-start.23 = (bf16[2576,128]{1,0:T(8,128)(2,1)S(1)}, bf16[2576,128]{1,0:T(8,128)(2,1)S(1)}, u32[]{:S(2)}, u32[]{:S(2)}) collective-permute-start(bf16[2576,128]{1,0:T(8,128)(2,1)S(1)} %get-tuple-element.56), channel_id=1, source_target_pairs={{0,12},{4,0},{8,4},{12,8},{1,13},{5,1},{9,5},{13,9},{2,14},{6,2},{... | collective-permute-start | bytes 1978376 | tf_op jit(solution)/shard_map/ppermute | solution.py:399
  179.3 4.4 %collective-permute-start.25 = (bf16[640,1280]{1,0:T(8,128)(2,1)S(1)}, bf16[640,1280]{1,0:T(8,128)(2,1)S(1)}, u32[]{:S(2)}, u32[]{:S(2)}) collective-permute-start(bf16[640,1280]{1,0:T(8,128)(2,1)S(1)} %shard_map.64.refs_0_), channel_id=1, source_target_pairs={{0,1},{1,0},{2,3},{3,2},{4,5},{5,4},{6,7},{7,6},{8,9},{9,8},{10,11... | collective-permute-start | bytes 4915208 | tf_op jit(solution)/shard_map/ppermute | solution.py:377
  (9 other events, 48.8 us)
